TPU v7x, 32 devices: a whole 2x2x4 slice. The times are simulated.
32 devices in a mesh: ev: 8 (over y, x, core), ch: 4 (over z).
Axes of the slice: x: 2, y: 2, z: 4, core: 2. Of those that a mesh axis runs over, the one named last changes fastest.
Arguments:
- spectra: float32 [128, 16, 16384], P('ev', None, 'ch'), as said below
- tile_mask: int32 [128, 128], P('ev', 'ch'), may hold values 0 or 1
- source_init: float32 [128, 16], P('ev'), may hold values from -6 to 6
- site_init: float32 [16, 16384], P(None, 'ch'), may hold values from -6 to 6
- event_pos: float32 [3, 128], P(None, 'ev'), may hold values from 5 to 50
- channel_pos: float32 [2, 16384], P(None, 'ch'), may hold values from 0 to 50
- atten: float32 [16], replicated, may hold values from 0.02 to 0.3
Outputs:
- source: float32 [128, 16], P('ev')
- site: float32 [16, 16384], P(None, 'ch')
Inputs may be any that keep to these rules, and one draw needn't show every extreme that they name: spectra are log amplitudes of order one to a few, with outliers. `tile_mask`: 0 marks an event invalid on a whole tile of 128 channels.
All inputs are finite; a program needn't handle non-finite values. No bound on the sum of `tile_mask` on one device may be relied on, other than what follows from the above.
Results may differ from a plain program's by a relative error of at most 0.0001.
Values sent between devices are 32-bit elements; how exact they have to be, the bound alone decides.
No kernel may reach another device: no remote copies, remote signals or barrier semaphores. Data moves between devices by JAX's collectives and lax.ppermute only.
A program may use at most 64 MiB of HBM per device.

v0:
```python
import jax
import jax.numpy as jnp
from jax import lax
from jax.sharding import PartitionSpec as P

ITERS = 2


def on_device(spectra, tile_mask, source_init, site_init, event_pos, channel_pos, atten):
    ev_n, freqs, ch_n = spectra.shape
    total_ch = ch_n * lax.axis_size("ch")
    valid = jnp.repeat(tile_mask, 128, axis=1).astype(jnp.float32)[:, None, :]
    count_part = jnp.sum(valid)
    east = event_pos[0][:, None] - channel_pos[0][None, :]
    north = event_pos[1][:, None] - channel_pos[1][None, :]
    depth = event_pos[2][:, None]
    travel = jnp.sqrt(east * east + north * north + depth * depth) / 3.0
    path = atten[None, :, None] * travel[:, None, :]
    source = source_init
    site = site_init
    for step in range(ITERS):
        resid = spectra - source[:, :, None] - site[None, :, :] + path
        abs_part = jnp.sum(valid * jnp.abs(resid), axis=(0, 2))
        absum, count = lax.psum((abs_part, count_part), ("ev", "ch"))
        delta = 1.345 * (1.2533 * absum / jnp.maximum(count, 1.0) + 1e-05)
        limit = delta[None, :, None]
        weight = limit / jnp.maximum(jnp.abs(resid), limit) * valid
        product = weight * resid
        src_num, src_den = lax.psum((jnp.sum(product, axis=2), jnp.sum(weight, axis=2)), "ch")
        site_num = jnp.sum(product, axis=0)
        site_den = jnp.sum(weight, axis=0)
        site_num, site_den = lax.psum((site_num, site_den), "ev")
        site = site + 0.5 * site_num / (site_den + 1.0)
        source = source + 0.5 * src_num / (src_den + 1.0)
        shift = lax.psum(jnp.sum(site, axis=1), "ch") / total_ch
        site = site - shift[:, None]
        source = source + shift[None, :]
    return (source, site)


def solution(mesh):
    in_specs = (
        P("ev", None, "ch"),
        P("ev", "ch"),
        P("ev", None),
        P(None, "ch"),
        P(None, "ev"),
        P(None, "ch"),
        P(),
    )
    out_specs = (P("ev", None), P(None, "ch"))
    return jax.shard_map(
        on_device, mesh=mesh, in_specs=in_specs, out_specs=out_specs, check_vma=False
    )
```

profile of v0, /device:TPU:0, one launch (start us, length us, event | category | flops | bytes accessed | tf_op | source)
XLA Modules:
  0.0 266.8 jit_solution(4690929802238256030)
XLA Ops:
  7.2 0.0 copy-start.2
  7.2 0.0 copy-start
  7.2 0.0 copy-start.1
  7.2 0.0 all-reduce.10.cloned.1.call-start
  7.2 0.8 slice_bitcast_fusion.1
  8.0 0.7 convert_element_type.13
  8.7 0.9 fusion.8
  9.6 0.1 broadcast_in_dim.2
  9.7 0.2 copy.11
  9.9 0.2 sqrt_multiply_fusion
  10.1 3.4 %multiply_reduce_fusion.1 = f32[16]{0:T(128)S(1)} fusion(f32[16,16,4096]{2,1,0:T(8,128)} %param.7, f32[16,4096]{1,0:T(8,128)S(1)} %sqrt_multiply_fusion, f32[16]{0:T(128)} %param.13, f32[16,4096]{1,0:T(8,128)} %param.10, f32[16,16]{1,0:T(8,128)} %param.9, f32[16,4096]{1,0:T(8,128)S(1)} %bitcast.12), kind=kLoop, calls=%fused_computation.5 | loop fusion | flops 7340016 | bytes 4981888 | tf_op jit(solution)/shard_map/reduce_sum | solution.py:23
  13.5 0.7 broadcast_reduce_fusion
  14.2 42.2 %all-reduce = (f32[16]{0:T(128)S(1)}, f32[]{:T(128)}) all-reduce(f32[16]{0:T(128)S(1)} %multiply_reduce_fusion.1, f32[]{:T(128)} %broadcast_reduce_fusion), channel_id=1, replica_groups=mesh['ev'=8,'ch'=4] {'ev','ch'}, use_global_device_ids=true, to_apply=%region_1.0 | all-reduce | flops 17 | bytes 136 | tf_op jit(solution)/shard_map/psum | solution.py:24
  57.1 0.0 copy-done.2
  57.1 0.0 copy-done
  57.1 0.0 copy-done.1
  57.1 5.4 %fusion.4 = (f32[16,4096]{1,0:T(8,128)}, f32[16,16]{1,0:T(8,128)S(1)}, f32[16,4096]{1,0:T(8,128)}, f32[16,16]{1,0:T(8,128)S(1)}) fusion(f32[16,4096]{1,0:T(8,128)S(1)} %sqrt_multiply_fusion, f32[16]{0:T(128)S(1)} %copy-done.2, f32[16,4096]{1,0:T(8,128)S(1)} %copy-done, f32[16,16,4096]{2,1,0:T(8,128)} %param.7, f32[16,16]{1,0:T(8,128)S(1)} %copy-done.1, ...), kind=kLoop, calls=%fused_computation.26 | loop fusion | flops 13499904 | bytes 5508224 | tf_op jit(solution)/shard_map/reduce_sum | solution.py:30
  62.5 0.0 all-reduce.10.cloned.1.call-update
  62.5 0.0 all-reduce.8.cloned.1.call-start
  62.5 54.7 %all-reduce.10.cloned.1.call-done = (f32[16,4096]{1,0:T(8,128)}, f32[16,4096]{1,0:T(8,128)}) async-done(((f32[16,4096]{1,0:T(8,128)}, f32[16,4096]{1,0:T(8,128)}), (f32[16,4096]{1,0:T(8,128)}, f32[16,4096]{1,0:T(8,128)})) %all-reduce.10.cloned.1.call-update) | async-done | bytes 524304 | tf_op jit(solution)/shard_map/psum | solution.py:32
  117.3 1.2 fusion.7
  118.5 18.8 %all-reduce.4 = (f32[16,16]{1,0:T(8,128)S(1)}, f32[16,16]{1,0:T(8,128)S(1)}, f32[16]{0:T(128)S(1)}) all-reduce(f32[16,16]{1,0:T(8,128)S(1)} %get-tuple-element.9, f32[16,16]{1,0:T(8,128)S(1)} %get-tuple-element.5, f32[16]{0:T(128)S(1)} %get-tuple-element.24), channel_id=1, replica_groups=mesh['ev'=8,'ch'=4] {'ch'}, use_global_device_ids=true, to_apply=%region_7.0 | all-reduce | flops 528 | bytes 4224 | tf_op jit(solution)/shard_map/psum | solution.py:29
  137.3 0.1 broadcast_subtract_fusion.1
  137.4 3.3 %multiply_reduce_fusion = f32[16]{0:T(128)S(1)} fusion(f32[16,16,4096]{2,1,0:T(8,128)} %param.7, f32[16,4096]{1,0:T(8,128)S(1)} %broadcast_subtract_fusion.1, f32[16,16]{1,0:T(8,128)S(1)} %add_add_fusion.1, f32[16,4096]{1,0:T(8,128)S(1)} %sqrt_multiply_fusion, f32[16]{0:T(128)S(1)} %copy-done.2, f32[16,4096]{1,0:T(8,128)S(1)} %bitcast.14), kind=kLoop, calls=%fused_computation.3 | loop fusion | flops 7340016 | bytes 4981888 | tf_op jit(solution)/shard_map/reduce_sum | solution.py:23
  140.7 37.5 %psum.101 = f32[16]{0:T(128)S(1)} all-reduce(f32[16]{0:T(128)S(1)} %multiply_reduce_fusion), channel_id=1, replica_groups=mesh['ev'=8,'ch'=4] {'ev','ch'}, use_global_device_ids=true, to_apply=%region_15.0 | all-reduce | flops 16 | bytes 128 | tf_op jit(solution)/shard_map/psum | solution.py:24
  178.2 5.4 %fusion.2 = (f32[16,4096]{1,0:T(8,128)}, f32[16,16]{1,0:T(8,128)S(1)}, f32[16,4096]{1,0:T(8,128)}, f32[16,16]{1,0:T(8,128)S(1)}) fusion(f32[16,4096]{1,0:T(8,128)S(1)} %sqrt_multiply_fusion, f32[16]{0:T(128)S(1)} %copy-done.2, f32[16,4096]{1,0:T(8,128)S(1)} %broadcast_subtract_fusion.1, f32[16,16,4096]{2,1,0:T(8,128)} %param.7, ...), kind=kLoop, calls=%fused_computation.24 | loop fusion | flops 13499904 | bytes 5508224 | tf_op jit(solution)/shard_map/reduce_sum | solution.py:30
  183.6 0.0 all-reduce.8.cloned.1.call-update
  183.6 54.9 %all-reduce.8.cloned.1.call-done = (f32[16,4096]{1,0:T(8,128)}, f32[16,4096]{1,0:T(8,128)}) async-done(((f32[16,4096]{1,0:T(8,128)}, f32[16,4096]{1,0:T(8,128)}), (f32[16,4096]{1,0:T(8,128)}, f32[16,4096]{1,0:T(8,128)})) %all-reduce.8.cloned.1.call-update) | async-done | bytes 524304 | tf_op jit(solution)/shard_map/psum | solution.py:32
  238.5 1.2 fusion.6
  239.8 18.8 %all-reduce.3 = (f32[16,16]{1,0:T(8,128)S(1)}, f32[16,16]{1,0:T(8,128)S(1)}, f32[16]{0:T(128)S(1)}) all-reduce(f32[16,16]{1,0:T(8,128)S(1)} %get-tuple-element.7, f32[16,16]{1,0:T(8,128)S(1)} %get-tuple-element.3, f32[16]{0:T(128)S(1)} %get-tuple-element.22), channel_id=1, replica_groups=mesh['ev'=8,'ch'=4] {'ch'}, use_global_device_ids=true, to_apply=%region_19.0 | all-reduce | flops 528 | bytes 4224 | tf_op jit(solution)/shard_map/psum | solution.py:29
  258.6 0.8 broadcast_subtract_fusion
  259.4 0.6 add_add_fusion
  (5 shorter events, 0.0 us)
Async XLA Ops:
  7.2 49.9 %copy-start.2 = (f32[16]{0:T(128)S(1)}, f32[16]{0:T(128)}, u32[]{:S(2)}) copy-start(f32[16]{0:T(128)} %param.13) | copy-start | bytes 196
  7.2 49.9 %copy-start = (f32[16,4096]{1,0:T(8,128)S(1)}, f32[16,4096]{1,0:T(8,128)}, u32[]{:S(2)}) copy-start(f32[16,4096]{1,0:T(8,128)} %param.10) | copy-start | bytes 786436
  7.2 49.9 %copy-start.1 = (f32[16,16]{1,0:T(8,128)S(1)}, f32[16,16]{1,0:T(8,128)}, u32[]{:S(2)}) copy-start(f32[16,16]{1,0:T(8,128)} %param.9) | copy-start | bytes 3076
  7.2 110.1 %all-reduce.10.cloned.1.call-start = ((), (), s32[]{:S(2)}) async-start(), calls=%async_computation.1 | async-start | bytes 1048576 | tf_op jit(solution)/shard_map/psum | solution.py:32
  62.5 176.0 %all-reduce.8.cloned.1.call-start = ((), (), s32[]{:S(2)}) async-start(), calls=%async_computation | async-start | bytes 1048576 | tf_op jit(solution)/shard_map/psum | solution.py:32
Sparse Core Ops, SparseCore 0:
  62.6 54.6 all-reduce.9
  183.8 54.7 all-reduce.7
where the time goes:
time: 267 us
  blocking collectives  117 us (44%)
  waiting for transfers between devices  110 us (41%)
  other arithmetic  23.8 us (9%)
  between operations  14.8 us (6%)
    psum x2, waiting for transfers between devices, on_device(): site_num, site_den = lax.psum((site_num, site_den), 'ev')  110 us
    psum x2, blocking collectives, on_device(): absum, count = lax.psum((abs_part, count_part), ('ev', 'ch'))  79.7 us
    psum x2, blocking collectives, on_device(): lax.psum((jnp.sum(product, axis=2), jnp.sum(weight, axis=2)), 'ch')  37.6 us
    reduce_sum x2, other arithmetic, on_device(): site_num = jnp.sum(product, axis=0)  10.7 us
    reduce_sum x2, other arithmetic, on_device(): abs_part = jnp.sum(valid * jnp.abs(resid), axis=(0, 2))  6.67 us
  transfers between devices with their start and end apart: 2, of which 2 were waited for; matrix products, arithmetic and copies ran while one was open for 0% of the time, Pallas kernels for 0%

commit v1 on v0

v1 whole, which is shorter than its diff:
```python
import jax
import jax.numpy as jnp
from jax import lax
from jax.sharding import PartitionSpec as P

ITERS = 2
LANES = 128


def sum_all(vector, devices):
    sent = jnp.broadcast_to(vector, (devices, LANES))
    return jnp.sum(lax.all_to_all(sent, ("ev", "ch"), 0, 0), axis=0)


def sum_ch(value, ch_dev):
    bit = 1
    while bit < ch_dev:
        value = value + lax.ppermute(value, "ch", [(i, i ^ bit) for i in range(ch_dev)])
        bit *= 2
    return value


def on_device(spectra, tile_mask, source_init, site_init, event_pos, channel_pos, atten):
    ev_n, freqs, ch_n = spectra.shape
    ev_dev, ch_dev = lax.axis_size("ev"), lax.axis_size("ch")
    devices = ev_dev * ch_dev
    total_ch = ch_n * ch_dev
    piece = ch_n // ev_dev
    me = lax.axis_index("ev")
    valid = jnp.repeat(tile_mask, 128, axis=1).astype(jnp.float32)[:, None, :]
    count_part = jnp.sum(tile_mask.astype(jnp.float32)) * 128.0
    east = event_pos[0][:, None] - channel_pos[0][None, :]
    north = event_pos[1][:, None] - channel_pos[1][None, :]
    depth = event_pos[2][:, None]
    travel = jnp.sqrt(east * east + north * north + depth * depth) / 3.0
    path = atten[None, :, None] * travel[:, None, :]
    source = source_init
    site = site_init
    own = lax.dynamic_slice(site_init, (0, me * piece), (freqs, piece))
    count = None
    for step in range(ITERS):
        resid = spectra - source[:, :, None] - site[None, :, :] + path
        abs_part = jnp.sum(valid * jnp.abs(resid), axis=(0, 2))
        packed = jnp.concatenate([abs_part, count_part[None], jnp.zeros((LANES - freqs - 1,), jnp.float32)])
        total = sum_all(packed, devices)
        absum, count = total[:freqs], total[freqs]
        delta = 1.345 * (1.2533 * absum / jnp.maximum(count, 1.0) + 1e-05)
        limit = delta[None, :, None]
        weight = limit / jnp.maximum(jnp.abs(resid), limit) * valid
        product = weight * resid
        src = sum_ch(jnp.stack([jnp.sum(product, axis=2), jnp.sum(weight, axis=2)]), ch_dev)
        both = jnp.stack([jnp.sum(product, axis=0), jnp.sum(weight, axis=0)])
        both = both.reshape(2, freqs, ev_dev, piece).transpose(2, 0, 1, 3)
        both = jnp.sum(lax.all_to_all(both, "ev", 0, 0), axis=0)
        own = own + 0.5 * both[0] / (both[1] + 1.0)
        source = source + 0.5 * src[0] / (src[1] + 1.0)
        if step == ITERS - 1:
            sums = jnp.concatenate([jnp.sum(own, axis=1), jnp.zeros((LANES - freqs,), jnp.float32)])
            shift = sum_all(sums, devices)[:freqs] / total_ch
        sent = jnp.broadcast_to(own[None], (ev_dev, freqs, piece))
        site = lax.all_to_all(sent, "ev", 0, 0).transpose(1, 0, 2).reshape(freqs, ch_n)
    return (source + shift[None, :], site - shift[:, None])


def solution(mesh):
    in_specs = (
        P("ev", None, "ch"),
        P("ev", "ch"),
        P("ev", None),
        P(None, "ch"),
        P(None, "ev"),
        P(None, "ch"),
        P(),
    )
    out_specs = (P("ev", None), P(None, "ch"))
    return jax.shard_map(
        on_device, mesh=mesh, in_specs=in_specs, out_specs=out_specs, check_vma=False
    )
```

time: 267 us -> 111 us (0.42)
  blocking collectives: 117 us -> 23.1 us
  waiting for transfers between devices: 110 us -> 37.2 us
  starting transfers between devices: 0.08 us -> 18.6 us
  between operations: 14.8 us -> 2.87 us
  local copies, waits for them, and re-layouts: 1.16 us -> 7.3 us
  other arithmetic: 23.8 us -> 20.9 us
    psum x4 -> x0, blocking collectives: 117 us -> none  [the longest x2 79.7 us: on_device(): absum, count = lax.psum((abs_part, count_part), ('ev', 'ch'))]
    psum x2 -> x0, waiting for transfers between devices: 110 us -> none  [on_device(): site_num, site_den = lax.psum((site_num, site_den), 'ev')]
    all_to_all x0 -> x5, waiting for transfers between devices: none -> 30.7 us  [the longest x2 13 us: on_device(): lax.all_to_all(sent, 'ev', 0, 0).transpose(1, 0, 2).reshape(freqs, ch_n)]
    all_to_all x0 -> x2, blocking collectives: none -> 23.1 us  [sum_all(): return jnp.sum(lax.all_to_all(sent, ('ev', 'ch'), 0, 0), axis=0)]
    all_to_all x0 -> x5, starting transfers between devices: none -> 16.4 us  [the longest x2 6.98 us: on_device(): both = jnp.sum(lax.all_to_all(both, 'ev', 0, 0), axis=0)]
    ppermute x0 -> x4, waiting for transfers between devices: none -> 6.52 us  [sum_ch(): lax.ppermute(value, 'ch', [(i, i ^ bit) for i in range(ch_dev)])]
    reduce_sum x5 -> x9, other arithmetic: 13.9 us -> 10.8 us  [the longest x2 9.2 us: on_device(): both = jnp.stack([jnp.sum(product, axis=0), jnp.sum(weight, axis=0)])]
  transfers between devices with their start and end apart: 2 -> 9, of which waited for: 2 -> 7; matrix products, arithmetic and copies ran while one was open for 0% -> 2% of each run, Pallas kernels for 0% -> 0%
where the time goes in v1:
time: 111 us; the launch traced here: 110 us
  waiting for transfers between devices  37.2 us (34%)
  blocking collectives  23.1 us (21%)
  other arithmetic  20.9 us (19%)
  starting transfers between devices  18.6 us (17%)
  local copies, waits for them, and re-layouts  7.3 us (7%)
  between operations  2.87 us (3%)
    all_to_all x2, blocking collectives, sum_all(): return jnp.sum(lax.all_to_all(sent, ('ev', 'ch'), 0, 0), axis=0)  23.1 us
    all_to_all x2, waiting for transfers between devices, on_device(): lax.all_to_all(sent, 'ev', 0, 0).transpose(1, 0, 2).reshape(freqs, ch_n)  13 us
    all_to_all x2, waiting for transfers between devices, on_device(): both = jnp.sum(lax.all_to_all(both, 'ev', 0, 0), axis=0)  10.6 us
    reduce_sum x2, other arithmetic, on_device(): both = jnp.stack([jnp.sum(product, axis=0), jnp.sum(weight, axis=0)])  9.2 us
    all_to_all x1, waiting for transfers between devices, sum_all(): return jnp.sum(lax.all_to_all(sent, ('ev', 'ch'), 0, 0), axis=0)  7.07 us
    all_to_all x2, starting transfers between devices, on_device(): both = jnp.sum(lax.all_to_all(both, 'ev', 0, 0), axis=0)  6.98 us
    all_to_all x2, starting transfers between devices, on_device(): lax.all_to_all(sent, 'ev', 0, 0).transpose(1, 0, 2).reshape(freqs, ch_n)  6.83 us
    reduce_sum x2, other arithmetic, on_device(): abs_part = jnp.sum(valid * jnp.abs(resid), axis=(0, 2))  6.67 us
  transfers between devices with their start and end apart: 9, of which 7 were waited for; matrix products, arithmetic and copies ran while one was open for 2% of the time, Pallas kernels for 0%

profile of v1, /device:TPU:0, one launch (start us, length us, event | category | flops | bytes accessed | tf_op | source)
XLA Modules:
  0.0 110.0 jit_solution(15134395232262790955)
XLA Ops:
  0.7 0.7 convert_element_type.12
  1.4 1.3 %convert_reduce_fusion = f32[]{:T(128)} fusion(s32[16,32]{1,0:T(8,128)} %param.8), kind=kLoop, calls=%fused_computation.44 | loop fusion | flops 1023 | bytes 2052 | tf_op jit(solution)/shard_map/reduce_sum | solution.py:31
  2.7 0.8 slice_bitcast_fusion.1
  3.5 0.9 fusion.23
  5.5 3.4 %multiply_reduce_fusion.1 = f32[16]{0:T(128)S(1)} fusion(f32[16,16,4096]{2,1,0:T(8,128)} %param.7, f32[16,4096]{1,0:T(8,128)S(1)} %sqrt_multiply_fusion, f32[16]{0:T(128)} %param.13, f32[16,4096]{1,0:T(8,128)} %param.10, f32[16,16]{1,0:T(8,128)} %param.9, f32[16,4096]{1,0:T(8,128)S(1)} %bitcast.63), kind=kLoop, calls=%fused_computation.5 | loop fusion | flops 7340016 | bytes 4981888 | tf_op jit(solution)/shard_map/reduce_sum | solution.py:43
  9.0 14.3 %all_to_all.38 = f32[32,1,128]{2,1,0:T(1,128)S(1)} all-to-all(f32[32,1,128]{2,1,0:T(1,128)S(1)} %broadcast_in_dim.16), channel_id=1, replica_groups=mesh['ev'=8,'ch'=4] {'ev','ch'}, dimensions={0} | all-to-all | bytes 32768 | tf_op jit(solution)/shard_map/all_to_all | solution.py:12
  23.3 0.6 slice.60
  24.6 4.6 %fusion.19 = (f32[16,4096]{1,0:T(8,128)S(1)}, f32[16,16]{1,0:T(8,128)S(1)}, f32[16,4096]{1,0:T(8,128)S(1)}, f32[16,16]{1,0:T(8,128)S(1)}) fusion(f32[16,4096]{1,0:T(8,128)S(1)} %sqrt_multiply_fusion, f32[16]{0:T(128)S(1)} %copy-done.2, f32[16,4096]{1,0:T(8,128)S(1)} %copy-done, f32[16,16,4096]{2,1,0:T(8,128)} %param.7, f32[16,16]{1,0:T(8,128)S(1)} %copy-done.1, ...), kind=kLoop, calls=%fused_computation.49 | loop fusion | flops 13499904 | bytes 5508224 | tf_op jit(solution)/shard_map/reduce_sum | solution.py:52
  29.5 1.1 copy.18
  30.6 3.5 %all-to-all-start.1 = ((f32[8,2,16,512]{3,2,1,0:T(8,128)}), f32[8,2,16,512]{3,2,1,0:T(8,128)S(1)}, u32[]{:S(2)}, u32[]{:S(2)}) async-start(f32[8,2,16,512]{3,2,1,0:T(8,128)} %copy.18), calls=%async_computation.1 | async-start | bytes 1048576 | tf_op jit(solution)/shard_map/all_to_all | solution.py:54
  34.1 0.6 collective-permute-start
  34.7 3.3 %collective-permute-done = f32[2,16,16]{2,1,0:T(8,128)S(1)} collective-permute-done((f32[2,16,16]{2,1,0:T(8,128)S(1)}, f32[2,16,16]{2,1,0:T(8,128)S(1)}, u32[]{:S(2)}, u32[]{:S(2)}) %collective-permute-start) | collective-permute-done | bytes 2080 | tf_op jit(solution)/shard_map/ppermute | solution.py:18
  38.5 5.3 %all-to-all-done.1 = f32[8,2,16,512]{3,2,1,0:T(8,128)S(1)} async-done(((f32[8,2,16,512]{3,2,1,0:T(8,128)}), f32[8,2,16,512]{3,2,1,0:T(8,128)S(1)}, u32[]{:S(2)}, u32[]{:S(2)}) %all-to-all-start.1) | async-done | bytes 524320 | tf_op jit(solution)/shard_map/all_to_all | solution.py:54
  43.8 0.7 broadcast_in_dim.17
  44.6 3.4 %all-to-all-start.2 = ((f32[8,16,512]{2,1,0:T(8,128)}), f32[8,16,512]{2,1,0:T(8,128)S(1)}, u32[]{:S(2)}, u32[]{:S(2)}) async-start(f32[8,16,512]{2,1,0:T(8,128)} %broadcast_in_dim.17), calls=%async_computation.2 | async-start | bytes 524288 | tf_op jit(solution)/shard_map/all_to_all | solution.py:61
  48.0 6.8 %all-to-all-done.2 = f32[8,16,512]{2,1,0:T(8,128)S(1)} async-done(((f32[8,16,512]{2,1,0:T(8,128)}), f32[8,16,512]{2,1,0:T(8,128)S(1)}, u32[]{:S(2)}, u32[]{:S(2)}) %all-to-all-start.2) | async-done | bytes 262176 | tf_op jit(solution)/shard_map/all_to_all | solution.py:61
  54.9 3.3 %multiply_reduce_fusion = f32[16]{0:T(128)S(1)} fusion(f32[16,16,4096]{2,1,0:T(8,128)} %param.7, f32[16,4096]{1,0:T(8,128)S(1)} %bitcast.67, f32[16,16]{1,0:T(8,128)S(1)} %fusion.14, f32[16,4096]{1,0:T(8,128)S(1)} %sqrt_multiply_fusion, f32[16]{0:T(128)S(1)} %copy-done.2, f32[16,4096]{1,0:T(8,128)S(1)} %bitcast.65), kind=kLoop, calls=%fused_computation.3 | loop fusion | flops 7340016 | bytes 4981888 | tf_op jit(solution)/shard_map/reduce_sum | solution.py:43
  58.3 8.9 %all_to_all.39 = f32[32,1,128]{2,1,0:T(1,128)S(1)} all-to-all(f32[32,1,128]{2,1,0:T(1,128)S(1)} %broadcast_in_dim.18), channel_id=1, replica_groups=mesh['ev'=8,'ch'=4] {'ev','ch'}, dimensions={0} | all-to-all | bytes 32768 | tf_op jit(solution)/shard_map/all_to_all | solution.py:12
  67.2 0.6 slice.66
  68.4 4.6 %fusion.17 = (f32[16,4096]{1,0:T(8,128)S(1)}, f32[16,16]{1,0:T(8,128)S(1)}, f32[16,4096]{1,0:T(8,128)S(1)}, f32[16,16]{1,0:T(8,128)S(1)}) fusion(f32[16,4096]{1,0:T(8,128)S(1)} %sqrt_multiply_fusion, f32[16]{0:T(128)S(1)} %copy-done.2, f32[16,4096]{1,0:T(8,128)S(1)} %bitcast.68, f32[16,16,4096]{2,1,0:T(8,128)} %param.7, f32[16,16]{1,0:T(8,128)S(1)} %fusion.14, ...), kind=kLoop, calls=%fused_computation.47 | loop fusion | flops 13499904 | bytes 5508224 | tf_op jit(solution)/shard_map/reduce_sum | solution.py:52
  73.4 1.1 copy.21
  74.5 3.5 %all-to-all-start.4 = ((f32[8,2,16,512]{3,2,1,0:T(8,128)}), f32[8,2,16,512]{3,2,1,0:T(8,128)S(1)}, u32[]{:S(2)}, u32[]{:S(2)}) async-start(f32[8,2,16,512]{3,2,1,0:T(8,128)} %copy.21), calls=%async_computation.4 | async-start | bytes 1048576 | tf_op jit(solution)/shard_map/all_to_all | solution.py:54
  78.6 3.3 %collective-permute-done.2 = f32[2,16,16]{2,1,0:T(8,128)S(1)} collective-permute-done((f32[2,16,16]{2,1,0:T(8,128)S(1)}, f32[2,16,16]{2,1,0:T(8,128)S(1)}, u32[]{:S(2)}, u32[]{:S(2)}) %collective-permute-start.2) | collective-permute-done | bytes 2080 | tf_op jit(solution)/shard_map/ppermute | solution.py:18
  82.4 5.3 %all-to-all-done.4 = f32[8,2,16,512]{3,2,1,0:T(8,128)S(1)} async-done(((f32[8,2,16,512]{3,2,1,0:T(8,128)}), f32[8,2,16,512]{3,2,1,0:T(8,128)S(1)}, u32[]{:S(2)}, u32[]{:S(2)}) %all-to-all-start.4) | async-done | bytes 524320 | tf_op jit(solution)/shard_map/all_to_all | solution.py:54
  87.9 0.6 broadcast_in_dim.19
  88.5 2.5 %all-to-all-start.5 = ((f32[32,1,128]{2,1,0:T(1,128)}), f32[32,1,128]{2,1,0:T(1,128)S(1)}, u32[]{:S(2)}, u32[]{:S(2)}) async-start(f32[32,1,128]{2,1,0:T(1,128)} %broadcast_in_dim.19), calls=%async_computation.5 | async-start | bytes 32768 | tf_op jit(solution)/shard_map/all_to_all | solution.py:12
  91.1 7.1 %all-to-all-done.5 = f32[32,1,128]{2,1,0:T(1,128)S(1)} async-done(((f32[32,1,128]{2,1,0:T(1,128)}), f32[32,1,128]{2,1,0:T(1,128)S(1)}, u32[]{:S(2)}, u32[]{:S(2)}) %all-to-all-start.5) | async-done | bytes 16416 | tf_op jit(solution)/shard_map/all_to_all | solution.py:12
  98.1 0.7 broadcast_in_dim.20
  98.9 3.4 %all-to-all-start.6 = ((f32[8,16,512]{2,1,0:T(8,128)}), f32[8,16,512]{2,1,0:T(8,128)S(1)}, u32[]{:S(2)}, u32[]{:S(2)}) async-start(f32[8,16,512]{2,1,0:T(8,128)} %broadcast_in_dim.20), calls=%async_computation.6 | async-start | bytes 524288 | tf_op jit(solution)/shard_map/all_to_all | solution.py:61
  102.3 0.6 fusion.11
  102.9 6.2 %all-to-all-done.6 = f32[8,16,512]{2,1,0:T(8,128)S(1)} async-done(((f32[8,16,512]{2,1,0:T(8,128)}), f32[8,16,512]{2,1,0:T(8,128)S(1)}, u32[]{:S(2)}, u32[]{:S(2)}) %all-to-all-start.6) | async-done | bytes 262176 | tf_op jit(solution)/shard_map/all_to_all | solution.py:61
  109.2 0.8 broadcast_subtract_fusion
  (45 shorter events, 3.4 us)
Async XLA Ops:
  0.6 23.9 %copy-start = (f32[16,4096]{1,0:T(8,128)S(1)}, f32[16,4096]{1,0:T(8,128)}, u32[]{:S(2)}) copy-start(f32[16,4096]{1,0:T(8,128)} %param.10) | copy-start | bytes 786436
  0.6 23.9 %copy-start.2 = (f32[16]{0:T(128)S(1)}, f32[16]{0:T(128)}, u32[]{:S(2)}) copy-start(f32[16]{0:T(128)} %param.13) | copy-start | bytes 196
  0.7 23.9 %copy-start.1 = (f32[16,16]{1,0:T(8,128)S(1)}, f32[16,16]{1,0:T(8,128)}, u32[]{:S(2)}) copy-start(f32[16,16]{1,0:T(8,128)} %param.9) | copy-start | bytes 3076
  30.6 13.2 %all-to-all-start.1 = ((f32[8,2,16,512]{3,2,1,0:T(8,128)}), f32[8,2,16,512]{3,2,1,0:T(8,128)S(1)}, u32[]{:S(2)}, u32[]{:S(2)}) async-start(f32[8,2,16,512]{3,2,1,0:T(8,128)} %copy.18), calls=%async_computation.1 | async-start | bytes 1048576 | tf_op jit(solution)/shard_map/all_to_all | solution.py:54
  34.1 3.8 %collective-permute-start = (f32[2,16,16]{2,1,0:T(8,128)S(1)}, f32[2,16,16]{2,1,0:T(8,128)S(1)}, u32[]{:S(2)}, u32[]{:S(2)}) collective-permute-start(f32[2,16,16]{2,1,0:T(8,128)S(1)} %pad_maximum_fusion), channel_id=1, source_target_pairs={{0,1},{1,0},{2,3},{3,2},{4,5},{5,4},{6,7},{7,6},{8,9},{9,8},{10,11... | collective-permute-start | bytes 6152 | tf_op jit(solution)/shard_map/ppermute | solution.py:18
  38.0 10.0 %collective-permute-start.1 = (f32[2,16,16]{2,1,0:T(8,128)S(1)}, f32[2,16,16]{2,1,0:T(8,128)S(1)}, u32[]{:S(2)}, u32[]{:S(2)}) collective-permute-start(f32[2,16,16]{2,1,0:T(8,128)S(1)} %fusion.16), channel_id=1, source_target_pairs={{0,2},{1,3},{2,0},{3,1},{4,6},{5,7},{6,4},{7,5},{8,10},{9,11},{10,... | collective-permute-start | bytes 6152 | tf_op jit(solution)/shard_map/ppermute | solution.py:18
  44.6 10.3 %all-to-all-start.2 = ((f32[8,16,512]{2,1,0:T(8,128)}), f32[8,16,512]{2,1,0:T(8,128)S(1)}, u32[]{:S(2)}, u32[]{:S(2)}) async-start(f32[8,16,512]{2,1,0:T(8,128)} %broadcast_in_dim.17), calls=%async_computation.2 | async-start | bytes 524288 | tf_op jit(solution)/shard_map/all_to_all | solution.py:61
  74.5 13.2 %all-to-all-start.4 = ((f32[8,2,16,512]{3,2,1,0:T(8,128)}), f32[8,2,16,512]{3,2,1,0:T(8,128)S(1)}, u32[]{:S(2)}, u32[]{:S(2)}) async-start(f32[8,2,16,512]{3,2,1,0:T(8,128)} %copy.21), calls=%async_computation.4 | async-start | bytes 1048576 | tf_op jit(solution)/shard_map/all_to_all | solution.py:54
  78.0 3.8 %collective-permute-start.2 = (f32[2,16,16]{2,1,0:T(8,128)S(1)}, f32[2,16,16]{2,1,0:T(8,128)S(1)}, u32[]{:S(2)}, u32[]{:S(2)}) collective-permute-start(f32[2,16,16]{2,1,0:T(8,128)S(1)} %pad_maximum_fusion.1), channel_id=1, source_target_pairs={{0,1},{1,0},{2,3},{3,2},{4,5},{5,4},{6,7},{7,6},{8,9},{9,8},{10,11... | collective-permute-start | bytes 6152 | tf_op jit(solution)/shard_map/ppermute | solution.py:18
  81.9 9.2 %collective-permute-start.3 = (f32[2,16,16]{2,1,0:T(8,128)S(1)}, f32[2,16,16]{2,1,0:T(8,128)S(1)}, u32[]{:S(2)}, u32[]{:S(2)}) collective-permute-start(f32[2,16,16]{2,1,0:T(8,128)S(1)} %fusion.15), channel_id=1, source_target_pairs={{0,2},{1,3},{2,0},{3,1},{4,6},{5,7},{6,4},{7,5},{8,10},{9,11},{10,... | collective-permute-start | bytes 6152 | tf_op jit(solution)/shard_map/ppermute | solution.py:18
  88.5 9.6 %all-to-all-start.5 = ((f32[32,1,128]{2,1,0:T(1,128)}), f32[32,1,128]{2,1,0:T(1,128)S(1)}, u32[]{:S(2)}, u32[]{:S(2)}) async-start(f32[32,1,128]{2,1,0:T(1,128)} %broadcast_in_dim.19), calls=%async_computation.5 | async-start | bytes 32768 | tf_op jit(solution)/shard_map/all_to_all | solution.py:12
  98.9 10.3 %all-to-all-start.6 = ((f32[8,16,512]{2,1,0:T(8,128)}), f32[8,16,512]{2,1,0:T(8,128)S(1)}, u32[]{:S(2)}, u32[]{:S(2)}) async-start(f32[8,16,512]{2,1,0:T(8,128)} %broadcast_in_dim.20), calls=%async_computation.6 | async-start | bytes 524288 | tf_op jit(solution)/shard_map/all_to_all | solution.py:61

commit v2 on v0

v2 whole, which is shorter than its diff:
```python
import functools

import jax
import jax.numpy as jnp
from jax import lax
from jax.experimental import pallas as pl
from jax.experimental.pallas import tpu as pltpu
from jax.sharding import PartitionSpec as P

ITERS = 2
LANES = 128
TILE = 128
GROUP = 4
F32 = jnp.float32
VMEM = pl.BlockSpec(memory_space=pltpu.VMEM)
ANY = pl.BlockSpec(memory_space=pl.ANY)
LIMIT = 24 * 1024 * 1024


def eye(rows):
    shape = (rows, LANES)
    return lax.broadcasted_iota(jnp.int32, shape, 0) == lax.broadcasted_iota(jnp.int32, shape, 1)


def as_column(row, rows):
    spread = jnp.where(eye(rows), jnp.broadcast_to(row, (rows, LANES)), 0.0)
    return jnp.sum(spread, axis=1, keepdims=True)


def as_row(column):
    rows = column.shape[0]
    spread = jnp.where(eye(rows), jnp.broadcast_to(column, (rows, LANES)), 0.0)
    return jnp.sum(spread, axis=0, keepdims=True)


def widen(row):
    return jnp.concatenate([row, jnp.zeros((1, LANES - row.shape[1]), F32)], axis=1)


def tile_at(index):
    return pl.ds(pl.multiple_of(index * TILE, TILE), TILE)


def core_index():
    return lax.rem(lax.axis_index("ev"), 2)


def resid_kernel(spec_hbm, mask_ref, src_ref, site_ref, pos_ref, chan_ref, atten_ref,
                 mine_ref, theirs_ref, send_ref, spec, travel, source, sems):
    ev_n, freqs, ch_n = spec_hbm.shape
    half = ch_n // 2
    half_tiles = half // TILE
    core = core_index()
    copies = []
    for e in range(ev_n):
        copy = pltpu.make_async_copy(spec_hbm.at[e], spec.at[e], sems.at[e])
        copy.start()
        copies.append(copy)
    maskf = mask_ref[...].astype(F32)
    low, high = maskf[:, :half_tiles], maskf[:, half_tiles:]
    upper = core == 1
    for ref, own in ((mine_ref, True), (theirs_ref, False)):
        first, second = (high, low) if own else (low, high)
        picked = jnp.where(upper, first, second)
        for t in range(half_tiles):
            ref[ev_n, :, t * TILE:(t + 1) * TILE] = jnp.broadcast_to(picked[:, t:t + 1], (ev_n, TILE))
    count = jnp.sum(jnp.sum(maskf, axis=1, keepdims=True), axis=0, keepdims=True) * float(TILE)
    cols = [jnp.broadcast_to(as_column(widen(pos_ref[k:k + 1, :]), ev_n), (ev_n, TILE)) for k in range(3)]

    def travel_step(t, _):
        at = tile_at(t)
        east = cols[0] - chan_ref[0:1, at]
        north = cols[1] - chan_ref[1:2, at]
        travel[:, at] = jnp.sqrt(east * east + north * north + cols[2] * cols[2]) / 3.0
        return 0
    lax.fori_loop(0, ch_n // TILE, travel_step, 0, unroll=4)
    att = jnp.broadcast_to(as_column(widen(atten_ref[...]), freqs), (freqs, TILE))
    for e in range(ev_n):
        source[e] = jnp.broadcast_to(as_column(widen(src_ref[e:e + 1, :]), freqs), (freqs, TILE))
    total = jnp.zeros((freqs, TILE), F32)
    for e in range(ev_n):
        copies[e].wait()
        src = source[e]
        for ref, own in ((mine_ref, True), (theirs_ref, False)):
            base = (core if own else 1 - core) * half_tiles

            def step(t, acc, ref=ref, base=base, e=e, src=src):
                here, at = tile_at(t), tile_at(base + t)
                time = jnp.broadcast_to(travel[e:e + 1, at], (freqs, TILE))
                resid = (spec[e, :, at] - src) + (att * time - site_ref[:, at])
                ref[e, :, here] = resid
                valid = jnp.broadcast_to(ref[ev_n, e:e + 1, here], (freqs, TILE))
                return acc + jnp.abs(resid) * valid
            total = lax.fori_loop(0, half_tiles, step, total, unroll=8)
    row = as_row(jnp.sum(total, axis=1, keepdims=True))
    lane = lax.broadcasted_iota(jnp.int32, row.shape, 1)
    row = row + jnp.where(lane == freqs, jnp.broadcast_to(count, row.shape), 0.0)
    send_ref[...] = jnp.broadcast_to(row, send_ref.shape)


def weight_kernel(freqs, total_ref, count_ref, mine_ref, theirs_ref, a_ref, b_ref, src_ref):
    ev_n = mine_ref.shape[0] - 1
    half = mine_ref.shape[2]
    quarter = half // 2
    core = core_index()
    row = jnp.sum(total_ref[...], axis=0, keepdims=True)
    counts = jnp.sum(count_ref[...], axis=0, keepdims=True)
    lane = lax.broadcasted_iota(jnp.int32, row.shape, 1)
    count = jnp.sum(jnp.where(lane == freqs, counts, 0.0), axis=1, keepdims=True)
    delta = 1.345 * (1.2533 * row / jnp.maximum(count, 1.0) + 1e-05)
    delta = jnp.broadcast_to(as_column(delta, freqs), (freqs, TILE))
    per_row = LANES // freqs
    zero = jnp.zeros((freqs, TILE), F32)
    a_ref[...] = jnp.zeros_like(a_ref)
    b_ref[...] = jnp.zeros_like(b_ref)
    for which, ref in enumerate((mine_ref, theirs_ref)):
        owner = core if which == 0 else 1 - core
        nums, dens = [], []
        for start in range(0, ev_n, GROUP):
            events = range(start, start + GROUP)

            def step(t, acc, ref=ref, events=events):
                acc = list(acc)
                for out, base in ((a_ref, 0), (b_ref, quarter // TILE)):
                    here, at = tile_at(t), tile_at(base + t)
                    num, den = out[0, :, here], out[1, :, here]
                    for k, e in enumerate(events):
                        resid = ref[e, :, at]
                        valid = jnp.broadcast_to(ref[ev_n, e:e + 1, at], (freqs, TILE))
                        weight = valid * delta / jnp.maximum(jnp.abs(resid), delta)
                        product = weight * resid
                        num, den = num + product, den + weight
                        acc[2 * k] += product
                        acc[2 * k + 1] += weight
                    out[0, :, here] = num
                    out[1, :, here] = den
                return tuple(acc)
            acc = lax.fori_loop(0, quarter // TILE, step, (zero,) * (2 * GROUP))
            nums += acc[0::2]
            dens += acc[1::2]
        rows_each = ev_n // per_row
        for kind, parts in ((0, nums), (1, dens)):
            for i in range(rows_each):
                block = jnp.concatenate(parts[i * per_row:(i + 1) * per_row], axis=0)
                line = jnp.sum(block.T, axis=0, keepdims=True)
                src_ref[pl.ds(kind * 2 * rows_each + owner * rows_each + i, 1), :] = line


def increments(src_a, src_b):
    sums = src_a + src_b
    rows = sums.shape[0] // 2
    return 0.5 * sums[:rows] / (sums[rows:] + 1.0)


def site_increment(refs, at):
    num = refs[0][0, :, at] + refs[1][0, :, at]
    den = refs[0][1, :, at] + refs[1][1, :, at]
    return 0.5 * num / (den + 1.0)


def update_kernel(a0, a1, b0, b1, s0, s1, mine_ref, theirs_ref,
                  new_mine, new_theirs, dsite_ref, dsrc_ref, send_ref, shift):
    ev_n = mine_ref.shape[0] - 1
    freqs, half = mine_ref.shape[1:]
    quarter = half // 2
    core = core_index()
    dsrc = increments(s0[...], s1[...])
    dsrc_ref[...] = dsrc
    for i in range(dsrc.shape[0]):
        shift[i * LANES:(i + 1) * LANES, :] = jnp.broadcast_to(dsrc[i:i + 1, :], (LANES, LANES)).T
    for refs, base in (((a0, a1), 0), ((b0, b1), quarter // TILE)):
        for t in range(quarter // TILE):
            at = slice(t * TILE, (t + 1) * TILE)
            there = slice((base + t) * TILE, (base + t + 1) * TILE)
            dsite_ref[:, there] = site_increment(refs, at)
    total = jnp.zeros((freqs, TILE), F32)
    for which, (ref, out) in enumerate(((mine_ref, new_mine), (theirs_ref, new_theirs))):
        owner = core if which == 0 else 1 - core
        out[ev_n] = ref[ev_n]
        for e in range(ev_n):
            first = pl.multiple_of((owner * ev_n + e) * freqs, freqs)
            src = shift[pl.ds(first, freqs), :]

            def step(t, acc, ref=ref, out=out, e=e, src=src):
                at = tile_at(t)
                resid = ref[e, :, at] - src - dsite_ref[:, at]
                out[e, :, at] = resid
                valid = jnp.broadcast_to(ref[ev_n, e:e + 1, at], (freqs, TILE))
                return acc + jnp.abs(resid) * valid
            total = lax.fori_loop(0, half // TILE, step, total, unroll=8)
    row = as_row(jnp.sum(total, axis=1, keepdims=True))
    send_ref[...] = jnp.broadcast_to(row, send_ref.shape)


def site_kernel(a0, a1, b0, b1, s0, s1, site_ref, dsite_ref, dsrc_ref,
                new_ref, src_ref, send_ref):
    freqs, half = dsite_ref.shape
    quarter = half // 2
    core = core_index()
    src_ref[...] = dsrc_ref[...] + increments(s0[...], s1[...])
    total = jnp.zeros((freqs, TILE), F32)
    for refs, base in (((a0, a1), 0), ((b0, b1), quarter // TILE)):
        for t in range(quarter // TILE):
            at = slice(t * TILE, (t + 1) * TILE)
            there = slice((base + t) * TILE, (base + t + 1) * TILE)
            init = site_ref[:, tile_at(core * (half // TILE) + base + t)]
            value = init + dsite_ref[:, there] + site_increment(refs, at)
            new_ref[:, there] = value
            total = total + value
    row = as_row(jnp.sum(total, axis=1, keepdims=True))
    send_ref[...] = jnp.broadcast_to(row, send_ref.shape)


def finish_kernel(total_ch, sums_ref, mine_ref, theirs_ref, source_ref, out_source, out_site):
    freqs, half = mine_ref.shape
    core = core_index()
    row = jnp.sum(sums_ref[...], axis=0, keepdims=True) / total_ch
    column = jnp.broadcast_to(as_column(row, freqs), (freqs, TILE))
    out_source[...] = source_ref[...] + row[:, :freqs]
    for ref, owner in ((mine_ref, core), (theirs_ref, 1 - core)):
        for t in range(half // TILE):
            at = tile_at(owner * (half // TILE) + t)
            out_site[:, at] = ref[:, t * TILE:(t + 1) * TILE] - column


def call(kernel, out_shape, in_specs, scratch=()):
    outs = [jax.ShapeDtypeStruct(shape, F32) for shape in out_shape]
    return pl.pallas_call(
        kernel,
        out_shape=outs,
        in_specs=in_specs,
        out_specs=[VMEM] * len(outs),
        scratch_shapes=list(scratch),
        compiler_params=pltpu.CompilerParams(vmem_limit_bytes=LIMIT),
    )


def swap(value, axis, size, bit):
    return lax.ppermute(value, axis, [(i, i ^ bit) for i in range(size)])


def on_device(spectra, tile_mask, source_init, site_init, event_pos, channel_pos, atten):
    ev_n, freqs, ch_n = spectra.shape
    ev_dev, ch_dev = lax.axis_size("ev"), lax.axis_size("ch")
    devices = ev_dev * ch_dev
    half, quarter = ch_n // 2, ch_n // 4
    slabs = (ev_n + 1, freqs, half)
    src_rows = 2 * ev_n * freqs // LANES
    ev_bits = [1 << k for k in range(1, ev_dev.bit_length() - 1)]
    ch_bits = [1 << k for k in range(ch_dev.bit_length() - 1)]
    pairs = [[(2 * g + c) * ch_dev + z for c in range(2) for z in range(ch_dev)] for g in range(ev_dev // 2)]

    mine, theirs, sums = call(
        resid_kernel, [slabs, slabs, (devices, LANES)], [ANY] + [VMEM] * 6,
        [pltpu.VMEM(spectra.shape, F32), pltpu.VMEM((ev_n, ch_n), F32),
         pltpu.VMEM((ev_n, freqs, TILE), F32), pltpu.SemaphoreType.DMA((ev_n,))],
    )(spectra, tile_mask, source_init, site_init, event_pos, channel_pos, atten.reshape(1, freqs))
    theirs = swap(theirs, "ev", ev_dev, 1)
    first = None
    for step in range(ITERS):
        total = lax.all_to_all(sums, ("ev", "ch"), 0, 0)
        first = total if first is None else first
        a, b, src = call(
            functools.partial(weight_kernel, freqs),
            [(2, freqs, quarter), (2, freqs, quarter), (2 * src_rows, LANES)], [VMEM] * 4,
        )(total, first, mine, theirs)
        src = src + swap(src, "ev", ev_dev, 1)
        for k in range(len(ev_bits)):
            a_other = swap(a, "ev", ev_dev, ev_bits[k])
            b_other = swap(b, "ev", ev_dev, ev_bits[(k + len(ev_bits) // 2) % len(ev_bits)])
            if k < len(ev_bits) - 1:
                a, b = a + a_other, b + b_other
        for k, bit in enumerate(ch_bits):
            src_other = swap(src, "ch", ch_dev, bit)
            if k < len(ch_bits) - 1:
                src = src + src_other
        parts = (a, a_other, b, b_other, src, src_other)
        if step < ITERS - 1:
            mine, theirs, dsite, dsrc, sums = call(
                update_kernel, [slabs, slabs, (freqs, half), (src_rows, LANES), (devices, LANES)], [VMEM] * 8,
                [pltpu.VMEM((src_rows * LANES, LANES), F32)],
            )(*parts, mine, theirs)
    site, dsrc, sums = call(
        site_kernel, [(freqs, half), (src_rows, LANES), (2 * ch_dev, LANES)], [VMEM] * 9,
    )(*parts, site_init, dsite, dsrc)
    site_other = swap(site, "ev", ev_dev, 1)
    sums = lax.all_to_all(sums, ("ev", "ch"), 0, 0, axis_index_groups=pairs)
    core = lax.rem(lax.axis_index("ev"), 2)
    own = lax.dynamic_slice(dsrc, (core * (src_rows // 2), 0), (src_rows // 2, LANES))
    source = source_init + own.reshape(ev_n, freqs)
    return tuple(call(
        functools.partial(finish_kernel, float(ch_n * ch_dev)), [(ev_n, freqs), (freqs, ch_n)], [VMEM] * 4,
    )(sums, site, site_other, source))


def solution(mesh):
    in_specs = (
        P("ev", None, "ch"),
        P("ev", "ch"),
        P("ev", None),
        P(None, "ch"),
        P(None, "ev"),
        P(None, "ch"),
        P(),
    )
    out_specs = (P("ev", None), P(None, "ch"))
    return jax.shard_map(
        on_device, mesh=mesh, in_specs=in_specs, out_specs=out_specs, check_vma=False
    )
```

time: 267 us -> 85 us (0.32)
  blocking collectives: 117 us -> 23 us
  waiting for transfers between devices: 110 us -> 29.9 us
  other arithmetic: 23.8 us -> 0.09 us
  between operations: 14.8 us -> 0.72 us
  Pallas kernels: 0 us -> 12.1 us
  starting transfers between devices: 0.08 us -> 12 us
  local copies, waits for them, and re-layouts: 1.16 us -> 6.71 us
    psum x4 -> x0, blocking collectives: 117 us -> none  [the longest x2 79.7 us: on_device(): absum, count = lax.psum((abs_part, count_part), ('ev', 'ch'))]
    psum x2 -> x0, waiting for transfers between devices: 110 us -> none  [on_device(): site_num, site_den = lax.psum((site_num, site_den), 'ev')]
    ppermute x0 -> x16, waiting for transfers between devices: none -> 24.6 us  [swap(): return lax.ppermute(value, axis, [(i, i ^ bit) for i in range(size)])]
    all_to_all x0 -> x2, blocking collectives: none -> 23 us  [on_device(): total = lax.all_to_all(sums, ('ev', 'ch'), 0, 0)]
    reduce_sum x7 -> x0, other arithmetic: 20.6 us -> none  [the longest x2 10.7 us: on_device(): site_num = jnp.sum(product, axis=0)]
    pallas_call x0 -> x6, Pallas kernels: none -> 12.1 us  [the longest x2 5.27 us: on_device(): call(functools.partial(weight_kernel, freqs), [(2, freqs, quarter), (2, f...]
    ppermute x0 -> x16, starting transfers between devices: none -> 8.74 us  [swap(): return lax.ppermute(value, axis, [(i, i ^ bit) for i in range(size)])]
    unnamed x7 -> x18, local copies, waits for them, and re-layouts: 0.18 us -> 6.62 us
  transfers between devices with their start and end apart: 2 -> 17, of which waited for: 2 -> 9; matrix products, arithmetic and copies ran while one was open for 0% -> 0% of each run, Pallas kernels for 0% -> 0%
where the time goes in v2:
time: 85 us; the launch traced here: 84.6 us
  waiting for transfers between devices  29.9 us (35%)
  blocking collectives  23 us (27%)
  Pallas kernels  12.1 us (14%)
  starting transfers between devices  12 us (14%)
  local copies, waits for them, and re-layouts  6.71 us (8%)
    ppermute x16, waiting for transfers between devices, swap(): return lax.ppermute(value, axis, [(i, i ^ bit) for i in range(size)])  24.6 us
    all_to_all x2, blocking collectives, on_device(): total = lax.all_to_all(sums, ('ev', 'ch'), 0, 0)  23 us
    ppermute x16, starting transfers between devices, swap(): return lax.ppermute(value, axis, [(i, i ^ bit) for i in range(size)])  8.74 us
    unnamed x18, local copies, waits for them, and re-layouts  6.62 us
    all_to_all x1, waiting for transfers between devices, on_device(): sums = lax.all_to_all(sums, ('ev', 'ch'), 0, 0, axis_index_groups=pairs)  5.29 us
    pallas_call x2, Pallas kernels, on_device(): call(functools.partial(weight_kernel, freqs), [(2, freqs, quarter), (2, f...  5.27 us
    all_to_all x1, starting transfers between devices, on_device(): sums = lax.all_to_all(sums, ('ev', 'ch'), 0, 0, axis_index_groups=pairs)  3.31 us
    pallas_call x1, Pallas kernels, on_device(): call(resid_kernel, [slabs, slabs, (devices, LANES)], [ANY] + [VMEM] * 6,...  3.26 us
  transfers between devices with their start and end apart: 17, of which 9 were waited for; matrix products, arithmetic and copies ran while one was open for 0% of the time, Pallas kernels for 0%

profile of v2, /device:TPU:0, one launch (start us, length us, event | category | flops | bytes accessed | tf_op | source)
XLA Modules:
  0.0 84.6 jit_solution(17157892993938695400)
XLA Ops:
  0.6 2.2 %copy-done = f32[16,16,4096]{2,1,0:T(8,128)S(1)} copy-done((f32[16,16,4096]{2,1,0:T(8,128)S(1)}, f32[16,16,4096]{2,1,0:T(8,128)}, u32[]{:S(2)}) %copy-start) | copy-done | bytes 4194328
  2.8 0.9 %copy-done.1 = f32[16,4096]{1,0:T(8,128)S(1)} copy-done((f32[16,4096]{1,0:T(8,128)S(1)}, f32[16,4096]{1,0:T(8,128)}, u32[]{:S(2)}) %copy-start.1) | copy-done | bytes 262168
  3.8 0.8 copy-done.3
  4.5 0.7 copy-done.4
  5.2 0.7 copy-done.6
  5.9 0.7 copy-done.7
  6.6 0.7 copy-done.8
  7.3 3.3 %shard_map.86 = (f32[17,16,2048]{2,1,0:T(8,128)S(1)}, f32[17,16,2048]{2,1,0:T(8,128)S(1)}, f32[32,128]{1,0:T(8,128)S(1)}) custom-call(f32[16,16,4096]{2,1,0:T(8,128)S(1)} %copy-done, s32[16,32]{1,0:T(8,128)S(1)} %copy-done.6, f32[16,16]{1,0:T(8,128)S(1)} %copy-done.4, f32[16,4096]{1,0:T(8,128)S(1)} %copy-done.1, f32[3,16]{1,0:T(4,128)S(1)} %copy-done.7, ...), custom_call_target="tpu_custom_call" | custom-call | tf_op jit(solution)/shard_map/pallas_call | solution.py:253
  11.0 13.9 %all_to_all.33 = f32[32,1,128]{2,1,0:T(1,128)S(1)} all-to-all(f32[32,1,128]{2,1,0:T(1,128)S(1)} %bitcast.19), channel_id=1, replica_groups=mesh['ev'=8,'ch'=4] {'ev','ch'}, dimensions={0} | all-to-all | bytes 32768 | tf_op jit(solution)/shard_map/all_to_all | solution.py:261
  25.0 2.6 %shard_map.87 = (f32[2,16,1024]{2,1,0:T(8,128)S(1)}, f32[2,16,1024]{2,1,0:T(8,128)S(1)}, f32[8,128]{1,0:T(8,128)S(1)}) custom-call(f32[32,128]{1,0:T(8,128)S(1)} %bitcast.13, f32[32,128]{1,0:T(8,128)S(1)} %bitcast.14, f32[17,16,2048]{2,1,0:T(8,128)S(1)} %get-tuple-element.20.mine_ref, f32[17,16,2048]{2,1,0:T(8,128)S(1)} %collective-permute-done.theirs_ref), custom_call_target="tpu_custom_call" | custom-call | tf_op jit(solution)/shard_map/pallas_call | solution.py:263
  27.6 0.7 collective-permute-start.3
  28.8 4.1 %collective-permute-done.3 = f32[2,16,1024]{2,1,0:T(8,128)S(1)} collective-permute-done((f32[2,16,1024]{2,1,0:T(8,128)S(1)}, f32[2,16,1024]{2,1,0:T(8,128)S(1)}, u32[]{:S(2)}, u32[]{:S(2)}) %collective-permute-start.3) | collective-permute-done | bytes 131104 | tf_op jit(solution)/shard_map/ppermute | solution.py:239
  32.9 0.6 collective-permute-start.4
  33.5 1.2 %collective-permute-start.2 = (f32[2,16,1024]{2,1,0:T(8,128)S(1)}, f32[2,16,1024]{2,1,0:T(8,128)S(1)}, u32[]{:S(2)}, u32[]{:S(2)}) collective-permute-start(f32[2,16,1024]{2,1,0:T(8,128)S(1)} %add.30.a0), channel_id=1, source_target_pairs={{0,16},{4,20},{8,24},{12,28},{16,0},{20,4},{24,8},{28,12},{1,17},{... | collective-permute-start | bytes 393224 | tf_op jit(solution)/shard_map/ppermute | solution.py:239
  34.8 1.2 %collective-permute-done.5 = f32[8,128]{1,0:T(8,128)S(1)} collective-permute-done((f32[8,128]{1,0:T(8,128)S(1)}, f32[8,128]{1,0:T(8,128)S(1)}, u32[]{:S(2)}, u32[]{:S(2)}) %collective-permute-start.5) | collective-permute-done | bytes 4128 | tf_op jit(solution)/shard_map/ppermute | solution.py:239
  36.5 3.1 %collective-permute-done.6 = f32[8,128]{1,0:T(8,128)S(1)} collective-permute-done((f32[8,128]{1,0:T(8,128)S(1)}, f32[8,128]{1,0:T(8,128)S(1)}, u32[]{:S(2)}, u32[]{:S(2)}) %collective-permute-start.6) | collective-permute-done | bytes 4128 | tf_op jit(solution)/shard_map/ppermute | solution.py:239
  39.5 0.5 collective-permute-start.7
  40.1 4.0 %collective-permute-done.7.s1 = f32[8,128]{1,0:T(8,128)S(1)} collective-permute-done((f32[8,128]{1,0:T(8,128)S(1)}, f32[8,128]{1,0:T(8,128)S(1)}, u32[]{:S(2)}, u32[]{:S(2)}) %collective-permute-start.7) | collective-permute-done | bytes 4128 | tf_op jit(solution)/shard_map/ppermute | solution.py:239
  44.1 2.0 %shard_map.88 = (f32[17,16,2048]{2,1,0:T(8,128)S(1)}, f32[17,16,2048]{2,1,0:T(8,128)S(1)}, f32[16,2048]{1,0:T(8,128)S(1)}, f32[4,128]{1,0:T(4,128)S(1)}, f32[32,128]{1,0:T(8,128)S(1)}) custom-call(f32[2,16,1024]{2,1,0:T(8,128)S(1)} %add.30.a0, f32[2,16,1024]{2,1,0:T(8,128)S(1)} %collective-permute-done.2.a1, f32[2,16,1024]{2,1,0:T(8,128)S(1)} %add.31.b0, ...), custom_call_target="tpu_custom_call" | custom-call | tf_op jit(solution)/shard_map/pallas_call | solution.py:279
  46.1 9.1 %all_to_all.34 = f32[32,1,128]{2,1,0:T(1,128)S(1)} all-to-all(f32[32,1,128]{2,1,0:T(1,128)S(1)} %bitcast.18), channel_id=1, replica_groups=mesh['ev'=8,'ch'=4] {'ev','ch'}, dimensions={0} | all-to-all | bytes 32768 | tf_op jit(solution)/shard_map/all_to_all | solution.py:261
  55.2 2.6 %shard_map.89 = (f32[2,16,1024]{2,1,0:T(8,128)S(1)}, f32[2,16,1024]{2,1,0:T(8,128)S(1)}, f32[8,128]{1,0:T(8,128)S(1)}) custom-call(f32[32,128]{1,0:T(8,128)S(1)} %bitcast.16, f32[32,128]{1,0:T(8,128)S(1)} %bitcast.15, f32[17,16,2048]{2,1,0:T(8,128)S(1)} %get-tuple-element.26.mine_ref, f32[17,16,2048]{2,1,0:T(8,128)S(1)} %get-tuple-element.27.theirs_ref), custom_call_target="tpu_custom_call" | custom-call | tf_op jit(solution)/shard_map/pallas_call | solution.py:263
  57.8 0.7 collective-permute-start.10
  59.0 4.1 %collective-permute-done.10 = f32[2,16,1024]{2,1,0:T(8,128)S(1)} collective-permute-done((f32[2,16,1024]{2,1,0:T(8,128)S(1)}, f32[2,16,1024]{2,1,0:T(8,128)S(1)}, u32[]{:S(2)}, u32[]{:S(2)}) %collective-permute-start.10) | collective-permute-done | bytes 131104 | tf_op jit(solution)/shard_map/ppermute | solution.py:239
  63.1 0.6 collective-permute-start.11
  63.7 1.2 %collective-permute-start.9 = (f32[2,16,1024]{2,1,0:T(8,128)S(1)}, f32[2,16,1024]{2,1,0:T(8,128)S(1)}, u32[]{:S(2)}, u32[]{:S(2)}) collective-permute-start(f32[2,16,1024]{2,1,0:T(8,128)S(1)} %add.34.a0), channel_id=1, source_target_pairs={{0,16},{4,20},{8,24},{12,28},{16,0},{20,4},{24,8},{28,12},{1,17},{... | collective-permute-start | bytes 393224 | tf_op jit(solution)/shard_map/ppermute | solution.py:239
  65.0 1.2 %collective-permute-done.12 = f32[8,128]{1,0:T(8,128)S(1)} collective-permute-done((f32[8,128]{1,0:T(8,128)S(1)}, f32[8,128]{1,0:T(8,128)S(1)}, u32[]{:S(2)}, u32[]{:S(2)}) %collective-permute-start.12) | collective-permute-done | bytes 4128 | tf_op jit(solution)/shard_map/ppermute | solution.py:239
  66.7 3.1 %collective-permute-done.13 = f32[8,128]{1,0:T(8,128)S(1)} collective-permute-done((f32[8,128]{1,0:T(8,128)S(1)}, f32[8,128]{1,0:T(8,128)S(1)}, u32[]{:S(2)}, u32[]{:S(2)}) %collective-permute-start.13) | collective-permute-done | bytes 4128 | tf_op jit(solution)/shard_map/ppermute | solution.py:239
  70.3 4.0 %collective-permute-done.14.s1 = f32[8,128]{1,0:T(8,128)S(1)} collective-permute-done((f32[8,128]{1,0:T(8,128)S(1)}, f32[8,128]{1,0:T(8,128)S(1)}, u32[]{:S(2)}, u32[]{:S(2)}) %collective-permute-start.14) | collective-permute-done | bytes 4128 | tf_op jit(solution)/shard_map/ppermute | solution.py:239
  74.3 0.7 shard_map.90
  75.0 3.3 %all-to-all-start.2 = ((f32[8,1,128]{2,1,0:T(1,128)}), f32[8,1,128]{2,1,0:T(1,128)S(1)}, u32[]{:S(2)}, u32[]{:S(2)}) async-start(f32[8,1,128]{2,1,0:T(1,128)} %bitcast.8), calls=%async_computation.2 | async-start | bytes 8192 | tf_op jit(solution)/shard_map/all_to_all | solution.py:287
  78.5 5.3 %all-to-all-done.2 = f32[8,1,128]{2,1,0:T(1,128)S(1)} async-done(((f32[8,1,128]{2,1,0:T(1,128)}), f32[8,1,128]{2,1,0:T(1,128)S(1)}, u32[]{:S(2)}, u32[]{:S(2)}) %all-to-all-start.2) | async-done | bytes 4128 | tf_op jit(solution)/shard_map/all_to_all | solution.py:287
  83.8 0.8 shard_map.91
  (39 shorter events, 3.4 us)
Async XLA Ops:
  0.6 2.2 %copy-start = (f32[16,16,4096]{2,1,0:T(8,128)S(1)}, f32[16,16,4096]{2,1,0:T(8,128)}, u32[]{:S(2)}) copy-start(f32[16,16,4096]{2,1,0:T(8,128)} %spec_hbm.1) | copy-start | bytes 12582916
  2.8 0.9 %copy-start.1 = (f32[16,4096]{1,0:T(8,128)S(1)}, f32[16,4096]{1,0:T(8,128)}, u32[]{:S(2)}) copy-start(f32[16,4096]{1,0:T(8,128)} %site_ref.3) | copy-start | bytes 786436
  3.8 0.8 copy-start.3
  4.5 0.7 copy-start.4
  5.2 0.7 copy-start.6
  5.9 0.7 copy-start.7
  6.6 0.7 copy-start.8
  10.5 14.4 %collective-permute-start = (f32[17,16,2048]{2,1,0:T(8,128)S(1)}, f32[17,16,2048]{2,1,0:T(8,128)S(1)}, u32[]{:S(2)}, u32[]{:S(2)}) collective-permute-start(f32[17,16,2048]{2,1,0:T(8,128)S(1)} %get-tuple-element.21), channel_id=1, source_target_pairs={{0,4},{4,0},{8,12},{12,8},{16,20},{20,16},{24,28},{28,24},{1,5},{5... | collective-permute-start | bytes 6684680 | tf_op jit(solution)/shard_map/ppermute | solution.py:239
  27.6 5.2 %collective-permute-start.3 = (f32[2,16,1024]{2,1,0:T(8,128)S(1)}, f32[2,16,1024]{2,1,0:T(8,128)S(1)}, u32[]{:S(2)}, u32[]{:S(2)}) collective-permute-start(f32[2,16,1024]{2,1,0:T(8,128)S(1)} %get-tuple-element.23), channel_id=1, source_target_pairs={{0,16},{4,20},{8,24},{12,28},{16,0},{20,4},{24,8},{28,12},{1,17},{... | collective-permute-start | bytes 393224 | tf_op jit(solution)/shard_map/ppermute | solution.py:239
  28.3 5.2 %collective-permute-start.1 = (f32[2,16,1024]{2,1,0:T(8,128)S(1)}, f32[2,16,1024]{2,1,0:T(8,128)S(1)}, u32[]{:S(2)}, u32[]{:S(2)}) collective-permute-start(f32[2,16,1024]{2,1,0:T(8,128)S(1)} %get-tuple-element.22), channel_id=1, source_target_pairs={{0,8},{4,12},{8,0},{12,4},{16,24},{20,28},{24,16},{28,20},{1,9},{5... | collective-permute-start | bytes 393224 | tf_op jit(solution)/shard_map/ppermute | solution.py:239
  32.9 11.2 %collective-permute-start.4 = (f32[2,16,1024]{2,1,0:T(8,128)S(1)}, f32[2,16,1024]{2,1,0:T(8,128)S(1)}, u32[]{:S(2)}, u32[]{:S(2)}) collective-permute-start(f32[2,16,1024]{2,1,0:T(8,128)S(1)} %add.31.b0), channel_id=1, source_target_pairs={{0,8},{4,12},{8,0},{12,4},{16,24},{20,28},{24,16},{28,20},{1,9},{5... | collective-permute-start | bytes 393224 | tf_op jit(solution)/shard_map/ppermute | solution.py:239
  33.5 10.5 %collective-permute-start.2 = (f32[2,16,1024]{2,1,0:T(8,128)S(1)}, f32[2,16,1024]{2,1,0:T(8,128)S(1)}, u32[]{:S(2)}, u32[]{:S(2)}) collective-permute-start(f32[2,16,1024]{2,1,0:T(8,128)S(1)} %add.30.a0), channel_id=1, source_target_pairs={{0,16},{4,20},{8,24},{12,28},{16,0},{20,4},{24,8},{28,12},{1,17},{... | collective-permute-start | bytes 393224 | tf_op jit(solution)/shard_map/ppermute | solution.py:239
  34.8 1.2 %collective-permute-start.5 = (f32[8,128]{1,0:T(8,128)S(1)}, f32[8,128]{1,0:T(8,128)S(1)}, u32[]{:S(2)}, u32[]{:S(2)}) collective-permute-start(f32[8,128]{1,0:T(8,128)S(1)} %get-tuple-element.24), channel_id=1, source_target_pairs={{0,4},{4,0},{8,12},{12,8},{16,20},{20,16},{24,28},{28,24},{1,5},{5... | collective-permute-start | bytes 12296 | tf_op jit(solution)/shard_map/ppermute | solution.py:239
  35.9 3.6 %collective-permute-start.6 = (f32[8,128]{1,0:T(8,128)S(1)}, f32[8,128]{1,0:T(8,128)S(1)}, u32[]{:S(2)}, u32[]{:S(2)}) collective-permute-start(f32[8,128]{1,0:T(8,128)S(1)} %add.32), channel_id=1, source_target_pairs={{0,1},{1,0},{2,3},{3,2},{4,5},{5,4},{6,7},{7,6},{8,9},{9,8},{10,11... | collective-permute-start | bytes 12296 | tf_op jit(solution)/shard_map/ppermute | solution.py:239
  39.5 4.5 %collective-permute-start.7 = (f32[8,128]{1,0:T(8,128)S(1)}, f32[8,128]{1,0:T(8,128)S(1)}, u32[]{:S(2)}, u32[]{:S(2)}) collective-permute-start(f32[8,128]{1,0:T(8,128)S(1)} %add.33.s0), channel_id=1, source_target_pairs={{0,2},{1,3},{2,0},{3,1},{4,6},{5,7},{6,4},{7,5},{8,10},{9,11},{10,... | collective-permute-start | bytes 12296 | tf_op jit(solution)/shard_map/ppermute | solution.py:239
  55.2 19.1 %copy-start.2 = (f32[16,4096]{1,0:T(8,128)S(1)}, f32[16,4096]{1,0:T(8,128)}, u32[]{:S(2)}) copy-start(f32[16,4096]{1,0:T(8,128)} %site_ref.3) | copy-start | bytes 786436
  55.2 23.3 %copy-start.5 = (f32[16,16]{1,0:T(8,128)S(1)}, f32[16,16]{1,0:T(8,128)}, u32[]{:S(2)}) copy-start(f32[16,16]{1,0:T(8,128)} %src_ref.1) | copy-start | bytes 3076
  57.8 5.2 %collective-permute-start.10 = (f32[2,16,1024]{2,1,0:T(8,128)S(1)}, f32[2,16,1024]{2,1,0:T(8,128)S(1)}, u32[]{:S(2)}, u32[]{:S(2)}) collective-permute-start(f32[2,16,1024]{2,1,0:T(8,128)S(1)} %get-tuple-element.29), channel_id=1, source_target_pairs={{0,16},{4,20},{8,24},{12,28},{16,0},{20,4},{24,8},{28,12},{1,17},{... | collective-permute-start | bytes 393224 | tf_op jit(solution)/shard_map/ppermute | solution.py:239
  58.5 5.2 %collective-permute-start.8 = (f32[2,16,1024]{2,1,0:T(8,128)S(1)}, f32[2,16,1024]{2,1,0:T(8,128)S(1)}, u32[]{:S(2)}, u32[]{:S(2)}) collective-permute-start(f32[2,16,1024]{2,1,0:T(8,128)S(1)} %get-tuple-element.28), channel_id=1, source_target_pairs={{0,8},{4,12},{8,0},{12,4},{16,24},{20,28},{24,16},{28,20},{1,9},{5... | collective-permute-start | bytes 393224 | tf_op jit(solution)/shard_map/ppermute | solution.py:239
  63.1 11.2 %collective-permute-start.11 = (f32[2,16,1024]{2,1,0:T(8,128)S(1)}, f32[2,16,1024]{2,1,0:T(8,128)S(1)}, u32[]{:S(2)}, u32[]{:S(2)}) collective-permute-start(f32[2,16,1024]{2,1,0:T(8,128)S(1)} %add.35.b0), channel_id=1, source_target_pairs={{0,8},{4,12},{8,0},{12,4},{16,24},{20,28},{24,16},{28,20},{1,9},{5... | collective-permute-start | bytes 393224 | tf_op jit(solution)/shard_map/ppermute | solution.py:239
  63.7 10.5 %collective-permute-start.9 = (f32[2,16,1024]{2,1,0:T(8,128)S(1)}, f32[2,16,1024]{2,1,0:T(8,128)S(1)}, u32[]{:S(2)}, u32[]{:S(2)}) collective-permute-start(f32[2,16,1024]{2,1,0:T(8,128)S(1)} %add.34.a0), channel_id=1, source_target_pairs={{0,16},{4,20},{8,24},{12,28},{16,0},{20,4},{24,8},{28,12},{1,17},{... | collective-permute-start | bytes 393224 | tf_op jit(solution)/shard_map/ppermute | solution.py:239
  65.0 1.2 %collective-permute-start.12 = (f32[8,128]{1,0:T(8,128)S(1)}, f32[8,128]{1,0:T(8,128)S(1)}, u32[]{:S(2)}, u32[]{:S(2)}) collective-permute-start(f32[8,128]{1,0:T(8,128)S(1)} %get-tuple-element.30), channel_id=1, source_target_pairs={{0,4},{4,0},{8,12},{12,8},{16,20},{20,16},{24,28},{28,24},{1,5},{5... | collective-permute-start | bytes 12296 | tf_op jit(solution)/shard_map/ppermute | solution.py:239
  66.1 3.6 %collective-permute-start.13 = (f32[8,128]{1,0:T(8,128)S(1)}, f32[8,128]{1,0:T(8,128)S(1)}, u32[]{:S(2)}, u32[]{:S(2)}) collective-permute-start(f32[8,128]{1,0:T(8,128)S(1)} %add.36), channel_id=1, source_target_pairs={{0,1},{1,0},{2,3},{3,2},{4,5},{5,4},{6,7},{7,6},{8,9},{9,8},{10,11... | collective-permute-start | bytes 12296 | tf_op jit(solution)/shard_map/ppermute | solution.py:239
  69.8 4.5 %collective-permute-start.14 = (f32[8,128]{1,0:T(8,128)S(1)}, f32[8,128]{1,0:T(8,128)S(1)}, u32[]{:S(2)}, u32[]{:S(2)}) collective-permute-start(f32[8,128]{1,0:T(8,128)S(1)} %add.37.s0), channel_id=1, source_target_pairs={{0,2},{1,3},{2,0},{3,1},{4,6},{5,7},{6,4},{7,5},{8,10},{9,11},{10,... | collective-permute-start | bytes 12296 | tf_op jit(solution)/shard_map/ppermute | solution.py:239
  75.0 8.7 %collective-permute-start.15 = (f32[16,2048]{1,0:T(8,128)S(1)}, f32[16,2048]{1,0:T(8,128)S(1)}, u32[]{:S(2)}, u32[]{:S(2)}) collective-permute-start(f32[16,2048]{1,0:T(8,128)S(1)} %get-tuple-element.34.mine_ref), channel_id=1, source_target_pairs={{0,4},{4,0},{8,12},{12,8},{16,20},{20,16},{24,28},{28,24},{1,5},{5... | collective-permute-start | bytes 393224 | tf_op jit(solution)/shard_map/ppermute | solution.py:239
  75.0 8.7 %all-to-all-start.2 = ((f32[8,1,128]{2,1,0:T(1,128)}), f32[8,1,128]{2,1,0:T(1,128)S(1)}, u32[]{:S(2)}, u32[]{:S(2)}) async-start(f32[8,1,128]{2,1,0:T(1,128)} %bitcast.8), calls=%async_computation.2 | async-start | bytes 8192 | tf_op jit(solution)/shard_map/all_to_all | solution.py:287

commit v3 on v2

--- a/solution.py
+++ b/solution.py
@@ -13,7 +13,7 @@
 GROUP = 4
 F32 = jnp.float32
 VMEM = pl.BlockSpec(memory_space=pltpu.VMEM)
-ANY = pl.BlockSpec(memory_space=pl.ANY)
+HBM = pl.BlockSpec(memory_space=pltpu.HBM)
 LIMIT = 24 * 1024 * 1024
 
 
@@ -45,17 +45,27 @@
     return lax.rem(lax.axis_index("ev"), 2)
 
 
-def resid_kernel(spec_hbm, mask_ref, src_ref, site_ref, pos_ref, chan_ref, atten_ref,
-                 mine_ref, theirs_ref, send_ref, spec, travel, source, sems):
+def resid_kernel(spec_hbm, mask_hbm, src_hbm, site_hbm, pos_hbm, chan_hbm, atten_hbm,
+                 mine_ref, theirs_ref, send_ref, mask_ref, src_ref, site_ref, pos_ref, chan_ref, atten_ref,
+                 spec, travel, source, small_sems, sems):
     ev_n, freqs, ch_n = spec_hbm.shape
     half = ch_n // 2
     half_tiles = half // TILE
     core = core_index()
+    small = []
+    for i, (src, dst) in enumerate((
+            (pos_hbm, pos_ref), (chan_hbm, chan_ref), (mask_hbm, mask_ref),
+            (atten_hbm, atten_ref), (src_hbm, src_ref), (site_hbm, site_ref))):
+        copy = pltpu.make_async_copy(src, dst, small_sems.at[i])
+        copy.start()
+        small.append(copy)
     copies = []
     for e in range(ev_n):
         copy = pltpu.make_async_copy(spec_hbm.at[e], spec.at[e], sems.at[e])
         copy.start()
         copies.append(copy)
+    for copy in small:
+        copy.wait()
     maskf = mask_ref[...].astype(F32)
     low, high = maskf[:, :half_tiles], maskf[:, half_tiles:]
     upper = core == 1
@@ -250,11 +260,16 @@
     ch_bits = [1 << k for k in range(ch_dev.bit_length() - 1)]
     pairs = [[(2 * g + c) * ch_dev + z for c in range(2) for z in range(ch_dev)] for g in range(ev_dev // 2)]
 
+    inputs = [pltpu.with_memory_space_constraint(x, pltpu.HBM) for x in (
+        spectra, tile_mask, source_init, site_init, event_pos, channel_pos, atten.reshape(1, freqs))]
+    small = inputs[1:]
     mine, theirs, sums = call(
-        resid_kernel, [slabs, slabs, (devices, LANES)], [ANY] + [VMEM] * 6,
-        [pltpu.VMEM(spectra.shape, F32), pltpu.VMEM((ev_n, ch_n), F32),
-         pltpu.VMEM((ev_n, freqs, TILE), F32), pltpu.SemaphoreType.DMA((ev_n,))],
-    )(spectra, tile_mask, source_init, site_init, event_pos, channel_pos, atten.reshape(1, freqs))
+        resid_kernel, [slabs, slabs, (devices, LANES)], [HBM] * 7,
+        [pltpu.VMEM(x.shape, x.dtype) for x in small]
+        + [pltpu.VMEM(spectra.shape, F32), pltpu.VMEM((ev_n, ch_n), F32),
+           pltpu.VMEM((ev_n, freqs, TILE), F32), pltpu.SemaphoreType.DMA((len(small),)),
+           pltpu.SemaphoreType.DMA((ev_n,))],
+    )(*inputs)
     theirs = swap(theirs, "ev", ev_dev, 1)
     first = None
     for step in range(ITERS):
@@ -265,15 +280,20 @@
             [(2, freqs, quarter), (2, freqs, quarter), (2 * src_rows, LANES)], [VMEM] * 4,
         )(total, first, mine, theirs)
         src = src + swap(src, "ev", ev_dev, 1)
-        for k in range(len(ev_bits)):
-            a_other = swap(a, "ev", ev_dev, ev_bits[k])
-            b_other = swap(b, "ev", ev_dev, ev_bits[(k + len(ev_bits) // 2) % len(ev_bits)])
-            if k < len(ev_bits) - 1:
-                a, b = a + a_other, b + b_other
-        for k, bit in enumerate(ch_bits):
-            src_other = swap(src, "ch", ch_dev, bit)
-            if k < len(ch_bits) - 1:
-                src = src + src_other
+        src_other = jnp.zeros_like(src)
+        for k in range(max(len(ev_bits), len(ch_bits))):
+            if k > 0:
+                a_sum, b_sum, src_sum = a, b, src
+                if k < len(ev_bits):
+                    a_sum, b_sum = a + a_other, b + b_other
+                if k < len(ch_bits):
+                    src_sum = src + src_other
+                a, b, src = lax.optimization_barrier((a_sum, b_sum, src_sum))
+            if k < len(ev_bits):
+                a_other = swap(a, "ev", ev_dev, ev_bits[k])
+                b_other = swap(b, "ev", ev_dev, ev_bits[(k + len(ev_bits) // 2) % len(ev_bits)])
+            if k < len(ch_bits):
+                src_other = swap(src, "ch", ch_dev, ch_bits[k])
         parts = (a, a_other, b, b_other, src, src_other)
         if step < ITERS - 1:
             mine, theirs, dsite, dsrc, sums = call(

time: 85 us -> 74 us (0.87)
  waiting for transfers between devices: 29.9 us -> 21.7 us
  local copies, waits for them, and re-layouts: 6.71 us -> 0.09 us
  starting transfers between devices: 12 us -> 14.4 us
  Pallas kernels: 12.1 us -> 14 us
    ppermute x16, waiting for transfers between devices: 24.6 us -> 16.4 us  [swap(): return lax.ppermute(value, axis, [(i, i ^ bit) for i in range(size)])]
    unnamed x18 -> x4, local copies, waits for them, and re-layouts: 6.62 us -> 0.01 us
    ppermute x16, starting transfers between devices: 8.74 us -> 11 us  [swap(): return lax.ppermute(value, axis, [(i, i ^ bit) for i in range(size)])]
    pallas_call x1, Pallas kernels: 3.26 us -> 5.15 us  [on_device(): call(resid_kernel, [slabs, slabs, (devices, LANES)], [HBM] * 7, [pltpu.VM...]
  transfers between devices with their start and end apart: 17 -> 17, of which waited for: 9 -> 7; matrix products, arithmetic and copies ran while one was open for 0% -> 0% of each run, Pallas kernels for 0% -> 0%
where the time goes in v3:
time: 74 us; the launch traced here: 73.8 us
  blocking collectives  22.8 us (31%)
  waiting for transfers between devices  21.7 us (29%)
  starting transfers between devices  14.4 us (19%)
  Pallas kernels  14 us (19%)
    all_to_all x2, blocking collectives, on_device(): total = lax.all_to_all(sums, ('ev', 'ch'), 0, 0)  22.8 us
    ppermute x16, waiting for transfers between devices, swap(): return lax.ppermute(value, axis, [(i, i ^ bit) for i in range(size)])  16.4 us
    ppermute x16, starting transfers between devices, swap(): return lax.ppermute(value, axis, [(i, i ^ bit) for i in range(size)])  11 us
    all_to_all x1, waiting for transfers between devices, on_device(): sums = lax.all_to_all(sums, ('ev', 'ch'), 0, 0, axis_index_groups=pairs)  5.29 us
    pallas_call x2, Pallas kernels, on_device(): call(functools.partial(weight_kernel, freqs), [(2, freqs, quarter), (2, f...  5.27 us
    pallas_call x1, Pallas kernels, on_device(): call(resid_kernel, [slabs, slabs, (devices, LANES)], [HBM] * 7, [pltpu.VM...  5.15 us
    all_to_all x1, starting transfers between devices, on_device(): sums = lax.all_to_all(sums, ('ev', 'ch'), 0, 0, axis_index_groups=pairs)  3.31 us
    pallas_call x1, Pallas kernels, on_device(): call(update_kernel, [slabs, slabs, (freqs, half), (src_rows, LANES), (dev...  2.01 us
  transfers between devices with their start and end apart: 17, of which 7 were waited for; matrix products, arithmetic and copies ran while one was open for 0% of the time, Pallas kernels for 0%

profile of v3, /device:TPU:0, one launch (start us, length us, event | category | flops | bytes accessed | tf_op | source)
XLA Modules:
  0.0 73.8 jit_solution(15822564443347050366)
XLA Ops:
  0.6 5.2 %shard_map.86 = (f32[17,16,2048]{2,1,0:T(8,128)S(1)}, f32[17,16,2048]{2,1,0:T(8,128)S(1)}, f32[32,128]{1,0:T(8,128)S(1)}) custom-call(f32[16,16,4096]{2,1,0:T(8,128)} %spec_hbm.1, s32[16,32]{1,0:T(8,128)} %mask_hbm.1, f32[16,16]{1,0:T(8,128)} %src_hbm.1, f32[16,4096]{1,0:T(8,128)} %site_ref.1, f32[3,16]{1,0:T(4,128)} %pos_hbm.1, f32[2,4096]{1,0:T(2,128)} %chan_hbm.1, ...), custom_call_target="tpu_custom_call" | custom-call | tf_op jit(solution)/shard_map/pallas_call | solution.py:266
  5.8 0.5 collective-permute-start
  6.3 13.9 %all_to_all.33 = f32[32,1,128]{2,1,0:T(1,128)S(1)} all-to-all(f32[32,1,128]{2,1,0:T(1,128)S(1)} %bitcast.19), channel_id=1, replica_groups=mesh['ev'=8,'ch'=4] {'ev','ch'}, dimensions={0} | all-to-all | bytes 32768 | tf_op jit(solution)/shard_map/all_to_all | solution.py:276
  20.2 0.0 collective-permute-done.theirs_ref
  20.2 2.6 %shard_map.87 = (f32[2,16,1024]{2,1,0:T(8,128)S(1)}, f32[2,16,1024]{2,1,0:T(8,128)S(1)}, f32[8,128]{1,0:T(8,128)S(1)}) custom-call(f32[32,128]{1,0:T(8,128)S(1)} %bitcast.13, f32[32,128]{1,0:T(8,128)S(1)} %bitcast.14, f32[17,16,2048]{2,1,0:T(8,128)S(1)} %get-tuple-element.26.mine_ref, f32[17,16,2048]{2,1,0:T(8,128)S(1)} %collective-permute-done.theirs_ref), custom_call_target="tpu_custom_call" | custom-call | tf_op jit(solution)/shard_map/pallas_call | solution.py:278
  22.9 0.7 collective-permute-start.2
  23.5 0.5 collective-permute-start.1
  24.1 0.0 collective-permute-start.3
  24.1 1.2 %collective-permute-done.3 = f32[8,128]{1,0:T(8,128)S(1)} collective-permute-done((f32[8,128]{1,0:T(8,128)S(1)}, f32[8,128]{1,0:T(8,128)S(1)}, u32[]{:S(2)}, u32[]{:S(2)}) %collective-permute-start.3) | collective-permute-done | bytes 4128 | tf_op jit(solution)/shard_map/ppermute | solution.py:249
  25.2 0.5 collective-permute-start.4
  25.8 3.1 %collective-permute-done.4 = f32[8,128]{1,0:T(8,128)S(1)} collective-permute-done((f32[8,128]{1,0:T(8,128)S(1)}, f32[8,128]{1,0:T(8,128)S(1)}, u32[]{:S(2)}, u32[]{:S(2)}) %collective-permute-start.4) | collective-permute-done | bytes 4128 | tf_op jit(solution)/shard_map/ppermute | solution.py:249
  28.9 1.6 %collective-permute-start.5 = (f32[2,16,1024]{2,1,0:T(8,128)S(1)}, f32[2,16,1024]{2,1,0:T(8,128)S(1)}, u32[]{:S(2)}, u32[]{:S(2)}) collective-permute-start(f32[2,16,1024]{2,1,0:T(8,128)S(1)} %add.30.a0), channel_id=1, source_target_pairs={{0,16},{4,20},{8,24},{12,28},{16,0},{20,4},{24,8},{28,12},{1,17},{... | collective-permute-start | bytes 393224 | tf_op jit(solution)/shard_map/ppermute | solution.py:249
  30.5 1.4 %collective-permute-start.6 = (f32[2,16,1024]{2,1,0:T(8,128)S(1)}, f32[2,16,1024]{2,1,0:T(8,128)S(1)}, u32[]{:S(2)}, u32[]{:S(2)}) collective-permute-start(f32[2,16,1024]{2,1,0:T(8,128)S(1)} %add.31.b0), channel_id=1, source_target_pairs={{0,8},{4,12},{8,0},{12,4},{16,24},{20,28},{24,16},{28,20},{1,9},{5... | collective-permute-start | bytes 393224 | tf_op jit(solution)/shard_map/ppermute | solution.py:249
  31.9 0.5 collective-permute-start.7
  32.4 4.0 %collective-permute-done.7.s1 = f32[8,128]{1,0:T(8,128)S(1)} collective-permute-done((f32[8,128]{1,0:T(8,128)S(1)}, f32[8,128]{1,0:T(8,128)S(1)}, u32[]{:S(2)}, u32[]{:S(2)}) %collective-permute-start.7) | collective-permute-done | bytes 4128 | tf_op jit(solution)/shard_map/ppermute | solution.py:249
  36.4 2.0 %shard_map.88 = (f32[17,16,2048]{2,1,0:T(8,128)S(1)}, f32[17,16,2048]{2,1,0:T(8,128)S(1)}, f32[16,2048]{1,0:T(8,128)S(1)}, f32[4,128]{1,0:T(4,128)S(1)}, f32[32,128]{1,0:T(8,128)S(1)}) custom-call(f32[2,16,1024]{2,1,0:T(8,128)S(1)} %add.30.a0, f32[2,16,1024]{2,1,0:T(8,128)S(1)} %collective-permute-done.5.a1, f32[2,16,1024]{2,1,0:T(8,128)S(1)} %add.31.b0, ...), custom_call_target="tpu_custom_call" | custom-call | tf_op jit(solution)/shard_map/pallas_call | solution.py:299
  38.4 8.8 %all_to_all.34 = f32[32,1,128]{2,1,0:T(1,128)S(1)} all-to-all(f32[32,1,128]{2,1,0:T(1,128)S(1)} %bitcast.18), channel_id=1, replica_groups=mesh['ev'=8,'ch'=4] {'ev','ch'}, dimensions={0} | all-to-all | bytes 32768 | tf_op jit(solution)/shard_map/all_to_all | solution.py:276
  47.3 2.6 %shard_map.89 = (f32[2,16,1024]{2,1,0:T(8,128)S(1)}, f32[2,16,1024]{2,1,0:T(8,128)S(1)}, f32[8,128]{1,0:T(8,128)S(1)}) custom-call(f32[32,128]{1,0:T(8,128)S(1)} %bitcast.16, f32[32,128]{1,0:T(8,128)S(1)} %bitcast.15, f32[17,16,2048]{2,1,0:T(8,128)S(1)} %get-tuple-element.35.mine_ref, f32[17,16,2048]{2,1,0:T(8,128)S(1)} %get-tuple-element.36.theirs_ref), custom_call_target="tpu_custom_call" | custom-call | tf_op jit(solution)/shard_map/pallas_call | solution.py:278
  49.9 0.7 collective-permute-start.9
  50.6 0.5 collective-permute-start.8
  51.1 1.2 %collective-permute-done.10 = f32[8,128]{1,0:T(8,128)S(1)} collective-permute-done((f32[8,128]{1,0:T(8,128)S(1)}, f32[8,128]{1,0:T(8,128)S(1)}, u32[]{:S(2)}, u32[]{:S(2)}) %collective-permute-start.10) | collective-permute-done | bytes 4128 | tf_op jit(solution)/shard_map/ppermute | solution.py:249
  52.3 0.5 collective-permute-start.11
  52.8 3.1 %collective-permute-done.11 = f32[8,128]{1,0:T(8,128)S(1)} collective-permute-done((f32[8,128]{1,0:T(8,128)S(1)}, f32[8,128]{1,0:T(8,128)S(1)}, u32[]{:S(2)}, u32[]{:S(2)}) %collective-permute-start.11) | collective-permute-done | bytes 4128 | tf_op jit(solution)/shard_map/ppermute | solution.py:249
  55.9 1.6 %collective-permute-start.12 = (f32[2,16,1024]{2,1,0:T(8,128)S(1)}, f32[2,16,1024]{2,1,0:T(8,128)S(1)}, u32[]{:S(2)}, u32[]{:S(2)}) collective-permute-start(f32[2,16,1024]{2,1,0:T(8,128)S(1)} %add.34.a0), channel_id=1, source_target_pairs={{0,16},{4,20},{8,24},{12,28},{16,0},{20,4},{24,8},{28,12},{1,17},{... | collective-permute-start | bytes 393224 | tf_op jit(solution)/shard_map/ppermute | solution.py:249
  57.5 1.4 %collective-permute-start.13 = (f32[2,16,1024]{2,1,0:T(8,128)S(1)}, f32[2,16,1024]{2,1,0:T(8,128)S(1)}, u32[]{:S(2)}, u32[]{:S(2)}) collective-permute-start(f32[2,16,1024]{2,1,0:T(8,128)S(1)} %add.35.b0), channel_id=1, source_target_pairs={{0,8},{4,12},{8,0},{12,4},{16,24},{20,28},{24,16},{28,20},{1,9},{5... | collective-permute-start | bytes 393224 | tf_op jit(solution)/shard_map/ppermute | solution.py:249
  58.9 0.5 collective-permute-start.14
  59.5 4.0 %collective-permute-done.14.s1 = f32[8,128]{1,0:T(8,128)S(1)} collective-permute-done((f32[8,128]{1,0:T(8,128)S(1)}, f32[8,128]{1,0:T(8,128)S(1)}, u32[]{:S(2)}, u32[]{:S(2)}) %collective-permute-start.14) | collective-permute-done | bytes 4128 | tf_op jit(solution)/shard_map/ppermute | solution.py:249
  63.5 0.7 %shard_map.90 = (f32[16,2048]{1,0:T(8,128)S(1)}, f32[4,128]{1,0:T(4,128)S(1)}, f32[8,128]{1,0:T(8,128)}) custom-call(f32[2,16,1024]{2,1,0:T(8,128)S(1)} %add.34.a0, f32[2,16,1024]{2,1,0:T(8,128)S(1)} %collective-permute-done.12.a1, f32[2,16,1024]{2,1,0:T(8,128)S(1)} %add.35.b0, f32[2,16,1024]{2,1,0:T(8,128)S(1)} %collective-permute-done.13.b1, ...), custom_call_target="tpu_custom_call" | custom-call | tf_op jit(solution)/shard_map/pallas_call | solution.py:303
  64.2 3.3 %all-to-all-start.2 = ((f32[8,1,128]{2,1,0:T(1,128)}), f32[8,1,128]{2,1,0:T(1,128)S(1)}, u32[]{:S(2)}, u32[]{:S(2)}) async-start(f32[8,1,128]{2,1,0:T(1,128)} %bitcast.8), calls=%async_computation.2 | async-start | bytes 8192 | tf_op jit(solution)/shard_map/all_to_all | solution.py:307
  67.5 0.1 reshape.17
  67.6 5.3 %all-to-all-done.2 = f32[8,1,128]{2,1,0:T(1,128)S(1)} async-done(((f32[8,1,128]{2,1,0:T(1,128)}), f32[8,1,128]{2,1,0:T(1,128)S(1)}, u32[]{:S(2)}, u32[]{:S(2)}) %all-to-all-start.2) | async-done | bytes 4128 | tf_op jit(solution)/shard_map/all_to_all | solution.py:307
  72.9 0.8 %shard_map.91 = (f32[16,16]{1,0:T(8,128)}, f32[16,4096]{1,0:T(8,128)}) custom-call(f32[8,128]{1,0:T(8,128)S(1)} %bitcast.17, f32[16,2048]{1,0:T(8,128)S(1)} %get-tuple-element.46.mine_ref, f32[16,2048]{1,0:T(8,128)S(1)} %collective-permute-done.15.theirs_ref, f32[16,16]{1,0:T(8,128)S(1)} %add.39.source_ref), custom_call_target="tpu_custom_call" | custom-call | tf_op jit(solution)/shard_map/pallas_call | solution.py:311
  (25 shorter events, 0.1 us)
Async XLA Ops:
  5.8 14.4 %collective-permute-start = (f32[17,16,2048]{2,1,0:T(8,128)S(1)}, f32[17,16,2048]{2,1,0:T(8,128)S(1)}, u32[]{:S(2)}, u32[]{:S(2)}) collective-permute-start(f32[17,16,2048]{2,1,0:T(8,128)S(1)} %get-tuple-element.27), channel_id=1, source_target_pairs={{0,4},{4,0},{8,12},{12,8},{16,20},{20,16},{24,28},{28,24},{1,5},{5... | collective-permute-start | bytes 6684680 | tf_op jit(solution)/shard_map/ppermute | solution.py:249
  22.9 6.0 %collective-permute-start.2 = (f32[2,16,1024]{2,1,0:T(8,128)S(1)}, f32[2,16,1024]{2,1,0:T(8,128)S(1)}, u32[]{:S(2)}, u32[]{:S(2)}) collective-permute-start(f32[2,16,1024]{2,1,0:T(8,128)S(1)} %get-tuple-element.29), channel_id=1, source_target_pairs={{0,16},{4,20},{8,24},{12,28},{16,0},{20,4},{24,8},{28,12},{1,17},{... | collective-permute-start | bytes 393224 | tf_op jit(solution)/shard_map/ppermute | solution.py:249
  23.5 5.3 %collective-permute-start.1 = (f32[2,16,1024]{2,1,0:T(8,128)S(1)}, f32[2,16,1024]{2,1,0:T(8,128)S(1)}, u32[]{:S(2)}, u32[]{:S(2)}) collective-permute-start(f32[2,16,1024]{2,1,0:T(8,128)S(1)} %get-tuple-element.28), channel_id=1, source_target_pairs={{0,8},{4,12},{8,0},{12,4},{16,24},{20,28},{24,16},{28,20},{1,9},{5... | collective-permute-start | bytes 393224 | tf_op jit(solution)/shard_map/ppermute | solution.py:249
  24.1 1.2 %collective-permute-start.3 = (f32[8,128]{1,0:T(8,128)S(1)}, f32[8,128]{1,0:T(8,128)S(1)}, u32[]{:S(2)}, u32[]{:S(2)}) collective-permute-start(f32[8,128]{1,0:T(8,128)S(1)} %get-tuple-element.30), channel_id=1, source_target_pairs={{0,4},{4,0},{8,12},{12,8},{16,20},{20,16},{24,28},{28,24},{1,5},{5... | collective-permute-start | bytes 12296 | tf_op jit(solution)/shard_map/ppermute | solution.py:249
  25.2 3.6 %collective-permute-start.4 = (f32[8,128]{1,0:T(8,128)S(1)}, f32[8,128]{1,0:T(8,128)S(1)}, u32[]{:S(2)}, u32[]{:S(2)}) collective-permute-start(f32[8,128]{1,0:T(8,128)S(1)} %add.32), channel_id=1, source_target_pairs={{0,1},{1,0},{2,3},{3,2},{4,5},{5,4},{6,7},{7,6},{8,9},{9,8},{10,11... | collective-permute-start | bytes 12296 | tf_op jit(solution)/shard_map/ppermute | solution.py:249
  28.9 7.5 %collective-permute-start.5 = (f32[2,16,1024]{2,1,0:T(8,128)S(1)}, f32[2,16,1024]{2,1,0:T(8,128)S(1)}, u32[]{:S(2)}, u32[]{:S(2)}) collective-permute-start(f32[2,16,1024]{2,1,0:T(8,128)S(1)} %add.30.a0), channel_id=1, source_target_pairs={{0,16},{4,20},{8,24},{12,28},{16,0},{20,4},{24,8},{28,12},{1,17},{... | collective-permute-start | bytes 393224 | tf_op jit(solution)/shard_map/ppermute | solution.py:249
  30.5 6.0 %collective-permute-start.6 = (f32[2,16,1024]{2,1,0:T(8,128)S(1)}, f32[2,16,1024]{2,1,0:T(8,128)S(1)}, u32[]{:S(2)}, u32[]{:S(2)}) collective-permute-start(f32[2,16,1024]{2,1,0:T(8,128)S(1)} %add.31.b0), channel_id=1, source_target_pairs={{0,8},{4,12},{8,0},{12,4},{16,24},{20,28},{24,16},{28,20},{1,9},{5... | collective-permute-start | bytes 393224 | tf_op jit(solution)/shard_map/ppermute | solution.py:249
  31.9 4.5 %collective-permute-start.7 = (f32[8,128]{1,0:T(8,128)S(1)}, f32[8,128]{1,0:T(8,128)S(1)}, u32[]{:S(2)}, u32[]{:S(2)}) collective-permute-start(f32[8,128]{1,0:T(8,128)S(1)} %add.33.s0), channel_id=1, source_target_pairs={{0,2},{1,3},{2,0},{3,1},{4,6},{5,7},{6,4},{7,5},{8,10},{9,11},{10,... | collective-permute-start | bytes 12296 | tf_op jit(solution)/shard_map/ppermute | solution.py:249
  47.3 16.2 %copy-start = (f32[16,4096]{1,0:T(8,128)S(1)}, f32[16,4096]{1,0:T(8,128)}, u32[]{:S(2)}) copy-start(f32[16,4096]{1,0:T(8,128)} %site_ref.1) | copy-start | bytes 786436
  47.3 20.4 %copy-start.1 = (f32[16,16]{1,0:T(8,128)S(1)}, f32[16,16]{1,0:T(8,128)}, u32[]{:S(2)}) copy-start(f32[16,16]{1,0:T(8,128)} %src_hbm.1) | copy-start | bytes 3076
  49.9 6.0 %collective-permute-start.9 = (f32[2,16,1024]{2,1,0:T(8,128)S(1)}, f32[2,16,1024]{2,1,0:T(8,128)S(1)}, u32[]{:S(2)}, u32[]{:S(2)}) collective-permute-start(f32[2,16,1024]{2,1,0:T(8,128)S(1)} %get-tuple-element.38), channel_id=1, source_target_pairs={{0,16},{4,20},{8,24},{12,28},{16,0},{20,4},{24,8},{28,12},{1,17},{... | collective-permute-start | bytes 393224 | tf_op jit(solution)/shard_map/ppermute | solution.py:249
  50.6 5.3 %collective-permute-start.8 = (f32[2,16,1024]{2,1,0:T(8,128)S(1)}, f32[2,16,1024]{2,1,0:T(8,128)S(1)}, u32[]{:S(2)}, u32[]{:S(2)}) collective-permute-start(f32[2,16,1024]{2,1,0:T(8,128)S(1)} %get-tuple-element.37), channel_id=1, source_target_pairs={{0,8},{4,12},{8,0},{12,4},{16,24},{20,28},{24,16},{28,20},{1,9},{5... | collective-permute-start | bytes 393224 | tf_op jit(solution)/shard_map/ppermute | solution.py:249
  51.1 1.2 %collective-permute-start.10 = (f32[8,128]{1,0:T(8,128)S(1)}, f32[8,128]{1,0:T(8,128)S(1)}, u32[]{:S(2)}, u32[]{:S(2)}) collective-permute-start(f32[8,128]{1,0:T(8,128)S(1)} %get-tuple-element.39), channel_id=1, source_target_pairs={{0,4},{4,0},{8,12},{12,8},{16,20},{20,16},{24,28},{28,24},{1,5},{5... | collective-permute-start | bytes 12296 | tf_op jit(solution)/shard_map/ppermute | solution.py:249
  52.3 3.6 %collective-permute-start.11 = (f32[8,128]{1,0:T(8,128)S(1)}, f32[8,128]{1,0:T(8,128)S(1)}, u32[]{:S(2)}, u32[]{:S(2)}) collective-permute-start(f32[8,128]{1,0:T(8,128)S(1)} %add.36), channel_id=1, source_target_pairs={{0,1},{1,0},{2,3},{3,2},{4,5},{5,4},{6,7},{7,6},{8,9},{9,8},{10,11... | collective-permute-start | bytes 12296 | tf_op jit(solution)/shard_map/ppermute | solution.py:249
  55.9 7.5 %collective-permute-start.12 = (f32[2,16,1024]{2,1,0:T(8,128)S(1)}, f32[2,16,1024]{2,1,0:T(8,128)S(1)}, u32[]{:S(2)}, u32[]{:S(2)}) collective-permute-start(f32[2,16,1024]{2,1,0:T(8,128)S(1)} %add.34.a0), channel_id=1, source_target_pairs={{0,16},{4,20},{8,24},{12,28},{16,0},{20,4},{24,8},{28,12},{1,17},{... | collective-permute-start | bytes 393224 | tf_op jit(solution)/shard_map/ppermute | solution.py:249
  57.5 6.0 %collective-permute-start.13 = (f32[2,16,1024]{2,1,0:T(8,128)S(1)}, f32[2,16,1024]{2,1,0:T(8,128)S(1)}, u32[]{:S(2)}, u32[]{:S(2)}) collective-permute-start(f32[2,16,1024]{2,1,0:T(8,128)S(1)} %add.35.b0), channel_id=1, source_target_pairs={{0,8},{4,12},{8,0},{12,4},{16,24},{20,28},{24,16},{28,20},{1,9},{5... | collective-permute-start | bytes 393224 | tf_op jit(solution)/shard_map/ppermute | solution.py:249
  58.9 4.5 %collective-permute-start.14 = (f32[8,128]{1,0:T(8,128)S(1)}, f32[8,128]{1,0:T(8,128)S(1)}, u32[]{:S(2)}, u32[]{:S(2)}) collective-permute-start(f32[8,128]{1,0:T(8,128)S(1)} %add.37.s0), channel_id=1, source_target_pairs={{0,2},{1,3},{2,0},{3,1},{4,6},{5,7},{6,4},{7,5},{8,10},{9,11},{10,... | collective-permute-start | bytes 12296 | tf_op jit(solution)/shard_map/ppermute | solution.py:249
  64.2 8.7 %collective-permute-start.15 = (f32[16,2048]{1,0:T(8,128)S(1)}, f32[16,2048]{1,0:T(8,128)S(1)}, u32[]{:S(2)}, u32[]{:S(2)}) collective-permute-start(f32[16,2048]{1,0:T(8,128)S(1)} %get-tuple-element.46.mine_ref), channel_id=1, source_target_pairs={{0,4},{4,0},{8,12},{12,8},{16,20},{20,16},{24,28},{28,24},{1,5},{5... | collective-permute-start | bytes 393224 | tf_op jit(solution)/shard_map/ppermute | solution.py:249
  64.2 8.7 %all-to-all-start.2 = ((f32[8,1,128]{2,1,0:T(1,128)}), f32[8,1,128]{2,1,0:T(1,128)S(1)}, u32[]{:S(2)}, u32[]{:S(2)}) async-start(f32[8,1,128]{2,1,0:T(1,128)} %bitcast.8), calls=%async_computation.2 | async-start | bytes 8192 | tf_op jit(solution)/shard_map/all_to_all | solution.py:307

commit v4 on v3

--- a/solution.py
+++ b/solution.py
@@ -11,6 +11,8 @@
 LANES = 128
 TILE = 128
 GROUP = 4
+CHAINS = 4
+BATCH = 4
 F32 = jnp.float32
 VMEM = pl.BlockSpec(memory_space=pltpu.VMEM)
 HBM = pl.BlockSpec(memory_space=pltpu.HBM)
@@ -59,13 +61,13 @@
         copy = pltpu.make_async_copy(src, dst, small_sems.at[i])
         copy.start()
         small.append(copy)
-    copies = []
-    for e in range(ev_n):
-        copy = pltpu.make_async_copy(spec_hbm.at[e], spec.at[e], sems.at[e])
+    copies = [pltpu.make_async_copy(spec_hbm.at[e], spec.at[e], sems.at[e]) for e in range(ev_n)]
+    for copy in copies[:4]:
         copy.start()
-        copies.append(copy)
     for copy in small:
         copy.wait()
+    for copy in copies[4:]:
+        copy.start()
     maskf = mask_ref[...].astype(F32)
     low, high = maskf[:, :half_tiles], maskf[:, half_tiles:]
     upper = core == 1
@@ -87,21 +89,27 @@
     att = jnp.broadcast_to(as_column(widen(atten_ref[...]), freqs), (freqs, TILE))
     for e in range(ev_n):
         source[e] = jnp.broadcast_to(as_column(widen(src_ref[e:e + 1, :]), freqs), (freqs, TILE))
-    total = jnp.zeros((freqs, TILE), F32)
-    for e in range(ev_n):
-        copies[e].wait()
-        src = source[e]
-        for ref, own in ((mine_ref, True), (theirs_ref, False)):
-            base = (core if own else 1 - core) * half_tiles
-
-            def step(t, acc, ref=ref, base=base, e=e, src=src):
-                here, at = tile_at(t), tile_at(base + t)
-                time = jnp.broadcast_to(travel[e:e + 1, at], (freqs, TILE))
-                resid = (spec[e, :, at] - src) + (att * time - site_ref[:, at])
-                ref[e, :, here] = resid
-                valid = jnp.broadcast_to(ref[ev_n, e:e + 1, here], (freqs, TILE))
-                return acc + jnp.abs(resid) * valid
-            total = lax.fori_loop(0, half_tiles, step, total, unroll=8)
+    totals = (jnp.zeros((freqs, TILE), F32),) * CHAINS
+    for start in range(0, ev_n, BATCH):
+        events = range(start, start + BATCH)
+        for e in events:
+            copies[e].wait()
+
+        def step(t, totals, events=events):
+            totals = list(totals)
+            here = tile_at(t)
+            for ref, own in ((mine_ref, True), (theirs_ref, False)):
+                at = tile_at((core if own else 1 - core) * half_tiles + t)
+                site = site_ref[:, at]
+                for k, e in enumerate(events):
+                    time = jnp.broadcast_to(travel[e:e + 1, at], (freqs, TILE))
+                    resid = (spec[e, :, at] - source[e]) + (att * time - site)
+                    ref[e, :, here] = resid
+                    valid = jnp.broadcast_to(ref[ev_n, e:e + 1, here], (freqs, TILE))
+                    totals[k % CHAINS] += jnp.abs(resid) * valid
+            return tuple(totals)
+        totals = lax.fori_loop(0, half_tiles, step, totals, unroll=2)
+    total = sum(totals[1:], totals[0])
     row = as_row(jnp.sum(total, axis=1, keepdims=True))
     lane = lax.broadcasted_iota(jnp.int32, row.shape, 1)
     row = row + jnp.where(lane == freqs, jnp.broadcast_to(count, row.shape), 0.0)
@@ -125,11 +133,13 @@
     b_ref[...] = jnp.zeros_like(b_ref)
     for which, ref in enumerate((mine_ref, theirs_ref)):
         owner = core if which == 0 else 1 - core
+        final = which == 1
         nums, dens = [], []
         for start in range(0, ev_n, GROUP):
             events = range(start, start + GROUP)
-
-            def step(t, acc, ref=ref, events=events):
+            scale = final and start + GROUP >= ev_n
+
+            def step(t, acc, ref=ref, events=events, scale=scale):
                 acc = list(acc)
                 for out, base in ((a_ref, 0), (b_ref, quarter // TILE)):
                     here, at = tile_at(t), tile_at(base + t)
@@ -137,44 +147,48 @@
                     for k, e in enumerate(events):
                         resid = ref[e, :, at]
                         valid = jnp.broadcast_to(ref[ev_n, e:e + 1, at], (freqs, TILE))
-                        weight = valid * delta / jnp.maximum(jnp.abs(resid), delta)
+                        weight = pl.reciprocal(jnp.maximum(jnp.abs(resid), delta), approx=True) * valid
                         product = weight * resid
                         num, den = num + product, den + weight
                         acc[2 * k] += product
                         acc[2 * k + 1] += weight
+                    if scale:
+                        num, den = num * delta, den * delta
                     out[0, :, here] = num
                     out[1, :, here] = den
                 return tuple(acc)
-            acc = lax.fori_loop(0, quarter // TILE, step, (zero,) * (2 * GROUP))
-            nums += acc[0::2]
-            dens += acc[1::2]
+            acc = lax.fori_loop(0, quarter // TILE, step, (zero,) * (2 * GROUP), unroll=8)
+            nums += [x * delta for x in acc[0::2]]
+            dens += [x * delta for x in acc[1::2]]
         rows_each = ev_n // per_row
         for kind, parts in ((0, nums), (1, dens)):
             for i in range(rows_each):
                 block = jnp.concatenate(parts[i * per_row:(i + 1) * per_row], axis=0)
                 line = jnp.sum(block.T, axis=0, keepdims=True)
-                src_ref[pl.ds(kind * 2 * rows_each + owner * rows_each + i, 1), :] = line
-
-
-def increments(src_a, src_b):
-    sums = src_a + src_b
-    rows = sums.shape[0] // 2
-    return 0.5 * sums[:rows] / (sums[rows:] + 1.0)
+                at_row = kind * 2 * rows_each + owner * rows_each + i
+                for copy in range(src_ref.shape[0]):
+                    src_ref[copy, pl.ds(at_row, 1), :] = line
+
+
+def increments(num, den):
+    return 0.5 * num / (den + 1.0)
 
 
 def site_increment(refs, at):
     num = refs[0][0, :, at] + refs[1][0, :, at]
     den = refs[0][1, :, at] + refs[1][1, :, at]
-    return 0.5 * num / (den + 1.0)
-
-
-def update_kernel(a0, a1, b0, b1, s0, s1, mine_ref, theirs_ref,
+    return increments(num, den)
+
+
+def update_kernel(a0, a1, b0, b1, sums_ref, mine_ref, theirs_ref,
                   new_mine, new_theirs, dsite_ref, dsrc_ref, send_ref, shift):
     ev_n = mine_ref.shape[0] - 1
     freqs, half = mine_ref.shape[1:]
     quarter = half // 2
     core = core_index()
-    dsrc = increments(s0[...], s1[...])
+    sums = jnp.sum(sums_ref[...], axis=0)
+    rows = dsrc_ref.shape[0]
+    dsrc = increments(sums[:rows], sums[rows:])
     dsrc_ref[...] = dsrc
     for i in range(dsrc.shape[0]):
         shift[i * LANES:(i + 1) * LANES, :] = jnp.broadcast_to(dsrc[i:i + 1, :], (LANES, LANES)).T
@@ -183,31 +197,32 @@
             at = slice(t * TILE, (t + 1) * TILE)
             there = slice((base + t) * TILE, (base + t + 1) * TILE)
             dsite_ref[:, there] = site_increment(refs, at)
-    total = jnp.zeros((freqs, TILE), F32)
+    totals = (jnp.zeros((freqs, TILE), F32),) * CHAINS
     for which, (ref, out) in enumerate(((mine_ref, new_mine), (theirs_ref, new_theirs))):
         owner = core if which == 0 else 1 - core
         out[ev_n] = ref[ev_n]
-        for e in range(ev_n):
-            first = pl.multiple_of((owner * ev_n + e) * freqs, freqs)
-            src = shift[pl.ds(first, freqs), :]
-
-            def step(t, acc, ref=ref, out=out, e=e, src=src):
-                at = tile_at(t)
-                resid = ref[e, :, at] - src - dsite_ref[:, at]
+
+        def step(t, totals, ref=ref, out=out, owner=owner):
+            totals = list(totals)
+            at = tile_at(t)
+            site = dsite_ref[:, at]
+            for e in range(ev_n):
+                src = shift[pl.ds(pl.multiple_of((owner * ev_n + e) * freqs, freqs), freqs), :]
+                resid = (ref[e, :, at] - src) - site
                 out[e, :, at] = resid
                 valid = jnp.broadcast_to(ref[ev_n, e:e + 1, at], (freqs, TILE))
-                return acc + jnp.abs(resid) * valid
-            total = lax.fori_loop(0, half // TILE, step, total, unroll=8)
+                totals[e % CHAINS] += jnp.abs(resid) * valid
+            return tuple(totals)
+        totals = lax.fori_loop(0, half // TILE, step, totals, unroll=2)
+    total = sum(totals[1:], totals[0])
     row = as_row(jnp.sum(total, axis=1, keepdims=True))
     send_ref[...] = jnp.broadcast_to(row, send_ref.shape)
 
 
-def site_kernel(a0, a1, b0, b1, s0, s1, site_ref, dsite_ref, dsrc_ref,
-                new_ref, src_ref, send_ref):
+def site_kernel(a0, a1, b0, b1, src_ref, site_ref, dsite_ref, new_ref, send_ref):
     freqs, half = dsite_ref.shape
     quarter = half // 2
     core = core_index()
-    src_ref[...] = dsrc_ref[...] + increments(s0[...], s1[...])
     total = jnp.zeros((freqs, TILE), F32)
     for refs, base in (((a0, a1), 0), ((b0, b1), quarter // TILE)):
         for t in range(quarter // TILE):
@@ -218,19 +233,33 @@
             new_ref[:, there] = value
             total = total + value
     row = as_row(jnp.sum(total, axis=1, keepdims=True))
-    send_ref[...] = jnp.broadcast_to(row, send_ref.shape)
-
-
-def finish_kernel(total_ch, sums_ref, mine_ref, theirs_ref, source_ref, out_source, out_site):
+    rows = src_ref.shape[1] // 4
+    count = send_ref.shape[0] // 2
+    for owner in range(2):
+        parts = [src_ref[0, (2 * kind + owner) * rows:(2 * kind + owner + 1) * rows, :] for kind in range(2)]
+        pad = jnp.zeros((send_ref.shape[1] - 2 * rows - 1, LANES), F32)
+        block = jnp.concatenate(parts + [row, pad], axis=0)
+        for copy in range(count):
+            send_ref[owner * count + copy] = block
+
+
+def finish_kernel(total_ch, sums_ref, mine_ref, theirs_ref, dsrc_ref, source_ref, out_source, out_site):
     freqs, half = mine_ref.shape
     core = core_index()
-    row = jnp.sum(sums_ref[...], axis=0, keepdims=True) / total_ch
+    sums = jnp.sum(sums_ref[...], axis=0)
+    rows = dsrc_ref.shape[0] // 2
+    row = sums[2 * rows:2 * rows + 1] / total_ch
     column = jnp.broadcast_to(as_column(row, freqs), (freqs, TILE))
-    out_source[...] = source_ref[...] + row[:, :freqs]
     for ref, owner in ((mine_ref, core), (theirs_ref, 1 - core)):
         for t in range(half // TILE):
             at = tile_at(owner * (half // TILE) + t)
             out_site[:, at] = ref[:, t * TILE:(t + 1) * TILE] - column
+    change = dsrc_ref[pl.ds(core * rows, rows), :] + increments(sums[:rows], sums[rows:2 * rows])
+    per_row = LANES // freqs
+    for e in range(source_ref.shape[0]):
+        first = (e % per_row) * freqs
+        piece = change[e // per_row:e // per_row + 1, first:first + freqs]
+        out_source[e:e + 1, :] = source_ref[e:e + 1, :] + piece + row[:, :freqs]
 
 
 def call(kernel, out_shape, in_specs, scratch=()):
@@ -273,44 +302,44 @@
     theirs = swap(theirs, "ev", ev_dev, 1)
     first = None
     for step in range(ITERS):
+        last = step == ITERS - 1
         total = lax.all_to_all(sums, ("ev", "ch"), 0, 0)
         first = total if first is None else first
         a, b, src = call(
             functools.partial(weight_kernel, freqs),
-            [(2, freqs, quarter), (2, freqs, quarter), (2 * src_rows, LANES)], [VMEM] * 4,
+            [(2, freqs, quarter), (2, freqs, quarter), (1, 2 * src_rows, LANES)],
+            [VMEM] * 4,
         )(total, first, mine, theirs)
-        src = src + swap(src, "ev", ev_dev, 1)
-        src_other = jnp.zeros_like(src)
+        if not last:
+            src = src + swap(src, "ev", ev_dev, 1)
         for k in range(max(len(ev_bits), len(ch_bits))):
             if k > 0:
-                a_sum, b_sum, src_sum = a, b, src
                 if k < len(ev_bits):
-                    a_sum, b_sum = a + a_other, b + b_other
-                if k < len(ch_bits):
-                    src_sum = src + src_other
-                a, b, src = lax.optimization_barrier((a_sum, b_sum, src_sum))
+                    a, b = a + a_other, b + b_other
+                if not last and k <= len(ch_bits):
+                    src = src + src_other
+                    a, b, _ = lax.optimization_barrier((a, b, src))
             if k < len(ev_bits):
                 a_other = swap(a, "ev", ev_dev, ev_bits[k])
                 b_other = swap(b, "ev", ev_dev, ev_bits[(k + len(ev_bits) // 2) % len(ev_bits)])
-            if k < len(ch_bits):
+            if not last and k < len(ch_bits):
                 src_other = swap(src, "ch", ch_dev, ch_bits[k])
-        parts = (a, a_other, b, b_other, src, src_other)
-        if step < ITERS - 1:
+        if not last:
+            src = src + src_other
+        parts = (a, a_other, b, b_other, src)
+        if not last:
             mine, theirs, dsite, dsrc, sums = call(
-                update_kernel, [slabs, slabs, (freqs, half), (src_rows, LANES), (devices, LANES)], [VMEM] * 8,
+                update_kernel, [slabs, slabs, (freqs, half), (src_rows, LANES), (devices, LANES)], [VMEM] * 7,
                 [pltpu.VMEM((src_rows * LANES, LANES), F32)],
             )(*parts, mine, theirs)
-    site, dsrc, sums = call(
-        site_kernel, [(freqs, half), (src_rows, LANES), (2 * ch_dev, LANES)], [VMEM] * 9,
-    )(*parts, site_init, dsite, dsrc)
+    site, sums = call(
+        site_kernel, [(freqs, half), (len(pairs[0]), 8, LANES)], [VMEM] * 7,
+    )(*parts, site_init, dsite)
     site_other = swap(site, "ev", ev_dev, 1)
     sums = lax.all_to_all(sums, ("ev", "ch"), 0, 0, axis_index_groups=pairs)
-    core = lax.rem(lax.axis_index("ev"), 2)
-    own = lax.dynamic_slice(dsrc, (core * (src_rows // 2), 0), (src_rows // 2, LANES))
-    source = source_init + own.reshape(ev_n, freqs)
     return tuple(call(
-        functools.partial(finish_kernel, float(ch_n * ch_dev)), [(ev_n, freqs), (freqs, ch_n)], [VMEM] * 4,
-    )(sums, site, site_other, source))
+        functools.partial(finish_kernel, float(ch_n * ch_dev)), [(ev_n, freqs), (freqs, ch_n)], [VMEM] * 5,
+    )(sums, site, site_other, dsrc, source_init))
 
 
 def solution(mesh):

time: 74 us -> 66.4 us (0.90)
  blocking collectives: 22.8 us -> 30.9 us
  waiting for transfers between devices: 21.7 us -> 16.1 us
  starting transfers between devices: 14.4 us -> 8.86 us
  Pallas kernels: 14 us -> 9.47 us
    all_to_all x0 -> x1, blocking collectives: none -> 8.15 us  [on_device(): sums = lax.all_to_all(sums, ('ev', 'ch'), 0, 0, axis_index_groups=pairs)]
    all_to_all x1 -> x0, waiting for transfers between devices: 5.29 us -> none  [on_device(): sums = lax.all_to_all(sums, ('ev', 'ch'), 0, 0, axis_index_groups=pairs)]
    all_to_all x1 -> x0, starting transfers between devices: 3.31 us -> none  [on_device(): sums = lax.all_to_all(sums, ('ev', 'ch'), 0, 0, axis_index_groups=pairs)]
    ppermute x16 -> x13, starting transfers between devices: 11 us -> 8.86 us  [swap(): return lax.ppermute(value, axis, [(i, i ^ bit) for i in range(size)])]
    pallas_call x2, Pallas kernels: 5.27 us -> 3.45 us  [on_device(): call(functools.partial(weight_kernel, freqs), [(2, freqs, quarter), (2, f...]
    pallas_call x1, Pallas kernels: 5.15 us -> 3.68 us  [on_device(): call(resid_kernel, [slabs, slabs, (devices, LANES)], [HBM] * 7, [pltpu.VM...]
    ppermute x16 -> x13, waiting for transfers between devices: 16.4 us -> 16.1 us  [swap(): return lax.ppermute(value, axis, [(i, i ^ bit) for i in range(size)])]
  transfers between devices with their start and end apart: 17 -> 13, of which waited for: 7 -> 6; matrix products, arithmetic and copies ran while one was open for 0% -> 0% of each run, Pallas kernels for 0% -> 0%
where the time goes in v4:
time: 66.4 us; the launch traced here: 66.2 us
  blocking collectives  30.9 us (47%)
  waiting for transfers between devices  16.1 us (24%)
  Pallas kernels  9.47 us (14%)
  starting transfers between devices  8.86 us (13%)
  between operations  0.7 us (1%)
    all_to_all x2, blocking collectives, on_device(): total = lax.all_to_all(sums, ('ev', 'ch'), 0, 0)  22.8 us
    ppermute x13, waiting for transfers between devices, swap(): return lax.ppermute(value, axis, [(i, i ^ bit) for i in range(size)])  16.1 us
    ppermute x13, starting transfers between devices, swap(): return lax.ppermute(value, axis, [(i, i ^ bit) for i in range(size)])  8.86 us
    all_to_all x1, blocking collectives, on_device(): sums = lax.all_to_all(sums, ('ev', 'ch'), 0, 0, axis_index_groups=pairs)  8.15 us
    pallas_call x1, Pallas kernels, on_device(): call(resid_kernel, [slabs, slabs, (devices, LANES)], [HBM] * 7, [pltpu.VM...  3.68 us
    pallas_call x2, Pallas kernels, on_device(): call(functools.partial(weight_kernel, freqs), [(2, freqs, quarter), (2, f...  3.45 us
    pallas_call x1, Pallas kernels, on_device(): call(update_kernel, [slabs, slabs, (freqs, half), (src_rows, LANES), (dev...  1.36 us
  transfers between devices with their start and end apart: 13, of which 6 were waited for; matrix products, arithmetic and copies ran while one was open for 0% of the time, Pallas kernels for 0%

profile of v4, /device:TPU:0, one launch (start us, length us, event | category | flops | bytes accessed | tf_op | source)
XLA Modules:
  0.0 66.2 jit_solution(228550161351650032)
XLA Ops:
  0.6 3.7 %shard_map.86 = (f32[17,16,2048]{2,1,0:T(8,128)S(1)}, f32[17,16,2048]{2,1,0:T(8,128)S(1)}, f32[32,128]{1,0:T(8,128)S(1)}) custom-call(f32[16,16,4096]{2,1,0:T(8,128)} %spec_hbm.1, s32[16,32]{1,0:T(8,128)} %mask_hbm.1, f32[16,16]{1,0:T(8,128)} %source_ref.1, f32[16,4096]{1,0:T(8,128)} %site_ref.1, f32[3,16]{1,0:T(4,128)} %pos_hbm.1, f32[2,4096]{1,0:T(2,128)} %chan_hbm.1, ...), custom_call_target="tpu_custom_call" | custom-call | tf_op jit(solution)/shard_map/pallas_call | solution.py:295
  4.3 0.5 collective-permute-start
  4.8 13.9 %all_to_all.27 = f32[32,1,128]{2,1,0:T(1,128)S(1)} all-to-all(f32[32,1,128]{2,1,0:T(1,128)S(1)} %bitcast.14), channel_id=1, replica_groups=mesh['ev'=8,'ch'=4] {'ev','ch'}, dimensions={0} | all-to-all | bytes 32768 | tf_op jit(solution)/shard_map/all_to_all | solution.py:306
  18.8 0.0 collective-permute-done.theirs_ref
  18.8 1.7 %shard_map.87 = (f32[2,16,1024]{2,1,0:T(8,128)S(1)}, f32[2,16,1024]{2,1,0:T(8,128)S(1)}, f32[1,8,128]{2,1,0:T(8,128)S(1)}) custom-call(f32[32,128]{1,0:T(8,128)S(1)} %bitcast.9, f32[32,128]{1,0:T(8,128)S(1)} %bitcast.10, f32[17,16,2048]{2,1,0:T(8,128)S(1)} %get-tuple-element.21.mine_ref, f32[17,16,2048]{2,1,0:T(8,128)S(1)} %collective-permute-done.theirs_ref), custom_call_target="tpu_custom_call" | custom-call | tf_op jit(solution)/shard_map/pallas_call | solution.py:308
  20.5 0.6 collective-permute-start.1
  21.2 0.5 collective-permute-start.2
  21.7 0.0 collective-permute-start.3
  21.7 1.2 %collective-permute-done.3 = f32[1,8,128]{2,1,0:T(8,128)S(1)} collective-permute-done((f32[1,8,128]{2,1,0:T(8,128)S(1)}, f32[1,8,128]{2,1,0:T(8,128)S(1)}, u32[]{:S(2)}, u32[]{:S(2)}) %collective-permute-start.3) | collective-permute-done | bytes 4128 | tf_op jit(solution)/shard_map/ppermute | solution.py:278
  22.9 0.5 collective-permute-start.4
  23.4 3.1 %collective-permute-done.4 = f32[1,8,128]{2,1,0:T(8,128)S(1)} collective-permute-done((f32[1,8,128]{2,1,0:T(8,128)S(1)}, f32[1,8,128]{2,1,0:T(8,128)S(1)}, u32[]{:S(2)}, u32[]{:S(2)}) %collective-permute-start.4) | collective-permute-done | bytes 4128 | tf_op jit(solution)/shard_map/ppermute | solution.py:278
  26.5 1.6 %collective-permute-start.5 = (f32[2,16,1024]{2,1,0:T(8,128)S(1)}, f32[2,16,1024]{2,1,0:T(8,128)S(1)}, u32[]{:S(2)}, u32[]{:S(2)}) collective-permute-start(f32[2,16,1024]{2,1,0:T(8,128)S(1)} %add.21.a0), channel_id=1, source_target_pairs={{0,16},{4,20},{8,24},{12,28},{16,0},{20,4},{24,8},{28,12},{1,17},{... | collective-permute-start | bytes 393224 | tf_op jit(solution)/shard_map/ppermute | solution.py:278
  28.1 1.4 %collective-permute-start.6 = (f32[2,16,1024]{2,1,0:T(8,128)S(1)}, f32[2,16,1024]{2,1,0:T(8,128)S(1)}, u32[]{:S(2)}, u32[]{:S(2)}) collective-permute-start(f32[2,16,1024]{2,1,0:T(8,128)S(1)} %add.22.b0), channel_id=1, source_target_pairs={{0,8},{4,12},{8,0},{12,4},{16,24},{20,28},{24,16},{28,20},{1,9},{5... | collective-permute-start | bytes 393224 | tf_op jit(solution)/shard_map/ppermute | solution.py:278
  29.5 0.5 collective-permute-start.7
  30.1 4.0 %collective-permute-done.7 = f32[1,8,128]{2,1,0:T(8,128)S(1)} collective-permute-done((f32[1,8,128]{2,1,0:T(8,128)S(1)}, f32[1,8,128]{2,1,0:T(8,128)S(1)}, u32[]{:S(2)}, u32[]{:S(2)}) %collective-permute-start.7) | collective-permute-done | bytes 4128 | tf_op jit(solution)/shard_map/ppermute | solution.py:278
  34.0 0.0 collective-permute-done.5.a1
  34.1 1.4 %shard_map.88 = (f32[17,16,2048]{2,1,0:T(8,128)S(1)}, f32[17,16,2048]{2,1,0:T(8,128)S(1)}, f32[16,2048]{1,0:T(8,128)S(1)}, f32[4,128]{1,0:T(4,128)S(1)}, f32[32,128]{1,0:T(8,128)S(1)}) custom-call(f32[2,16,1024]{2,1,0:T(8,128)S(1)} %add.21.a0, f32[2,16,1024]{2,1,0:T(8,128)S(1)} %collective-permute-done.5.a1, f32[2,16,1024]{2,1,0:T(8,128)S(1)} %add.22.b0, ...), custom_call_target="tpu_custom_call" | custom-call | tf_op jit(solution)/shard_map/pallas_call | solution.py:331
  35.4 8.9 %all_to_all.28 = f32[32,1,128]{2,1,0:T(1,128)S(1)} all-to-all(f32[32,1,128]{2,1,0:T(1,128)S(1)} %bitcast.13), channel_id=1, replica_groups=mesh['ev'=8,'ch'=4] {'ev','ch'}, dimensions={0} | all-to-all | bytes 32768 | tf_op jit(solution)/shard_map/all_to_all | solution.py:306
  44.3 1.7 %shard_map.89 = (f32[2,16,1024]{2,1,0:T(8,128)S(1)}, f32[2,16,1024]{2,1,0:T(8,128)S(1)}, f32[1,8,128]{2,1,0:T(8,128)S(1)}) custom-call(f32[32,128]{1,0:T(8,128)S(1)} %bitcast.12, f32[32,128]{1,0:T(8,128)S(1)} %bitcast.11, f32[17,16,2048]{2,1,0:T(8,128)S(1)} %get-tuple-element.29.mine_ref, f32[17,16,2048]{2,1,0:T(8,128)S(1)} %get-tuple-element.30.theirs_ref), custom_call_target="tpu_custom_call" | custom-call | tf_op jit(solution)/shard_map/pallas_call | solution.py:308
  46.0 0.6 collective-permute-start.8
  46.7 0.5 collective-permute-start.10
  47.2 4.1 %collective-permute-done.8 = f32[2,16,1024]{2,1,0:T(8,128)S(1)} collective-permute-done((f32[2,16,1024]{2,1,0:T(8,128)S(1)}, f32[2,16,1024]{2,1,0:T(8,128)S(1)}, u32[]{:S(2)}, u32[]{:S(2)}) %collective-permute-start.8) | collective-permute-done | bytes 131104 | tf_op jit(solution)/shard_map/ppermute | solution.py:278
  51.3 0.7 collective-permute-start.9
  51.9 0.0 collective-permute-done.10
  51.9 1.2 %collective-permute-start.11 = (f32[2,16,1024]{2,1,0:T(8,128)S(1)}, f32[2,16,1024]{2,1,0:T(8,128)S(1)}, u32[]{:S(2)}, u32[]{:S(2)}) collective-permute-start(f32[2,16,1024]{2,1,0:T(8,128)S(1)} %add.27.b0), channel_id=1, source_target_pairs={{0,8},{4,12},{8,0},{12,4},{16,24},{20,28},{24,16},{28,20},{1,9},{5... | collective-permute-start | bytes 393224 | tf_op jit(solution)/shard_map/ppermute | solution.py:278
  53.2 3.1 %collective-permute-done.9.a1 = f32[2,16,1024]{2,1,0:T(8,128)S(1)} collective-permute-done((f32[2,16,1024]{2,1,0:T(8,128)S(1)}, f32[2,16,1024]{2,1,0:T(8,128)S(1)}, u32[]{:S(2)}, u32[]{:S(2)}) %collective-permute-start.9) | collective-permute-done | bytes 131104 | tf_op jit(solution)/shard_map/ppermute | solution.py:278
  56.3 0.7 %collective-permute-done.11.b1 = f32[2,16,1024]{2,1,0:T(8,128)S(1)} collective-permute-done((f32[2,16,1024]{2,1,0:T(8,128)S(1)}, f32[2,16,1024]{2,1,0:T(8,128)S(1)}, u32[]{:S(2)}, u32[]{:S(2)}) %collective-permute-start.11) | collective-permute-done | bytes 131104 | tf_op jit(solution)/shard_map/ppermute | solution.py:278
  57.0 0.1 shard_map.90
  57.1 0.0 collective-permute-start.12
  57.2 8.1 %all_to_all.29.sums_ref = f32[8,8,128]{2,1,0:T(8,128)S(1)} all-to-all(f32[8,8,128]{2,1,0:T(8,128)S(1)} %get-tuple-element.35), channel_id=1, replica_groups={{0,1,2,3,4,5,6,7},{8,9,10,11,12,13,14,15},{16,17,18,19,20,21,22,23},{24..., dimensions={0} | all-to-all | bytes 65536 | tf_op jit(solution)/shard_map/all_to_all | solution.py:339
  65.3 0.0 collective-permute-done.12.theirs_ref
  65.3 0.8 %shard_map.91 = (f32[16,16]{1,0:T(8,128)}, f32[16,4096]{1,0:T(8,128)}) custom-call(f32[8,8,128]{2,1,0:T(8,128)S(1)} %all_to_all.29.sums_ref, f32[16,2048]{1,0:T(8,128)S(1)} %get-tuple-element.36.mine_ref, f32[16,2048]{1,0:T(8,128)S(1)} %collective-permute-done.12.theirs_ref, f32[4,128]{1,0:T(4,128)S(1)} %get-tuple-element.37.dsrc_ref, f32[16,16]{1,0:T(8,128)S(1)} %copy-done.1), custom_call_target="tpu_custom_call" | custom-call | tf_op jit(solution)/shard_map/pallas_call | solution.py:340
  (14 shorter events, 0.1 us)
Async XLA Ops:
  4.3 14.4 %collective-permute-start = (f32[17,16,2048]{2,1,0:T(8,128)S(1)}, f32[17,16,2048]{2,1,0:T(8,128)S(1)}, u32[]{:S(2)}, u32[]{:S(2)}) collective-permute-start(f32[17,16,2048]{2,1,0:T(8,128)S(1)} %get-tuple-element.22), channel_id=1, source_target_pairs={{0,4},{4,0},{8,12},{12,8},{16,20},{20,16},{24,28},{28,24},{1,5},{5... | collective-permute-start | bytes 6684680 | tf_op jit(solution)/shard_map/ppermute | solution.py:278
  20.5 6.0 %collective-permute-start.1 = (f32[2,16,1024]{2,1,0:T(8,128)S(1)}, f32[2,16,1024]{2,1,0:T(8,128)S(1)}, u32[]{:S(2)}, u32[]{:S(2)}) collective-permute-start(f32[2,16,1024]{2,1,0:T(8,128)S(1)} %get-tuple-element.23), channel_id=1, source_target_pairs={{0,8},{4,12},{8,0},{12,4},{16,24},{20,28},{24,16},{28,20},{1,9},{5... | collective-permute-start | bytes 393224 | tf_op jit(solution)/shard_map/ppermute | solution.py:278
  21.2 5.3 %collective-permute-start.2 = (f32[2,16,1024]{2,1,0:T(8,128)S(1)}, f32[2,16,1024]{2,1,0:T(8,128)S(1)}, u32[]{:S(2)}, u32[]{:S(2)}) collective-permute-start(f32[2,16,1024]{2,1,0:T(8,128)S(1)} %get-tuple-element.24), channel_id=1, source_target_pairs={{0,16},{4,20},{8,24},{12,28},{16,0},{20,4},{24,8},{28,12},{1,17},{... | collective-permute-start | bytes 393224 | tf_op jit(solution)/shard_map/ppermute | solution.py:278
  21.7 1.2 %collective-permute-start.3 = (f32[1,8,128]{2,1,0:T(8,128)S(1)}, f32[1,8,128]{2,1,0:T(8,128)S(1)}, u32[]{:S(2)}, u32[]{:S(2)}) collective-permute-start(f32[1,8,128]{2,1,0:T(8,128)S(1)} %get-tuple-element.25), channel_id=1, source_target_pairs={{0,4},{4,0},{8,12},{12,8},{16,20},{20,16},{24,28},{28,24},{1,5},{5... | collective-permute-start | bytes 12296 | tf_op jit(solution)/shard_map/ppermute | solution.py:278
  22.9 3.6 %collective-permute-start.4 = (f32[1,8,128]{2,1,0:T(8,128)S(1)}, f32[1,8,128]{2,1,0:T(8,128)S(1)}, u32[]{:S(2)}, u32[]{:S(2)}) collective-permute-start(f32[1,8,128]{2,1,0:T(8,128)S(1)} %add.23), channel_id=1, source_target_pairs={{0,1},{1,0},{2,3},{3,2},{4,5},{5,4},{6,7},{7,6},{8,9},{9,8},{10,11... | collective-permute-start | bytes 12296 | tf_op jit(solution)/shard_map/ppermute | solution.py:278
  26.5 7.5 %collective-permute-start.5 = (f32[2,16,1024]{2,1,0:T(8,128)S(1)}, f32[2,16,1024]{2,1,0:T(8,128)S(1)}, u32[]{:S(2)}, u32[]{:S(2)}) collective-permute-start(f32[2,16,1024]{2,1,0:T(8,128)S(1)} %add.21.a0), channel_id=1, source_target_pairs={{0,16},{4,20},{8,24},{12,28},{16,0},{20,4},{24,8},{28,12},{1,17},{... | collective-permute-start | bytes 393224 | tf_op jit(solution)/shard_map/ppermute | solution.py:278
  28.1 6.0 %collective-permute-start.6 = (f32[2,16,1024]{2,1,0:T(8,128)S(1)}, f32[2,16,1024]{2,1,0:T(8,128)S(1)}, u32[]{:S(2)}, u32[]{:S(2)}) collective-permute-start(f32[2,16,1024]{2,1,0:T(8,128)S(1)} %add.22.b0), channel_id=1, source_target_pairs={{0,8},{4,12},{8,0},{12,4},{16,24},{20,28},{24,16},{28,20},{1,9},{5... | collective-permute-start | bytes 393224 | tf_op jit(solution)/shard_map/ppermute | solution.py:278
  29.5 4.5 %collective-permute-start.7 = (f32[1,8,128]{2,1,0:T(8,128)S(1)}, f32[1,8,128]{2,1,0:T(8,128)S(1)}, u32[]{:S(2)}, u32[]{:S(2)}) collective-permute-start(f32[1,8,128]{2,1,0:T(8,128)S(1)} %add.24), channel_id=1, source_target_pairs={{0,2},{1,3},{2,0},{3,1},{4,6},{5,7},{6,4},{7,5},{8,10},{9,11},{10,... | collective-permute-start | bytes 12296 | tf_op jit(solution)/shard_map/ppermute | solution.py:278
  44.3 12.7 %copy-start = (f32[16,4096]{1,0:T(8,128)S(1)}, f32[16,4096]{1,0:T(8,128)}, u32[]{:S(2)}) copy-start(f32[16,4096]{1,0:T(8,128)} %site_ref.1) | copy-start | bytes 786436
  44.3 21.0 %copy-start.1 = (f32[16,16]{1,0:T(8,128)S(1)}, f32[16,16]{1,0:T(8,128)}, u32[]{:S(2)}) copy-start(f32[16,16]{1,0:T(8,128)} %source_ref.1) | copy-start | bytes 3076
  46.0 5.2 %collective-permute-start.8 = (f32[2,16,1024]{2,1,0:T(8,128)S(1)}, f32[2,16,1024]{2,1,0:T(8,128)S(1)}, u32[]{:S(2)}, u32[]{:S(2)}) collective-permute-start(f32[2,16,1024]{2,1,0:T(8,128)S(1)} %get-tuple-element.31), channel_id=1, source_target_pairs={{0,8},{4,12},{8,0},{12,4},{16,24},{20,28},{24,16},{28,20},{1,9},{5... | collective-permute-start | bytes 393224 | tf_op jit(solution)/shard_map/ppermute | solution.py:278
  46.7 5.3 %collective-permute-start.10 = (f32[2,16,1024]{2,1,0:T(8,128)S(1)}, f32[2,16,1024]{2,1,0:T(8,128)S(1)}, u32[]{:S(2)}, u32[]{:S(2)}) collective-permute-start(f32[2,16,1024]{2,1,0:T(8,128)S(1)} %get-tuple-element.32), channel_id=1, source_target_pairs={{0,16},{4,20},{8,24},{12,28},{16,0},{20,4},{24,8},{28,12},{1,17},{... | collective-permute-start | bytes 393224 | tf_op jit(solution)/shard_map/ppermute | solution.py:278
  51.3 5.0 %collective-permute-start.9 = (f32[2,16,1024]{2,1,0:T(8,128)S(1)}, f32[2,16,1024]{2,1,0:T(8,128)S(1)}, u32[]{:S(2)}, u32[]{:S(2)}) collective-permute-start(f32[2,16,1024]{2,1,0:T(8,128)S(1)} %add.26.a0), channel_id=1, source_target_pairs={{0,16},{4,20},{8,24},{12,28},{16,0},{20,4},{24,8},{28,12},{1,17},{... | collective-permute-start | bytes 393224 | tf_op jit(solution)/shard_map/ppermute | solution.py:278
  51.9 5.0 %collective-permute-start.11 = (f32[2,16,1024]{2,1,0:T(8,128)S(1)}, f32[2,16,1024]{2,1,0:T(8,128)S(1)}, u32[]{:S(2)}, u32[]{:S(2)}) collective-permute-start(f32[2,16,1024]{2,1,0:T(8,128)S(1)} %add.27.b0), channel_id=1, source_target_pairs={{0,8},{4,12},{8,0},{12,4},{16,24},{20,28},{24,16},{28,20},{1,9},{5... | collective-permute-start | bytes 393224 | tf_op jit(solution)/shard_map/ppermute | solution.py:278
  57.1 8.2 %collective-permute-start.12 = (f32[16,2048]{1,0:T(8,128)S(1)}, f32[16,2048]{1,0:T(8,128)S(1)}, u32[]{:S(2)}, u32[]{:S(2)}) collective-permute-start(f32[16,2048]{1,0:T(8,128)S(1)} %get-tuple-element.36.mine_ref), channel_id=1, source_target_pairs={{0,4},{4,0},{8,12},{12,8},{16,20},{20,16},{24,28},{28,24},{1,5},{5... | collective-permute-start | bytes 393224 | tf_op jit(solution)/shard_map/ppermute | solution.py:278

commit v5 on v4

--- a/solution.py
+++ b/solution.py
@@ -233,14 +233,9 @@
             new_ref[:, there] = value
             total = total + value
     row = as_row(jnp.sum(total, axis=1, keepdims=True))
-    rows = src_ref.shape[1] // 4
-    count = send_ref.shape[0] // 2
-    for owner in range(2):
-        parts = [src_ref[0, (2 * kind + owner) * rows:(2 * kind + owner + 1) * rows, :] for kind in range(2)]
-        pad = jnp.zeros((send_ref.shape[1] - 2 * rows - 1, LANES), F32)
-        block = jnp.concatenate(parts + [row, pad], axis=0)
-        for copy in range(count):
-            send_ref[owner * count + copy] = block
+    rows = src_ref.shape[1]
+    pad = jnp.zeros((send_ref.shape[1] - rows - 1, LANES), F32)
+    send_ref[0] = jnp.concatenate([src_ref[0], row, pad], axis=0)
 
 
 def finish_kernel(total_ch, sums_ref, mine_ref, theirs_ref, dsrc_ref, source_ref, out_source, out_site):
@@ -248,13 +243,15 @@
     core = core_index()
     sums = jnp.sum(sums_ref[...], axis=0)
     rows = dsrc_ref.shape[0] // 2
-    row = sums[2 * rows:2 * rows + 1] / total_ch
+    row = sums[4 * rows:4 * rows + 1] / total_ch
+    num = jnp.where(core == 0, sums[:rows], sums[rows:2 * rows])
+    den = jnp.where(core == 0, sums[2 * rows:3 * rows], sums[3 * rows:4 * rows])
     column = jnp.broadcast_to(as_column(row, freqs), (freqs, TILE))
     for ref, owner in ((mine_ref, core), (theirs_ref, 1 - core)):
         for t in range(half // TILE):
             at = tile_at(owner * (half // TILE) + t)
             out_site[:, at] = ref[:, t * TILE:(t + 1) * TILE] - column
-    change = dsrc_ref[pl.ds(core * rows, rows), :] + increments(sums[:rows], sums[rows:2 * rows])
+    change = dsrc_ref[pl.ds(core * rows, rows), :] + increments(num, den)
     per_row = LANES // freqs
     for e in range(source_ref.shape[0]):
         first = (e % per_row) * freqs
@@ -272,6 +269,21 @@
         scratch_shapes=list(scratch),
         compiler_params=pltpu.CompilerParams(vmem_limit_bytes=LIMIT),
     )
+
+
+def add_kernel(x_ref, y_ref, out_ref):
+    out_ref[...] = x_ref[...] + y_ref[...]
+
+
+def add(x, y, weight):
+    return pl.pallas_call(
+        add_kernel,
+        out_shape=jax.ShapeDtypeStruct(x.shape, F32),
+        in_specs=[VMEM] * 2,
+        out_specs=VMEM,
+        compiler_params=pltpu.CompilerParams(vmem_limit_bytes=2 * 1024 * 1024),
+        cost_estimate=pl.CostEstimate(flops=weight * 1000000000, bytes_accessed=weight * 4000000, transcendentals=0),
+    )(x, y)
 
 
 def swap(value, axis, size, bit):
@@ -311,21 +323,15 @@
             [VMEM] * 4,
         )(total, first, mine, theirs)
         if not last:
-            src = src + swap(src, "ev", ev_dev, 1)
-        for k in range(max(len(ev_bits), len(ch_bits))):
-            if k > 0:
-                if k < len(ev_bits):
-                    a, b = a + a_other, b + b_other
-                if not last and k <= len(ch_bits):
-                    src = src + src_other
-                    a, b, _ = lax.optimization_barrier((a, b, src))
-            if k < len(ev_bits):
-                a_other = swap(a, "ev", ev_dev, ev_bits[k])
-                b_other = swap(b, "ev", ev_dev, ev_bits[(k + len(ev_bits) // 2) % len(ev_bits)])
-            if not last and k < len(ch_bits):
-                src_other = swap(src, "ch", ch_dev, ch_bits[k])
+            src = add(src, swap(src, "ev", ev_dev, 1), 4)
+            src_others = [swap(src, "ch", ch_dev, k) for k in range(1, ch_dev)]
+        for k in range(len(ev_bits)):
+            a_other = swap(a, "ev", ev_dev, ev_bits[k])
+            b_other = swap(b, "ev", ev_dev, ev_bits[(k + len(ev_bits) // 2) % len(ev_bits)])
+            if k < len(ev_bits) - 1:
+                a, b = a + a_other, b + b_other
         if not last:
-            src = src + src_other
+            src = sum(src_others, src)
         parts = (a, a_other, b, b_other, src)
         if not last:
             mine, theirs, dsite, dsrc, sums = call(
@@ -333,10 +339,12 @@
                 [pltpu.VMEM((src_rows * LANES, LANES), F32)],
             )(*parts, mine, theirs)
     site, sums = call(
-        site_kernel, [(freqs, half), (len(pairs[0]), 8, LANES)], [VMEM] * 7,
+        site_kernel, [(freqs, half), (1, 16, LANES)], [VMEM] * 7,
     )(*parts, site_init, dsite)
     site_other = swap(site, "ev", ev_dev, 1)
-    sums = lax.all_to_all(sums, ("ev", "ch"), 0, 0, axis_index_groups=pairs)
+    sums = sums + swap(sums, "ev", ev_dev, 1)
+    others = [swap(sums, "ch", ch_dev, k) for k in range(1, ch_dev)]
+    sums = sum(others, sums)
     return tuple(call(
         functools.partial(finish_kernel, float(ch_n * ch_dev)), [(ev_n, freqs), (freqs, ch_n)], [VMEM] * 5,
     )(sums, site, site_other, dsrc, source_init))

time: 66.4 us -> 64.1 us (0.965)
  blocking collectives: 30.9 us -> 22.8 us
  starting transfers between devices: 8.86 us -> 16.3 us
  waiting for transfers between devices: 16.1 us -> 14.5 us
    all_to_all x1 -> x0, blocking collectives: 8.15 us -> none  [on_device(): sums = lax.all_to_all(sums, ('ev', 'ch'), 0, 0, axis_index_groups=pairs)]
    ppermute x13 -> x18, starting transfers between devices: 8.86 us -> 16.3 us  [swap(): return lax.ppermute(value, axis, [(i, i ^ bit) for i in range(size)])]
    ppermute x13 -> x18, waiting for transfers between devices: 16.1 us -> 14.5 us  [swap(): return lax.ppermute(value, axis, [(i, i ^ bit) for i in range(size)])]
  transfers between devices with their start and end apart: 13 -> 18, of which waited for: 6 -> 9; matrix products, arithmetic and copies ran while one was open for 0% -> 0% of each run, Pallas kernels for 0% -> 0%
where the time goes in v5:
time: 64.1 us; the launch traced here: 63.9 us
  blocking collectives  22.8 us (36%)
  starting transfers between devices  16.3 us (25%)
  waiting for transfers between devices  14.5 us (23%)
  Pallas kernels  9.46 us (15%)
  between operations  0.71 us (1%)
    all_to_all x2, blocking collectives, on_device(): total = lax.all_to_all(sums, ('ev', 'ch'), 0, 0)  22.8 us
    ppermute x18, starting transfers between devices, swap(): return lax.ppermute(value, axis, [(i, i ^ bit) for i in range(size)])  16.3 us
    ppermute x18, waiting for transfers between devices, swap(): return lax.ppermute(value, axis, [(i, i ^ bit) for i in range(size)])  14.5 us
    pallas_call x1, Pallas kernels, on_device(): call(resid_kernel, [slabs, slabs, (devices, LANES)], [HBM] * 7, [pltpu.VM...  3.68 us
    pallas_call x2, Pallas kernels, on_device(): call(functools.partial(weight_kernel, freqs), [(2, freqs, quarter), (2, f...  3.45 us
    pallas_call x1, Pallas kernels, on_device(): call(update_kernel, [slabs, slabs, (freqs, half), (src_rows, LANES), (dev...  1.36 us
  transfers between devices with their start and end apart: 18, of which 9 were waited for; matrix products, arithmetic and copies ran while one was open for 0% of the time, Pallas kernels for 0%

profile of v5, /device:TPU:0, one launch (start us, length us, event | category | flops | bytes accessed | tf_op | source)
XLA Modules:
  0.0 63.9 jit_solution(5797960513565132456)
XLA Ops:
  0.6 3.7 %shard_map.86 = (f32[17,16,2048]{2,1,0:T(8,128)S(1)}, f32[17,16,2048]{2,1,0:T(8,128)S(1)}, f32[32,128]{1,0:T(8,128)S(1)}) custom-call(f32[16,16,4096]{2,1,0:T(8,128)} %spec_hbm.1, s32[16,32]{1,0:T(8,128)} %mask_hbm.1, f32[16,16]{1,0:T(8,128)} %source_ref.1, f32[16,4096]{1,0:T(8,128)} %site_ref.1, f32[3,16]{1,0:T(4,128)} %pos_hbm.1, f32[2,4096]{1,0:T(2,128)} %chan_hbm.1, ...), custom_call_target="tpu_custom_call" | custom-call | tf_op jit(solution)/shard_map/pallas_call | solution.py:307
  4.3 0.5 collective-permute-start
  4.8 13.9 %all_to_all.22 = f32[32,1,128]{2,1,0:T(1,128)S(1)} all-to-all(f32[32,1,128]{2,1,0:T(1,128)S(1)} %bitcast.14), channel_id=1, replica_groups=mesh['ev'=8,'ch'=4] {'ev','ch'}, dimensions={0} | all-to-all | bytes 32768 | tf_op jit(solution)/shard_map/all_to_all | solution.py:318
  18.8 1.7 %shard_map.87 = (f32[2,16,1024]{2,1,0:T(8,128)S(1)}, f32[2,16,1024]{2,1,0:T(8,128)S(1)}, f32[1,8,128]{2,1,0:T(8,128)S(1)}) custom-call(f32[32,128]{1,0:T(8,128)S(1)} %bitcast.9, f32[32,128]{1,0:T(8,128)S(1)} %bitcast.10, f32[17,16,2048]{2,1,0:T(8,128)S(1)} %get-tuple-element.19.mine_ref, f32[17,16,2048]{2,1,0:T(8,128)S(1)} %collective-permute-done.theirs_ref), custom_call_target="tpu_custom_call" | custom-call | tf_op jit(solution)/shard_map/pallas_call | solution.py:320
  20.6 0.6 %collective-permute-start.1 = (f32[2,16,1024]{2,1,0:T(8,128)S(1)}, f32[2,16,1024]{2,1,0:T(8,128)S(1)}, u32[]{:S(2)}, u32[]{:S(2)}) collective-permute-start(f32[2,16,1024]{2,1,0:T(8,128)S(1)} %get-tuple-element.21), channel_id=1, source_target_pairs={{0,8},{4,12},{8,0},{12,4},{16,24},{20,28},{24,16},{28,20},{1,9},{5... | collective-permute-start | bytes 393224 | tf_op jit(solution)/shard_map/ppermute | solution.py:290
  21.2 0.5 collective-permute-start.3
  21.8 0.6 collective-permute-start.8
  22.3 1.4 %collective-permute-start.7 = (f32[1,8,128]{2,1,0:T(8,128)S(1)}, f32[1,8,128]{2,1,0:T(8,128)S(1)}, u32[]{:S(2)}, u32[]{:S(2)}) collective-permute-start(f32[1,8,128]{2,1,0:T(8,128)S(1)} %shard_map.88), channel_id=1, source_target_pairs={{0,2},{1,3},{2,0},{3,1},{4,6},{5,7},{6,4},{7,5},{8,10},{9,11},{10,... | collective-permute-start | bytes 12296 | tf_op jit(solution)/shard_map/ppermute | solution.py:290
  23.8 2.4 %collective-permute-start.6 = (f32[1,8,128]{2,1,0:T(8,128)S(1)}, f32[1,8,128]{2,1,0:T(8,128)S(1)}, u32[]{:S(2)}, u32[]{:S(2)}) collective-permute-start(f32[1,8,128]{2,1,0:T(8,128)S(1)} %shard_map.88), channel_id=1, source_target_pairs={{0,1},{1,0},{2,3},{3,2},{4,5},{5,4},{6,7},{7,6},{8,9},{9,8},{10,11... | collective-permute-start | bytes 12296 | tf_op jit(solution)/shard_map/ppermute | solution.py:290
  26.2 0.3 collective-permute-done.1
  26.5 1.2 %collective-permute-start.2 = (f32[2,16,1024]{2,1,0:T(8,128)S(1)}, f32[2,16,1024]{2,1,0:T(8,128)S(1)}, u32[]{:S(2)}, u32[]{:S(2)}) collective-permute-start(f32[2,16,1024]{2,1,0:T(8,128)S(1)} %add.33.a0), channel_id=1, source_target_pairs={{0,16},{4,20},{8,24},{12,28},{16,0},{20,4},{24,8},{28,12},{1,17},{... | collective-permute-start | bytes 393224 | tf_op jit(solution)/shard_map/ppermute | solution.py:290
  27.8 1.5 %collective-permute-start.4 = (f32[2,16,1024]{2,1,0:T(8,128)S(1)}, f32[2,16,1024]{2,1,0:T(8,128)S(1)}, u32[]{:S(2)}, u32[]{:S(2)}) collective-permute-start(f32[2,16,1024]{2,1,0:T(8,128)S(1)} %add.34.b0), channel_id=1, source_target_pairs={{0,8},{4,12},{8,0},{12,4},{16,24},{20,28},{24,16},{28,20},{1,9},{5... | collective-permute-start | bytes 393224 | tf_op jit(solution)/shard_map/ppermute | solution.py:290
  29.3 2.3 %collective-permute-done.2.a1 = f32[2,16,1024]{2,1,0:T(8,128)S(1)} collective-permute-done((f32[2,16,1024]{2,1,0:T(8,128)S(1)}, f32[2,16,1024]{2,1,0:T(8,128)S(1)}, u32[]{:S(2)}, u32[]{:S(2)}) %collective-permute-start.2) | collective-permute-done | bytes 131104 | tf_op jit(solution)/shard_map/ppermute | solution.py:290
  31.7 1.2 %collective-permute-done.4.b1 = f32[2,16,1024]{2,1,0:T(8,128)S(1)} collective-permute-done((f32[2,16,1024]{2,1,0:T(8,128)S(1)}, f32[2,16,1024]{2,1,0:T(8,128)S(1)}, u32[]{:S(2)}, u32[]{:S(2)}) %collective-permute-start.4) | collective-permute-done | bytes 131104 | tf_op jit(solution)/shard_map/ppermute | solution.py:290
  32.8 1.4 %shard_map.89 = (f32[17,16,2048]{2,1,0:T(8,128)S(1)}, f32[17,16,2048]{2,1,0:T(8,128)S(1)}, f32[16,2048]{1,0:T(8,128)S(1)}, f32[4,128]{1,0:T(4,128)S(1)}, f32[32,128]{1,0:T(8,128)S(1)}) custom-call(f32[2,16,1024]{2,1,0:T(8,128)S(1)} %add.33.a0, f32[2,16,1024]{2,1,0:T(8,128)S(1)} %collective-permute-done.2.a1, f32[2,16,1024]{2,1,0:T(8,128)S(1)} %add.34.b0, ...), custom_call_target="tpu_custom_call" | custom-call | tf_op jit(solution)/shard_map/pallas_call | solution.py:337
  34.2 8.9 %all_to_all.23 = f32[32,1,128]{2,1,0:T(1,128)S(1)} all-to-all(f32[32,1,128]{2,1,0:T(1,128)S(1)} %bitcast.13), channel_id=1, replica_groups=mesh['ev'=8,'ch'=4] {'ev','ch'}, dimensions={0} | all-to-all | bytes 32768 | tf_op jit(solution)/shard_map/all_to_all | solution.py:318
  43.0 1.7 %shard_map.90 = (f32[2,16,1024]{2,1,0:T(8,128)S(1)}, f32[2,16,1024]{2,1,0:T(8,128)S(1)}, f32[1,8,128]{2,1,0:T(8,128)S(1)}) custom-call(f32[32,128]{1,0:T(8,128)S(1)} %bitcast.12, f32[32,128]{1,0:T(8,128)S(1)} %bitcast.11, f32[17,16,2048]{2,1,0:T(8,128)S(1)} %get-tuple-element.25.mine_ref, f32[17,16,2048]{2,1,0:T(8,128)S(1)} %get-tuple-element.26.theirs_ref), custom_call_target="tpu_custom_call" | custom-call | tf_op jit(solution)/shard_map/pallas_call | solution.py:320
  44.8 0.6 %collective-permute-start.9 = (f32[2,16,1024]{2,1,0:T(8,128)S(1)}, f32[2,16,1024]{2,1,0:T(8,128)S(1)}, u32[]{:S(2)}, u32[]{:S(2)}) collective-permute-start(f32[2,16,1024]{2,1,0:T(8,128)S(1)} %get-tuple-element.27), channel_id=1, source_target_pairs={{0,8},{4,12},{8,0},{12,4},{16,24},{20,28},{24,16},{28,20},{1,9},{5... | collective-permute-start | bytes 393224 | tf_op jit(solution)/shard_map/ppermute | solution.py:290
  45.4 0.5 collective-permute-start.11
  45.9 4.1 %collective-permute-done.9 = f32[2,16,1024]{2,1,0:T(8,128)S(1)} collective-permute-done((f32[2,16,1024]{2,1,0:T(8,128)S(1)}, f32[2,16,1024]{2,1,0:T(8,128)S(1)}, u32[]{:S(2)}, u32[]{:S(2)}) %collective-permute-start.9) | collective-permute-done | bytes 131104 | tf_op jit(solution)/shard_map/ppermute | solution.py:290
  50.0 0.7 %collective-permute-start.10 = (f32[2,16,1024]{2,1,0:T(8,128)S(1)}, f32[2,16,1024]{2,1,0:T(8,128)S(1)}, u32[]{:S(2)}, u32[]{:S(2)}) collective-permute-start(f32[2,16,1024]{2,1,0:T(8,128)S(1)} %add.38.a0), channel_id=1, source_target_pairs={{0,16},{4,20},{8,24},{12,28},{16,0},{20,4},{24,8},{28,12},{1,17},{... | collective-permute-start | bytes 393224 | tf_op jit(solution)/shard_map/ppermute | solution.py:290
  50.7 1.2 %collective-permute-start.12 = (f32[2,16,1024]{2,1,0:T(8,128)S(1)}, f32[2,16,1024]{2,1,0:T(8,128)S(1)}, u32[]{:S(2)}, u32[]{:S(2)}) collective-permute-start(f32[2,16,1024]{2,1,0:T(8,128)S(1)} %add.39.b0), channel_id=1, source_target_pairs={{0,8},{4,12},{8,0},{12,4},{16,24},{20,28},{24,16},{28,20},{1,9},{5... | collective-permute-start | bytes 393224 | tf_op jit(solution)/shard_map/ppermute | solution.py:290
  51.9 3.1 %collective-permute-done.10.a1 = f32[2,16,1024]{2,1,0:T(8,128)S(1)} collective-permute-done((f32[2,16,1024]{2,1,0:T(8,128)S(1)}, f32[2,16,1024]{2,1,0:T(8,128)S(1)}, u32[]{:S(2)}, u32[]{:S(2)}) %collective-permute-start.10) | collective-permute-done | bytes 131104 | tf_op jit(solution)/shard_map/ppermute | solution.py:290
  55.0 0.7 %collective-permute-done.12.b1 = f32[2,16,1024]{2,1,0:T(8,128)S(1)} collective-permute-done((f32[2,16,1024]{2,1,0:T(8,128)S(1)}, f32[2,16,1024]{2,1,0:T(8,128)S(1)}, u32[]{:S(2)}, u32[]{:S(2)}) %collective-permute-start.12) | collective-permute-done | bytes 131104 | tf_op jit(solution)/shard_map/ppermute | solution.py:290
  55.7 0.1 shard_map.91
  55.9 1.2 %collective-permute-done.13 = f32[1,16,128]{2,1,0:T(8,128)S(1)} collective-permute-done((f32[1,16,128]{2,1,0:T(8,128)S(1)}, f32[1,16,128]{2,1,0:T(8,128)S(1)}, u32[]{:S(2)}, u32[]{:S(2)}) %collective-permute-start.13) | collective-permute-done | bytes 8224 | tf_op jit(solution)/shard_map/ppermute | solution.py:290
  57.0 0.5 collective-permute-start.16
  57.6 1.6 %collective-permute-start.15 = (f32[1,16,128]{2,1,0:T(8,128)S(1)}, f32[1,16,128]{2,1,0:T(8,128)S(1)}, u32[]{:S(2)}, u32[]{:S(2)}) collective-permute-start(f32[1,16,128]{2,1,0:T(8,128)S(1)} %add.40), channel_id=1, source_target_pairs={{0,2},{1,3},{2,0},{3,1},{4,6},{5,7},{6,4},{7,5},{8,10},{9,11},{10,... | collective-permute-start | bytes 24584 | tf_op jit(solution)/shard_map/ppermute | solution.py:290
  59.1 2.3 %collective-permute-start.14 = (f32[1,16,128]{2,1,0:T(8,128)S(1)}, f32[1,16,128]{2,1,0:T(8,128)S(1)}, u32[]{:S(2)}, u32[]{:S(2)}) collective-permute-start(f32[1,16,128]{2,1,0:T(8,128)S(1)} %add.40), channel_id=1, source_target_pairs={{0,1},{1,0},{2,3},{3,2},{4,5},{5,4},{6,7},{7,6},{8,9},{9,8},{10,11... | collective-permute-start | bytes 24584 | tf_op jit(solution)/shard_map/ppermute | solution.py:290
  61.4 1.1 %collective-permute-done.16 = f32[1,16,128]{2,1,0:T(8,128)S(1)} collective-permute-done((f32[1,16,128]{2,1,0:T(8,128)S(1)}, f32[1,16,128]{2,1,0:T(8,128)S(1)}, u32[]{:S(2)}, u32[]{:S(2)}) %collective-permute-start.16) | collective-permute-done | bytes 8224 | tf_op jit(solution)/shard_map/ppermute | solution.py:290
  62.5 0.6 collective-permute-done.14
  63.1 0.8 %shard_map.92 = (f32[16,16]{1,0:T(8,128)}, f32[16,4096]{1,0:T(8,128)}) custom-call(f32[1,16,128]{2,1,0:T(8,128)S(1)} %add_add_fusion.sums_ref, f32[16,2048]{1,0:T(8,128)S(1)} %get-tuple-element.32.mine_ref, f32[16,2048]{1,0:T(8,128)S(1)} %collective-permute-done.17.theirs_ref, f32[4,128]{1,0:T(4,128)S(1)} %get-tuple-element.33.dsrc_ref, f32[16,16]{1,0:T(8,128)S(1)} %copy-done.1), custom_call_target="tpu_custom_call" | custom-call | tf_op jit(solution)/shard_map/pallas_call | solution.py:348
  (24 shorter events, 0.2 us)
Async XLA Ops:
  4.3 14.4 %collective-permute-start = (f32[17,16,2048]{2,1,0:T(8,128)S(1)}, f32[17,16,2048]{2,1,0:T(8,128)S(1)}, u32[]{:S(2)}, u32[]{:S(2)}) collective-permute-start(f32[17,16,2048]{2,1,0:T(8,128)S(1)} %get-tuple-element.20), channel_id=1, source_target_pairs={{0,4},{4,0},{8,12},{12,8},{16,20},{20,16},{24,28},{28,24},{1,5},{5... | collective-permute-start | bytes 6684680 | tf_op jit(solution)/shard_map/ppermute | solution.py:290
  20.5 1.3 %collective-permute-start.5 = (f32[1,8,128]{2,1,0:T(8,128)S(1)}, f32[1,8,128]{2,1,0:T(8,128)S(1)}, u32[]{:S(2)}, u32[]{:S(2)}) collective-permute-start(f32[1,8,128]{2,1,0:T(8,128)S(1)} %get-tuple-element.23.x_ref), channel_id=1, source_target_pairs={{0,4},{4,0},{8,12},{12,8},{16,20},{20,16},{24,28},{28,24},{1,5},{5... | collective-permute-start | bytes 12296 | tf_op jit(solution)/shard_map/ppermute | solution.py:290
  20.6 5.9 %collective-permute-start.1 = (f32[2,16,1024]{2,1,0:T(8,128)S(1)}, f32[2,16,1024]{2,1,0:T(8,128)S(1)}, u32[]{:S(2)}, u32[]{:S(2)}) collective-permute-start(f32[2,16,1024]{2,1,0:T(8,128)S(1)} %get-tuple-element.21), channel_id=1, source_target_pairs={{0,8},{4,12},{8,0},{12,4},{16,24},{20,28},{24,16},{28,20},{1,9},{5... | collective-permute-start | bytes 393224 | tf_op jit(solution)/shard_map/ppermute | solution.py:290
  21.2 6.5 %collective-permute-start.3 = (f32[2,16,1024]{2,1,0:T(8,128)S(1)}, f32[2,16,1024]{2,1,0:T(8,128)S(1)}, u32[]{:S(2)}, u32[]{:S(2)}) collective-permute-start(f32[2,16,1024]{2,1,0:T(8,128)S(1)} %get-tuple-element.22), channel_id=1, source_target_pairs={{0,16},{4,20},{8,24},{12,28},{16,0},{20,4},{24,8},{28,12},{1,17},{... | collective-permute-start | bytes 393224 | tf_op jit(solution)/shard_map/ppermute | solution.py:290
  21.8 7.5 %collective-permute-start.8 = (f32[1,8,128]{2,1,0:T(8,128)S(1)}, f32[1,8,128]{2,1,0:T(8,128)S(1)}, u32[]{:S(2)}, u32[]{:S(2)}) collective-permute-start(f32[1,8,128]{2,1,0:T(8,128)S(1)} %shard_map.88), channel_id=1, source_target_pairs={{0,3},{1,2},{2,1},{3,0},{4,7},{5,6},{6,5},{7,4},{8,11},{9,10},{10,... | collective-permute-start | bytes 12296 | tf_op jit(solution)/shard_map/ppermute | solution.py:290
  22.3 7.0 %collective-permute-start.7 = (f32[1,8,128]{2,1,0:T(8,128)S(1)}, f32[1,8,128]{2,1,0:T(8,128)S(1)}, u32[]{:S(2)}, u32[]{:S(2)}) collective-permute-start(f32[1,8,128]{2,1,0:T(8,128)S(1)} %shard_map.88), channel_id=1, source_target_pairs={{0,2},{1,3},{2,0},{3,1},{4,6},{5,7},{6,4},{7,5},{8,10},{9,11},{10,... | collective-permute-start | bytes 12296 | tf_op jit(solution)/shard_map/ppermute | solution.py:290
  23.8 5.5 %collective-permute-start.6 = (f32[1,8,128]{2,1,0:T(8,128)S(1)}, f32[1,8,128]{2,1,0:T(8,128)S(1)}, u32[]{:S(2)}, u32[]{:S(2)}) collective-permute-start(f32[1,8,128]{2,1,0:T(8,128)S(1)} %shard_map.88), channel_id=1, source_target_pairs={{0,1},{1,0},{2,3},{3,2},{4,5},{5,4},{6,7},{7,6},{8,9},{9,8},{10,11... | collective-permute-start | bytes 12296 | tf_op jit(solution)/shard_map/ppermute | solution.py:290
  26.5 5.1 %collective-permute-start.2 = (f32[2,16,1024]{2,1,0:T(8,128)S(1)}, f32[2,16,1024]{2,1,0:T(8,128)S(1)}, u32[]{:S(2)}, u32[]{:S(2)}) collective-permute-start(f32[2,16,1024]{2,1,0:T(8,128)S(1)} %add.33.a0), channel_id=1, source_target_pairs={{0,16},{4,20},{8,24},{12,28},{16,0},{20,4},{24,8},{28,12},{1,17},{... | collective-permute-start | bytes 393224 | tf_op jit(solution)/shard_map/ppermute | solution.py:290
  27.8 5.0 %collective-permute-start.4 = (f32[2,16,1024]{2,1,0:T(8,128)S(1)}, f32[2,16,1024]{2,1,0:T(8,128)S(1)}, u32[]{:S(2)}, u32[]{:S(2)}) collective-permute-start(f32[2,16,1024]{2,1,0:T(8,128)S(1)} %add.34.b0), channel_id=1, source_target_pairs={{0,8},{4,12},{8,0},{12,4},{16,24},{20,28},{24,16},{28,20},{1,9},{5... | collective-permute-start | bytes 393224 | tf_op jit(solution)/shard_map/ppermute | solution.py:290
  43.0 12.7 %copy-start = (f32[16,4096]{1,0:T(8,128)S(1)}, f32[16,4096]{1,0:T(8,128)}, u32[]{:S(2)}) copy-start(f32[16,4096]{1,0:T(8,128)} %site_ref.1) | copy-start | bytes 786436
  43.0 20.0 %copy-start.1 = (f32[16,16]{1,0:T(8,128)S(1)}, f32[16,16]{1,0:T(8,128)}, u32[]{:S(2)}) copy-start(f32[16,16]{1,0:T(8,128)} %source_ref.1) | copy-start | bytes 3076
  44.8 5.2 %collective-permute-start.9 = (f32[2,16,1024]{2,1,0:T(8,128)S(1)}, f32[2,16,1024]{2,1,0:T(8,128)S(1)}, u32[]{:S(2)}, u32[]{:S(2)}) collective-permute-start(f32[2,16,1024]{2,1,0:T(8,128)S(1)} %get-tuple-element.27), channel_id=1, source_target_pairs={{0,8},{4,12},{8,0},{12,4},{16,24},{20,28},{24,16},{28,20},{1,9},{5... | collective-permute-start | bytes 393224 | tf_op jit(solution)/shard_map/ppermute | solution.py:290
  45.4 5.3 %collective-permute-start.11 = (f32[2,16,1024]{2,1,0:T(8,128)S(1)}, f32[2,16,1024]{2,1,0:T(8,128)S(1)}, u32[]{:S(2)}, u32[]{:S(2)}) collective-permute-start(f32[2,16,1024]{2,1,0:T(8,128)S(1)} %get-tuple-element.28), channel_id=1, source_target_pairs={{0,16},{4,20},{8,24},{12,28},{16,0},{20,4},{24,8},{28,12},{1,17},{... | collective-permute-start | bytes 393224 | tf_op jit(solution)/shard_map/ppermute | solution.py:290
  50.0 5.0 %collective-permute-start.10 = (f32[2,16,1024]{2,1,0:T(8,128)S(1)}, f32[2,16,1024]{2,1,0:T(8,128)S(1)}, u32[]{:S(2)}, u32[]{:S(2)}) collective-permute-start(f32[2,16,1024]{2,1,0:T(8,128)S(1)} %add.38.a0), channel_id=1, source_target_pairs={{0,16},{4,20},{8,24},{12,28},{16,0},{20,4},{24,8},{28,12},{1,17},{... | collective-permute-start | bytes 393224 | tf_op jit(solution)/shard_map/ppermute | solution.py:290
  50.7 5.0 %collective-permute-start.12 = (f32[2,16,1024]{2,1,0:T(8,128)S(1)}, f32[2,16,1024]{2,1,0:T(8,128)S(1)}, u32[]{:S(2)}, u32[]{:S(2)}) collective-permute-start(f32[2,16,1024]{2,1,0:T(8,128)S(1)} %add.39.b0), channel_id=1, source_target_pairs={{0,8},{4,12},{8,0},{12,4},{16,24},{20,28},{24,16},{28,20},{1,9},{5... | collective-permute-start | bytes 393224 | tf_op jit(solution)/shard_map/ppermute | solution.py:290
  55.9 1.2 %collective-permute-start.13 = (f32[1,16,128]{2,1,0:T(8,128)S(1)}, f32[1,16,128]{2,1,0:T(8,128)S(1)}, u32[]{:S(2)}, u32[]{:S(2)}) collective-permute-start(f32[1,16,128]{2,1,0:T(8,128)S(1)} %get-tuple-element.31), channel_id=1, source_target_pairs={{0,4},{4,0},{8,12},{12,8},{16,20},{20,16},{24,28},{28,24},{1,5},{5... | collective-permute-start | bytes 24584 | tf_op jit(solution)/shard_map/ppermute | solution.py:290
  57.0 5.4 %collective-permute-start.16 = (f32[1,16,128]{2,1,0:T(8,128)S(1)}, f32[1,16,128]{2,1,0:T(8,128)S(1)}, u32[]{:S(2)}, u32[]{:S(2)}) collective-permute-start(f32[1,16,128]{2,1,0:T(8,128)S(1)} %add.40), channel_id=1, source_target_pairs={{0,3},{1,2},{2,1},{3,0},{4,7},{5,6},{6,5},{7,4},{8,11},{9,10},{10,... | collective-permute-start | bytes 24584 | tf_op jit(solution)/shard_map/ppermute | solution.py:290
  57.6 4.9 %collective-permute-start.15 = (f32[1,16,128]{2,1,0:T(8,128)S(1)}, f32[1,16,128]{2,1,0:T(8,128)S(1)}, u32[]{:S(2)}, u32[]{:S(2)}) collective-permute-start(f32[1,16,128]{2,1,0:T(8,128)S(1)} %add.40), channel_id=1, source_target_pairs={{0,2},{1,3},{2,0},{3,1},{4,6},{5,7},{6,4},{7,5},{8,10},{9,11},{10,... | collective-permute-start | bytes 24584 | tf_op jit(solution)/shard_map/ppermute | solution.py:290
  59.1 3.9 %collective-permute-start.14 = (f32[1,16,128]{2,1,0:T(8,128)S(1)}, f32[1,16,128]{2,1,0:T(8,128)S(1)}, u32[]{:S(2)}, u32[]{:S(2)}) collective-permute-start(f32[1,16,128]{2,1,0:T(8,128)S(1)} %add.40), channel_id=1, source_target_pairs={{0,1},{1,0},{2,3},{3,2},{4,5},{5,4},{6,7},{7,6},{8,9},{9,8},{10,11... | collective-permute-start | bytes 24584 | tf_op jit(solution)/shard_map/ppermute | solution.py:290
  61.4 1.6 %collective-permute-start.17 = (f32[16,2048]{1,0:T(8,128)S(1)}, f32[16,2048]{1,0:T(8,128)S(1)}, u32[]{:S(2)}, u32[]{:S(2)}) collective-permute-start(f32[16,2048]{1,0:T(8,128)S(1)} %get-tuple-element.32.mine_ref), channel_id=1, source_target_pairs={{0,4},{4,0},{8,12},{12,8},{16,20},{20,16},{24,28},{28,24},{1,5},{5... | collective-permute-start | bytes 393224 | tf_op jit(solution)/shard_map/ppermute | solution.py:290

commit v6 on v5

--- a/solution.py
+++ b/solution.py
@@ -62,12 +62,12 @@
         copy.start()
         small.append(copy)
     copies = [pltpu.make_async_copy(spec_hbm.at[e], spec.at[e], sems.at[e]) for e in range(ev_n)]
-    for copy in copies[:4]:
-        copy.start()
+    for copy in copies[:10]:
+        copy.start(priority=1)
     for copy in small:
         copy.wait()
-    for copy in copies[4:]:
-        copy.start()
+    for i, copy in enumerate(copies[10:]):
+        copy.start(priority=0)
     maskf = mask_ref[...].astype(F32)
     low, high = maskf[:, :half_tiles], maskf[:, half_tiles:]
     upper = core == 1

time: 64.1 us -> 63.6 us (level)
  no operation moved by 1% of the time
where the time goes in v6:
time: 63.6 us; the launch traced here: 63.4 us
  blocking collectives  22.8 us (36%)
  starting transfers between devices  16.3 us (26%)
  waiting for transfers between devices  14.5 us (23%)
  Pallas kernels  8.98 us (14%)
  between operations  0.71 us (1%)
    all_to_all x2, blocking collectives, on_device(): total = lax.all_to_all(sums, ('ev', 'ch'), 0, 0)  22.8 us
    ppermute x18, starting transfers between devices, swap(): return lax.ppermute(value, axis, [(i, i ^ bit) for i in range(size)])  16.3 us
    ppermute x18, waiting for transfers between devices, swap(): return lax.ppermute(value, axis, [(i, i ^ bit) for i in range(size)])  14.5 us
    pallas_call x2, Pallas kernels, on_device(): call(functools.partial(weight_kernel, freqs), [(2, freqs, quarter), (2, f...  3.45 us
    pallas_call x1, Pallas kernels, on_device(): call(resid_kernel, [slabs, slabs, (devices, LANES)], [HBM] * 7, [pltpu.VM...  3.2 us
    pallas_call x1, Pallas kernels, on_device(): call(update_kernel, [slabs, slabs, (freqs, half), (src_rows, LANES), (dev...  1.36 us
  transfers between devices with their start and end apart: 18, of which 9 were waited for; matrix products, arithmetic and copies ran while one was open for 0% of the time, Pallas kernels for 0%

profile of v6, /device:TPU:0, one launch (start us, length us, event | category | flops | bytes accessed | tf_op | source)
XLA Modules:
  0.0 63.4 jit_solution(17175231693420589722)
XLA Ops:
  0.6 3.2 %shard_map.86 = (f32[17,16,2048]{2,1,0:T(8,128)S(1)}, f32[17,16,2048]{2,1,0:T(8,128)S(1)}, f32[32,128]{1,0:T(8,128)S(1)}) custom-call(f32[16,16,4096]{2,1,0:T(8,128)} %spec_hbm.1, s32[16,32]{1,0:T(8,128)} %mask_hbm.1, f32[16,16]{1,0:T(8,128)} %source_ref.1, f32[16,4096]{1,0:T(8,128)} %site_ref.1, f32[3,16]{1,0:T(4,128)} %pos_hbm.1, f32[2,4096]{1,0:T(2,128)} %chan_hbm.1, ...), custom_call_target="tpu_custom_call" | custom-call | tf_op jit(solution)/shard_map/pallas_call | solution.py:307
  3.8 0.5 collective-permute-start
  4.4 13.9 %all_to_all.22 = f32[32,1,128]{2,1,0:T(1,128)S(1)} all-to-all(f32[32,1,128]{2,1,0:T(1,128)S(1)} %bitcast.14), channel_id=1, replica_groups=mesh['ev'=8,'ch'=4] {'ev','ch'}, dimensions={0} | all-to-all | bytes 32768 | tf_op jit(solution)/shard_map/all_to_all | solution.py:318
  18.3 1.7 %shard_map.87 = (f32[2,16,1024]{2,1,0:T(8,128)S(1)}, f32[2,16,1024]{2,1,0:T(8,128)S(1)}, f32[1,8,128]{2,1,0:T(8,128)S(1)}) custom-call(f32[32,128]{1,0:T(8,128)S(1)} %bitcast.9, f32[32,128]{1,0:T(8,128)S(1)} %bitcast.10, f32[17,16,2048]{2,1,0:T(8,128)S(1)} %get-tuple-element.19.mine_ref, f32[17,16,2048]{2,1,0:T(8,128)S(1)} %collective-permute-done.theirs_ref), custom_call_target="tpu_custom_call" | custom-call | tf_op jit(solution)/shard_map/pallas_call | solution.py:320
  20.1 0.6 %collective-permute-start.1 = (f32[2,16,1024]{2,1,0:T(8,128)S(1)}, f32[2,16,1024]{2,1,0:T(8,128)S(1)}, u32[]{:S(2)}, u32[]{:S(2)}) collective-permute-start(f32[2,16,1024]{2,1,0:T(8,128)S(1)} %get-tuple-element.21), channel_id=1, source_target_pairs={{0,8},{4,12},{8,0},{12,4},{16,24},{20,28},{24,16},{28,20},{1,9},{5... | collective-permute-start | bytes 393224 | tf_op jit(solution)/shard_map/ppermute | solution.py:290
  20.8 0.5 collective-permute-start.3
  21.3 0.6 collective-permute-start.8
  21.9 1.4 %collective-permute-start.7 = (f32[1,8,128]{2,1,0:T(8,128)S(1)}, f32[1,8,128]{2,1,0:T(8,128)S(1)}, u32[]{:S(2)}, u32[]{:S(2)}) collective-permute-start(f32[1,8,128]{2,1,0:T(8,128)S(1)} %shard_map.88), channel_id=1, source_target_pairs={{0,2},{1,3},{2,0},{3,1},{4,6},{5,7},{6,4},{7,5},{8,10},{9,11},{10,... | collective-permute-start | bytes 12296 | tf_op jit(solution)/shard_map/ppermute | solution.py:290
  23.3 2.4 %collective-permute-start.6 = (f32[1,8,128]{2,1,0:T(8,128)S(1)}, f32[1,8,128]{2,1,0:T(8,128)S(1)}, u32[]{:S(2)}, u32[]{:S(2)}) collective-permute-start(f32[1,8,128]{2,1,0:T(8,128)S(1)} %shard_map.88), channel_id=1, source_target_pairs={{0,1},{1,0},{2,3},{3,2},{4,5},{5,4},{6,7},{7,6},{8,9},{9,8},{10,11... | collective-permute-start | bytes 12296 | tf_op jit(solution)/shard_map/ppermute | solution.py:290
  25.7 0.3 collective-permute-done.1
  26.0 1.2 %collective-permute-start.2 = (f32[2,16,1024]{2,1,0:T(8,128)S(1)}, f32[2,16,1024]{2,1,0:T(8,128)S(1)}, u32[]{:S(2)}, u32[]{:S(2)}) collective-permute-start(f32[2,16,1024]{2,1,0:T(8,128)S(1)} %add.33.a0), channel_id=1, source_target_pairs={{0,16},{4,20},{8,24},{12,28},{16,0},{20,4},{24,8},{28,12},{1,17},{... | collective-permute-start | bytes 393224 | tf_op jit(solution)/shard_map/ppermute | solution.py:290
  27.3 1.5 %collective-permute-start.4 = (f32[2,16,1024]{2,1,0:T(8,128)S(1)}, f32[2,16,1024]{2,1,0:T(8,128)S(1)}, u32[]{:S(2)}, u32[]{:S(2)}) collective-permute-start(f32[2,16,1024]{2,1,0:T(8,128)S(1)} %add.34.b0), channel_id=1, source_target_pairs={{0,8},{4,12},{8,0},{12,4},{16,24},{20,28},{24,16},{28,20},{1,9},{5... | collective-permute-start | bytes 393224 | tf_op jit(solution)/shard_map/ppermute | solution.py:290
  28.8 2.3 %collective-permute-done.2.a1 = f32[2,16,1024]{2,1,0:T(8,128)S(1)} collective-permute-done((f32[2,16,1024]{2,1,0:T(8,128)S(1)}, f32[2,16,1024]{2,1,0:T(8,128)S(1)}, u32[]{:S(2)}, u32[]{:S(2)}) %collective-permute-start.2) | collective-permute-done | bytes 131104 | tf_op jit(solution)/shard_map/ppermute | solution.py:290
  31.2 1.2 %collective-permute-done.4.b1 = f32[2,16,1024]{2,1,0:T(8,128)S(1)} collective-permute-done((f32[2,16,1024]{2,1,0:T(8,128)S(1)}, f32[2,16,1024]{2,1,0:T(8,128)S(1)}, u32[]{:S(2)}, u32[]{:S(2)}) %collective-permute-start.4) | collective-permute-done | bytes 131104 | tf_op jit(solution)/shard_map/ppermute | solution.py:290
  32.3 1.4 %shard_map.89 = (f32[17,16,2048]{2,1,0:T(8,128)S(1)}, f32[17,16,2048]{2,1,0:T(8,128)S(1)}, f32[16,2048]{1,0:T(8,128)S(1)}, f32[4,128]{1,0:T(4,128)S(1)}, f32[32,128]{1,0:T(8,128)S(1)}) custom-call(f32[2,16,1024]{2,1,0:T(8,128)S(1)} %add.33.a0, f32[2,16,1024]{2,1,0:T(8,128)S(1)} %collective-permute-done.2.a1, f32[2,16,1024]{2,1,0:T(8,128)S(1)} %add.34.b0, ...), custom_call_target="tpu_custom_call" | custom-call | tf_op jit(solution)/shard_map/pallas_call | solution.py:337
  33.7 8.9 %all_to_all.23 = f32[32,1,128]{2,1,0:T(1,128)S(1)} all-to-all(f32[32,1,128]{2,1,0:T(1,128)S(1)} %bitcast.13), channel_id=1, replica_groups=mesh['ev'=8,'ch'=4] {'ev','ch'}, dimensions={0} | all-to-all | bytes 32768 | tf_op jit(solution)/shard_map/all_to_all | solution.py:318
  42.6 1.7 %shard_map.90 = (f32[2,16,1024]{2,1,0:T(8,128)S(1)}, f32[2,16,1024]{2,1,0:T(8,128)S(1)}, f32[1,8,128]{2,1,0:T(8,128)S(1)}) custom-call(f32[32,128]{1,0:T(8,128)S(1)} %bitcast.12, f32[32,128]{1,0:T(8,128)S(1)} %bitcast.11, f32[17,16,2048]{2,1,0:T(8,128)S(1)} %get-tuple-element.25.mine_ref, f32[17,16,2048]{2,1,0:T(8,128)S(1)} %get-tuple-element.26.theirs_ref), custom_call_target="tpu_custom_call" | custom-call | tf_op jit(solution)/shard_map/pallas_call | solution.py:320
  44.3 0.6 %collective-permute-start.9 = (f32[2,16,1024]{2,1,0:T(8,128)S(1)}, f32[2,16,1024]{2,1,0:T(8,128)S(1)}, u32[]{:S(2)}, u32[]{:S(2)}) collective-permute-start(f32[2,16,1024]{2,1,0:T(8,128)S(1)} %get-tuple-element.27), channel_id=1, source_target_pairs={{0,8},{4,12},{8,0},{12,4},{16,24},{20,28},{24,16},{28,20},{1,9},{5... | collective-permute-start | bytes 393224 | tf_op jit(solution)/shard_map/ppermute | solution.py:290
  44.9 0.5 collective-permute-start.11
  45.5 4.1 %collective-permute-done.9 = f32[2,16,1024]{2,1,0:T(8,128)S(1)} collective-permute-done((f32[2,16,1024]{2,1,0:T(8,128)S(1)}, f32[2,16,1024]{2,1,0:T(8,128)S(1)}, u32[]{:S(2)}, u32[]{:S(2)}) %collective-permute-start.9) | collective-permute-done | bytes 131104 | tf_op jit(solution)/shard_map/ppermute | solution.py:290
  49.5 0.7 %collective-permute-start.10 = (f32[2,16,1024]{2,1,0:T(8,128)S(1)}, f32[2,16,1024]{2,1,0:T(8,128)S(1)}, u32[]{:S(2)}, u32[]{:S(2)}) collective-permute-start(f32[2,16,1024]{2,1,0:T(8,128)S(1)} %add.38.a0), channel_id=1, source_target_pairs={{0,16},{4,20},{8,24},{12,28},{16,0},{20,4},{24,8},{28,12},{1,17},{... | collective-permute-start | bytes 393224 | tf_op jit(solution)/shard_map/ppermute | solution.py:290
  50.2 1.2 %collective-permute-start.12 = (f32[2,16,1024]{2,1,0:T(8,128)S(1)}, f32[2,16,1024]{2,1,0:T(8,128)S(1)}, u32[]{:S(2)}, u32[]{:S(2)}) collective-permute-start(f32[2,16,1024]{2,1,0:T(8,128)S(1)} %add.39.b0), channel_id=1, source_target_pairs={{0,8},{4,12},{8,0},{12,4},{16,24},{20,28},{24,16},{28,20},{1,9},{5... | collective-permute-start | bytes 393224 | tf_op jit(solution)/shard_map/ppermute | solution.py:290
  51.4 3.1 %collective-permute-done.10.a1 = f32[2,16,1024]{2,1,0:T(8,128)S(1)} collective-permute-done((f32[2,16,1024]{2,1,0:T(8,128)S(1)}, f32[2,16,1024]{2,1,0:T(8,128)S(1)}, u32[]{:S(2)}, u32[]{:S(2)}) %collective-permute-start.10) | collective-permute-done | bytes 131104 | tf_op jit(solution)/shard_map/ppermute | solution.py:290
  54.6 0.7 %collective-permute-done.12.b1 = f32[2,16,1024]{2,1,0:T(8,128)S(1)} collective-permute-done((f32[2,16,1024]{2,1,0:T(8,128)S(1)}, f32[2,16,1024]{2,1,0:T(8,128)S(1)}, u32[]{:S(2)}, u32[]{:S(2)}) %collective-permute-start.12) | collective-permute-done | bytes 131104 | tf_op jit(solution)/shard_map/ppermute | solution.py:290
  55.2 0.1 shard_map.91
  55.4 1.2 %collective-permute-done.13 = f32[1,16,128]{2,1,0:T(8,128)S(1)} collective-permute-done((f32[1,16,128]{2,1,0:T(8,128)S(1)}, f32[1,16,128]{2,1,0:T(8,128)S(1)}, u32[]{:S(2)}, u32[]{:S(2)}) %collective-permute-start.13) | collective-permute-done | bytes 8224 | tf_op jit(solution)/shard_map/ppermute | solution.py:290
  56.6 0.5 collective-permute-start.16
  57.1 1.6 %collective-permute-start.15 = (f32[1,16,128]{2,1,0:T(8,128)S(1)}, f32[1,16,128]{2,1,0:T(8,128)S(1)}, u32[]{:S(2)}, u32[]{:S(2)}) collective-permute-start(f32[1,16,128]{2,1,0:T(8,128)S(1)} %add.40), channel_id=1, source_target_pairs={{0,2},{1,3},{2,0},{3,1},{4,6},{5,7},{6,4},{7,5},{8,10},{9,11},{10,... | collective-permute-start | bytes 24584 | tf_op jit(solution)/shard_map/ppermute | solution.py:290
  58.6 2.3 %collective-permute-start.14 = (f32[1,16,128]{2,1,0:T(8,128)S(1)}, f32[1,16,128]{2,1,0:T(8,128)S(1)}, u32[]{:S(2)}, u32[]{:S(2)}) collective-permute-start(f32[1,16,128]{2,1,0:T(8,128)S(1)} %add.40), channel_id=1, source_target_pairs={{0,1},{1,0},{2,3},{3,2},{4,5},{5,4},{6,7},{7,6},{8,9},{9,8},{10,11... | collective-permute-start | bytes 24584 | tf_op jit(solution)/shard_map/ppermute | solution.py:290
  61.0 1.1 %collective-permute-done.16 = f32[1,16,128]{2,1,0:T(8,128)S(1)} collective-permute-done((f32[1,16,128]{2,1,0:T(8,128)S(1)}, f32[1,16,128]{2,1,0:T(8,128)S(1)}, u32[]{:S(2)}, u32[]{:S(2)}) %collective-permute-start.16) | collective-permute-done | bytes 8224 | tf_op jit(solution)/shard_map/ppermute | solution.py:290
  62.0 0.6 collective-permute-done.14
  62.6 0.8 %shard_map.92 = (f32[16,16]{1,0:T(8,128)}, f32[16,4096]{1,0:T(8,128)}) custom-call(f32[1,16,128]{2,1,0:T(8,128)S(1)} %add_add_fusion.sums_ref, f32[16,2048]{1,0:T(8,128)S(1)} %get-tuple-element.32.mine_ref, f32[16,2048]{1,0:T(8,128)S(1)} %collective-permute-done.17.theirs_ref, f32[4,128]{1,0:T(4,128)S(1)} %get-tuple-element.33.dsrc_ref, f32[16,16]{1,0:T(8,128)S(1)} %copy-done.1), custom_call_target="tpu_custom_call" | custom-call | tf_op jit(solution)/shard_map/pallas_call | solution.py:348
  (24 shorter events, 0.2 us)
Async XLA Ops:
  3.8 14.4 %collective-permute-start = (f32[17,16,2048]{2,1,0:T(8,128)S(1)}, f32[17,16,2048]{2,1,0:T(8,128)S(1)}, u32[]{:S(2)}, u32[]{:S(2)}) collective-permute-start(f32[17,16,2048]{2,1,0:T(8,128)S(1)} %get-tuple-element.20), channel_id=1, source_target_pairs={{0,4},{4,0},{8,12},{12,8},{16,20},{20,16},{24,28},{28,24},{1,5},{5... | collective-permute-start | bytes 6684680 | tf_op jit(solution)/shard_map/ppermute | solution.py:290
  20.0 1.3 %collective-permute-start.5 = (f32[1,8,128]{2,1,0:T(8,128)S(1)}, f32[1,8,128]{2,1,0:T(8,128)S(1)}, u32[]{:S(2)}, u32[]{:S(2)}) collective-permute-start(f32[1,8,128]{2,1,0:T(8,128)S(1)} %get-tuple-element.23.x_ref), channel_id=1, source_target_pairs={{0,4},{4,0},{8,12},{12,8},{16,20},{20,16},{24,28},{28,24},{1,5},{5... | collective-permute-start | bytes 12296 | tf_op jit(solution)/shard_map/ppermute | solution.py:290
  20.1 5.9 %collective-permute-start.1 = (f32[2,16,1024]{2,1,0:T(8,128)S(1)}, f32[2,16,1024]{2,1,0:T(8,128)S(1)}, u32[]{:S(2)}, u32[]{:S(2)}) collective-permute-start(f32[2,16,1024]{2,1,0:T(8,128)S(1)} %get-tuple-element.21), channel_id=1, source_target_pairs={{0,8},{4,12},{8,0},{12,4},{16,24},{20,28},{24,16},{28,20},{1,9},{5... | collective-permute-start | bytes 393224 | tf_op jit(solution)/shard_map/ppermute | solution.py:290
  20.8 6.5 %collective-permute-start.3 = (f32[2,16,1024]{2,1,0:T(8,128)S(1)}, f32[2,16,1024]{2,1,0:T(8,128)S(1)}, u32[]{:S(2)}, u32[]{:S(2)}) collective-permute-start(f32[2,16,1024]{2,1,0:T(8,128)S(1)} %get-tuple-element.22), channel_id=1, source_target_pairs={{0,16},{4,20},{8,24},{12,28},{16,0},{20,4},{24,8},{28,12},{1,17},{... | collective-permute-start | bytes 393224 | tf_op jit(solution)/shard_map/ppermute | solution.py:290
  21.3 7.5 %collective-permute-start.8 = (f32[1,8,128]{2,1,0:T(8,128)S(1)}, f32[1,8,128]{2,1,0:T(8,128)S(1)}, u32[]{:S(2)}, u32[]{:S(2)}) collective-permute-start(f32[1,8,128]{2,1,0:T(8,128)S(1)} %shard_map.88), channel_id=1, source_target_pairs={{0,3},{1,2},{2,1},{3,0},{4,7},{5,6},{6,5},{7,4},{8,11},{9,10},{10,... | collective-permute-start | bytes 12296 | tf_op jit(solution)/shard_map/ppermute | solution.py:290
  21.9 7.0 %collective-permute-start.7 = (f32[1,8,128]{2,1,0:T(8,128)S(1)}, f32[1,8,128]{2,1,0:T(8,128)S(1)}, u32[]{:S(2)}, u32[]{:S(2)}) collective-permute-start(f32[1,8,128]{2,1,0:T(8,128)S(1)} %shard_map.88), channel_id=1, source_target_pairs={{0,2},{1,3},{2,0},{3,1},{4,6},{5,7},{6,4},{7,5},{8,10},{9,11},{10,... | collective-permute-start | bytes 12296 | tf_op jit(solution)/shard_map/ppermute | solution.py:290
  23.3 5.5 %collective-permute-start.6 = (f32[1,8,128]{2,1,0:T(8,128)S(1)}, f32[1,8,128]{2,1,0:T(8,128)S(1)}, u32[]{:S(2)}, u32[]{:S(2)}) collective-permute-start(f32[1,8,128]{2,1,0:T(8,128)S(1)} %shard_map.88), channel_id=1, source_target_pairs={{0,1},{1,0},{2,3},{3,2},{4,5},{5,4},{6,7},{7,6},{8,9},{9,8},{10,11... | collective-permute-start | bytes 12296 | tf_op jit(solution)/shard_map/ppermute | solution.py:290
  26.0 5.1 %collective-permute-start.2 = (f32[2,16,1024]{2,1,0:T(8,128)S(1)}, f32[2,16,1024]{2,1,0:T(8,128)S(1)}, u32[]{:S(2)}, u32[]{:S(2)}) collective-permute-start(f32[2,16,1024]{2,1,0:T(8,128)S(1)} %add.33.a0), channel_id=1, source_target_pairs={{0,16},{4,20},{8,24},{12,28},{16,0},{20,4},{24,8},{28,12},{1,17},{... | collective-permute-start | bytes 393224 | tf_op jit(solution)/shard_map/ppermute | solution.py:290
  27.3 5.0 %collective-permute-start.4 = (f32[2,16,1024]{2,1,0:T(8,128)S(1)}, f32[2,16,1024]{2,1,0:T(8,128)S(1)}, u32[]{:S(2)}, u32[]{:S(2)}) collective-permute-start(f32[2,16,1024]{2,1,0:T(8,128)S(1)} %add.34.b0), channel_id=1, source_target_pairs={{0,8},{4,12},{8,0},{12,4},{16,24},{20,28},{24,16},{28,20},{1,9},{5... | collective-permute-start | bytes 393224 | tf_op jit(solution)/shard_map/ppermute | solution.py:290
  42.5 12.7 %copy-start = (f32[16,4096]{1,0:T(8,128)S(1)}, f32[16,4096]{1,0:T(8,128)}, u32[]{:S(2)}) copy-start(f32[16,4096]{1,0:T(8,128)} %site_ref.1) | copy-start | bytes 786436
  42.5 20.0 %copy-start.1 = (f32[16,16]{1,0:T(8,128)S(1)}, f32[16,16]{1,0:T(8,128)}, u32[]{:S(2)}) copy-start(f32[16,16]{1,0:T(8,128)} %source_ref.1) | copy-start | bytes 3076
  44.3 5.2 %collective-permute-start.9 = (f32[2,16,1024]{2,1,0:T(8,128)S(1)}, f32[2,16,1024]{2,1,0:T(8,128)S(1)}, u32[]{:S(2)}, u32[]{:S(2)}) collective-permute-start(f32[2,16,1024]{2,1,0:T(8,128)S(1)} %get-tuple-element.27), channel_id=1, source_target_pairs={{0,8},{4,12},{8,0},{12,4},{16,24},{20,28},{24,16},{28,20},{1,9},{5... | collective-permute-start | bytes 393224 | tf_op jit(solution)/shard_map/ppermute | solution.py:290
  44.9 5.3 %collective-permute-start.11 = (f32[2,16,1024]{2,1,0:T(8,128)S(1)}, f32[2,16,1024]{2,1,0:T(8,128)S(1)}, u32[]{:S(2)}, u32[]{:S(2)}) collective-permute-start(f32[2,16,1024]{2,1,0:T(8,128)S(1)} %get-tuple-element.28), channel_id=1, source_target_pairs={{0,16},{4,20},{8,24},{12,28},{16,0},{20,4},{24,8},{28,12},{1,17},{... | collective-permute-start | bytes 393224 | tf_op jit(solution)/shard_map/ppermute | solution.py:290
  49.5 5.0 %collective-permute-start.10 = (f32[2,16,1024]{2,1,0:T(8,128)S(1)}, f32[2,16,1024]{2,1,0:T(8,128)S(1)}, u32[]{:S(2)}, u32[]{:S(2)}) collective-permute-start(f32[2,16,1024]{2,1,0:T(8,128)S(1)} %add.38.a0), channel_id=1, source_target_pairs={{0,16},{4,20},{8,24},{12,28},{16,0},{20,4},{24,8},{28,12},{1,17},{... | collective-permute-start | bytes 393224 | tf_op jit(solution)/shard_map/ppermute | solution.py:290
  50.2 5.0 %collective-permute-start.12 = (f32[2,16,1024]{2,1,0:T(8,128)S(1)}, f32[2,16,1024]{2,1,0:T(8,128)S(1)}, u32[]{:S(2)}, u32[]{:S(2)}) collective-permute-start(f32[2,16,1024]{2,1,0:T(8,128)S(1)} %add.39.b0), channel_id=1, source_target_pairs={{0,8},{4,12},{8,0},{12,4},{16,24},{20,28},{24,16},{28,20},{1,9},{5... | collective-permute-start | bytes 393224 | tf_op jit(solution)/shard_map/ppermute | solution.py:290
  55.4 1.2 %collective-permute-start.13 = (f32[1,16,128]{2,1,0:T(8,128)S(1)}, f32[1,16,128]{2,1,0:T(8,128)S(1)}, u32[]{:S(2)}, u32[]{:S(2)}) collective-permute-start(f32[1,16,128]{2,1,0:T(8,128)S(1)} %get-tuple-element.31), channel_id=1, source_target_pairs={{0,4},{4,0},{8,12},{12,8},{16,20},{20,16},{24,28},{28,24},{1,5},{5... | collective-permute-start | bytes 24584 | tf_op jit(solution)/shard_map/ppermute | solution.py:290
  56.6 5.4 %collective-permute-start.16 = (f32[1,16,128]{2,1,0:T(8,128)S(1)}, f32[1,16,128]{2,1,0:T(8,128)S(1)}, u32[]{:S(2)}, u32[]{:S(2)}) collective-permute-start(f32[1,16,128]{2,1,0:T(8,128)S(1)} %add.40), channel_id=1, source_target_pairs={{0,3},{1,2},{2,1},{3,0},{4,7},{5,6},{6,5},{7,4},{8,11},{9,10},{10,... | collective-permute-start | bytes 24584 | tf_op jit(solution)/shard_map/ppermute | solution.py:290
  57.1 4.9 %collective-permute-start.15 = (f32[1,16,128]{2,1,0:T(8,128)S(1)}, f32[1,16,128]{2,1,0:T(8,128)S(1)}, u32[]{:S(2)}, u32[]{:S(2)}) collective-permute-start(f32[1,16,128]{2,1,0:T(8,128)S(1)} %add.40), channel_id=1, source_target_pairs={{0,2},{1,3},{2,0},{3,1},{4,6},{5,7},{6,4},{7,5},{8,10},{9,11},{10,... | collective-permute-start | bytes 24584 | tf_op jit(solution)/shard_map/ppermute | solution.py:290
  58.6 3.9 %collective-permute-start.14 = (f32[1,16,128]{2,1,0:T(8,128)S(1)}, f32[1,16,128]{2,1,0:T(8,128)S(1)}, u32[]{:S(2)}, u32[]{:S(2)}) collective-permute-start(f32[1,16,128]{2,1,0:T(8,128)S(1)} %add.40), channel_id=1, source_target_pairs={{0,1},{1,0},{2,3},{3,2},{4,5},{5,4},{6,7},{7,6},{8,9},{9,8},{10,11... | collective-permute-start | bytes 24584 | tf_op jit(solution)/shard_map/ppermute | solution.py:290
  60.9 1.6 %collective-permute-start.17 = (f32[16,2048]{1,0:T(8,128)S(1)}, f32[16,2048]{1,0:T(8,128)S(1)}, u32[]{:S(2)}, u32[]{:S(2)}) collective-permute-start(f32[16,2048]{1,0:T(8,128)S(1)} %get-tuple-element.32.mine_ref), channel_id=1, source_target_pairs={{0,4},{4,0},{8,12},{12,8},{16,20},{20,16},{24,28},{28,24},{1,5},{5... | collective-permute-start | bytes 393224 | tf_op jit(solution)/shard_map/ppermute | solution.py:290

commit v7 on v6

--- a/solution.py
+++ b/solution.py
@@ -103,10 +103,10 @@
                 site = site_ref[:, at]
                 for k, e in enumerate(events):
                     time = jnp.broadcast_to(travel[e:e + 1, at], (freqs, TILE))
-                    resid = (spec[e, :, at] - source[e]) + (att * time - site)
+                    valid = jnp.broadcast_to(ref[ev_n, e:e + 1, here], (freqs, TILE))
+                    resid = ((spec[e, :, at] - source[e]) + (att * time - site)) * valid
                     ref[e, :, here] = resid
-                    valid = jnp.broadcast_to(ref[ev_n, e:e + 1, here], (freqs, TILE))
-                    totals[k % CHAINS] += jnp.abs(resid) * valid
+                    totals[k % CHAINS] += jnp.abs(resid)
             return tuple(totals)
         totals = lax.fori_loop(0, half_tiles, step, totals, unroll=2)
     total = sum(totals[1:], totals[0])
@@ -129,8 +129,15 @@
     delta = jnp.broadcast_to(as_column(delta, freqs), (freqs, TILE))
     per_row = LANES // freqs
     zero = jnp.zeros((freqs, TILE), F32)
-    a_ref[...] = jnp.zeros_like(a_ref)
-    b_ref[...] = jnp.zeros_like(b_ref)
+    unit = pl.reciprocal(delta, approx=True)
+    missing = [jnp.full((ev_n, TILE), -float(half // TILE), F32) for _ in range(2)]
+    for out, base in ((a_ref, 0), (b_ref, quarter)):
+        out[0] = jnp.zeros((freqs, quarter), F32)
+        for t in range(0, quarter, TILE):
+            rows = [ref[ev_n, :, base + t:base + t + TILE] for ref in (mine_ref, theirs_ref)]
+            missing = [x + y for x, y in zip(missing, rows)]
+            lost = jnp.sum(rows[0] + rows[1], axis=0, keepdims=True) - 2.0 * ev_n
+            out[1, :, t:t + TILE] = jnp.broadcast_to(lost, (freqs, TILE)) * unit
     for which, ref in enumerate((mine_ref, theirs_ref)):
         owner = core if which == 0 else 1 - core
         final = which == 1
@@ -146,8 +153,7 @@
                     num, den = out[0, :, here], out[1, :, here]
                     for k, e in enumerate(events):
                         resid = ref[e, :, at]
-                        valid = jnp.broadcast_to(ref[ev_n, e:e + 1, at], (freqs, TILE))
-                        weight = pl.reciprocal(jnp.maximum(jnp.abs(resid), delta), approx=True) * valid
+                        weight = pl.reciprocal(jnp.maximum(jnp.abs(resid), delta), approx=True)
                         product = weight * resid
                         num, den = num + product, den + weight
                         acc[2 * k] += product
@@ -157,7 +163,10 @@
                     out[0, :, here] = num
                     out[1, :, here] = den
                 return tuple(acc)
-            acc = lax.fori_loop(0, quarter // TILE, step, (zero,) * (2 * GROUP), unroll=8)
+            init = []
+            for e in events:
+                init += [zero, jnp.broadcast_to(missing[which][e:e + 1], (freqs, TILE)) * unit]
+            acc = lax.fori_loop(0, quarter // TILE, step, tuple(init), unroll=8)
             nums += [x * delta for x in acc[0::2]]
             dens += [x * delta for x in acc[1::2]]
         rows_each = ev_n // per_row
@@ -208,10 +217,10 @@
             site = dsite_ref[:, at]
             for e in range(ev_n):
                 src = shift[pl.ds(pl.multiple_of((owner * ev_n + e) * freqs, freqs), freqs), :]
-                resid = (ref[e, :, at] - src) - site
+                valid = jnp.broadcast_to(ref[ev_n, e:e + 1, at], (freqs, TILE))
+                resid = ((ref[e, :, at] - src) - site) * valid
                 out[e, :, at] = resid
-                valid = jnp.broadcast_to(ref[ev_n, e:e + 1, at], (freqs, TILE))
-                totals[e % CHAINS] += jnp.abs(resid) * valid
+                totals[e % CHAINS] += jnp.abs(resid)
             return tuple(totals)
         totals = lax.fori_loop(0, half // TILE, step, totals, unroll=2)
     total = sum(totals[1:], totals[0])

time: 63.6 us -> 63.2 us (level)
  no operation moved by 1% of the time
where the time goes in v7:
time: 63.2 us; the launch traced here: 63 us
  blocking collectives  22.8 us (36%)
  starting transfers between devices  16.3 us (26%)
  waiting for transfers between devices  14.5 us (23%)
  Pallas kernels  8.59 us (14%)
  between operations  0.71 us (1%)
    all_to_all x2, blocking collectives, on_device(): total = lax.all_to_all(sums, ('ev', 'ch'), 0, 0)  22.8 us
    ppermute x18, starting transfers between devices, swap(): return lax.ppermute(value, axis, [(i, i ^ bit) for i in range(size)])  16.3 us
    ppermute x18, waiting for transfers between devices, swap(): return lax.ppermute(value, axis, [(i, i ^ bit) for i in range(size)])  14.5 us
    pallas_call x1, Pallas kernels, on_device(): call(resid_kernel, [slabs, slabs, (devices, LANES)], [HBM] * 7, [pltpu.VM...  3.24 us
    pallas_call x2, Pallas kernels, on_device(): call(functools.partial(weight_kernel, freqs), [(2, freqs, quarter), (2, f...  3.04 us
    pallas_call x1, Pallas kernels, on_device(): call(update_kernel, [slabs, slabs, (freqs, half), (src_rows, LANES), (dev...  1.35 us
  transfers between devices with their start and end apart: 18, of which 9 were waited for; matrix products, arithmetic and copies ran while one was open for 0% of the time, Pallas kernels for 0%

profile of v7, /device:TPU:0, one launch (start us, length us, event | category | flops | bytes accessed | tf_op | source)
XLA Modules:
  0.0 63.0 jit_solution(15292385734944376628)
XLA Ops:
  0.6 3.2 %shard_map.86 = (f32[17,16,2048]{2,1,0:T(8,128)S(1)}, f32[17,16,2048]{2,1,0:T(8,128)S(1)}, f32[32,128]{1,0:T(8,128)S(1)}) custom-call(f32[16,16,4096]{2,1,0:T(8,128)} %spec_hbm.1, s32[16,32]{1,0:T(8,128)} %mask_hbm.1, f32[16,16]{1,0:T(8,128)} %source_ref.1, f32[16,4096]{1,0:T(8,128)} %site_ref.1, f32[3,16]{1,0:T(4,128)} %pos_hbm.1, f32[2,4096]{1,0:T(2,128)} %chan_hbm.1, ...), custom_call_target="tpu_custom_call" | custom-call | tf_op jit(solution)/shard_map/pallas_call | solution.py:316
  3.9 0.5 collective-permute-start
  4.4 13.9 %all_to_all.22 = f32[32,1,128]{2,1,0:T(1,128)S(1)} all-to-all(f32[32,1,128]{2,1,0:T(1,128)S(1)} %bitcast.14), channel_id=1, replica_groups=mesh['ev'=8,'ch'=4] {'ev','ch'}, dimensions={0} | all-to-all | bytes 32768 | tf_op jit(solution)/shard_map/all_to_all | solution.py:327
  18.3 1.5 %shard_map.87 = (f32[2,16,1024]{2,1,0:T(8,128)S(1)}, f32[2,16,1024]{2,1,0:T(8,128)S(1)}, f32[1,8,128]{2,1,0:T(8,128)S(1)}) custom-call(f32[32,128]{1,0:T(8,128)S(1)} %bitcast.9, f32[32,128]{1,0:T(8,128)S(1)} %bitcast.10, f32[17,16,2048]{2,1,0:T(8,128)S(1)} %get-tuple-element.19.mine_ref, f32[17,16,2048]{2,1,0:T(8,128)S(1)} %collective-permute-done.theirs_ref), custom_call_target="tpu_custom_call" | custom-call | tf_op jit(solution)/shard_map/pallas_call | solution.py:329
  19.9 0.6 %collective-permute-start.1 = (f32[2,16,1024]{2,1,0:T(8,128)S(1)}, f32[2,16,1024]{2,1,0:T(8,128)S(1)}, u32[]{:S(2)}, u32[]{:S(2)}) collective-permute-start(f32[2,16,1024]{2,1,0:T(8,128)S(1)} %get-tuple-element.21), channel_id=1, source_target_pairs={{0,8},{4,12},{8,0},{12,4},{16,24},{20,28},{24,16},{28,20},{1,9},{5... | collective-permute-start | bytes 393224 | tf_op jit(solution)/shard_map/ppermute | solution.py:299
  20.6 0.5 collective-permute-start.3
  21.1 0.6 collective-permute-start.8
  21.7 1.4 %collective-permute-start.7 = (f32[1,8,128]{2,1,0:T(8,128)S(1)}, f32[1,8,128]{2,1,0:T(8,128)S(1)}, u32[]{:S(2)}, u32[]{:S(2)}) collective-permute-start(f32[1,8,128]{2,1,0:T(8,128)S(1)} %shard_map.88), channel_id=1, source_target_pairs={{0,2},{1,3},{2,0},{3,1},{4,6},{5,7},{6,4},{7,5},{8,10},{9,11},{10,... | collective-permute-start | bytes 12296 | tf_op jit(solution)/shard_map/ppermute | solution.py:299
  23.1 2.4 %collective-permute-start.6 = (f32[1,8,128]{2,1,0:T(8,128)S(1)}, f32[1,8,128]{2,1,0:T(8,128)S(1)}, u32[]{:S(2)}, u32[]{:S(2)}) collective-permute-start(f32[1,8,128]{2,1,0:T(8,128)S(1)} %shard_map.88), channel_id=1, source_target_pairs={{0,1},{1,0},{2,3},{3,2},{4,5},{5,4},{6,7},{7,6},{8,9},{9,8},{10,11... | collective-permute-start | bytes 12296 | tf_op jit(solution)/shard_map/ppermute | solution.py:299
  25.5 0.3 collective-permute-done.1
  25.9 1.2 %collective-permute-start.2 = (f32[2,16,1024]{2,1,0:T(8,128)S(1)}, f32[2,16,1024]{2,1,0:T(8,128)S(1)}, u32[]{:S(2)}, u32[]{:S(2)}) collective-permute-start(f32[2,16,1024]{2,1,0:T(8,128)S(1)} %add.33.a0), channel_id=1, source_target_pairs={{0,16},{4,20},{8,24},{12,28},{16,0},{20,4},{24,8},{28,12},{1,17},{... | collective-permute-start | bytes 393224 | tf_op jit(solution)/shard_map/ppermute | solution.py:299
  27.1 1.5 %collective-permute-start.4 = (f32[2,16,1024]{2,1,0:T(8,128)S(1)}, f32[2,16,1024]{2,1,0:T(8,128)S(1)}, u32[]{:S(2)}, u32[]{:S(2)}) collective-permute-start(f32[2,16,1024]{2,1,0:T(8,128)S(1)} %add.34.b0), channel_id=1, source_target_pairs={{0,8},{4,12},{8,0},{12,4},{16,24},{20,28},{24,16},{28,20},{1,9},{5... | collective-permute-start | bytes 393224 | tf_op jit(solution)/shard_map/ppermute | solution.py:299
  28.7 2.3 %collective-permute-done.2.a1 = f32[2,16,1024]{2,1,0:T(8,128)S(1)} collective-permute-done((f32[2,16,1024]{2,1,0:T(8,128)S(1)}, f32[2,16,1024]{2,1,0:T(8,128)S(1)}, u32[]{:S(2)}, u32[]{:S(2)}) %collective-permute-start.2) | collective-permute-done | bytes 131104 | tf_op jit(solution)/shard_map/ppermute | solution.py:299
  31.0 1.2 %collective-permute-done.4.b1 = f32[2,16,1024]{2,1,0:T(8,128)S(1)} collective-permute-done((f32[2,16,1024]{2,1,0:T(8,128)S(1)}, f32[2,16,1024]{2,1,0:T(8,128)S(1)}, u32[]{:S(2)}, u32[]{:S(2)}) %collective-permute-start.4) | collective-permute-done | bytes 131104 | tf_op jit(solution)/shard_map/ppermute | solution.py:299
  32.1 1.3 %shard_map.89 = (f32[17,16,2048]{2,1,0:T(8,128)S(1)}, f32[17,16,2048]{2,1,0:T(8,128)S(1)}, f32[16,2048]{1,0:T(8,128)S(1)}, f32[4,128]{1,0:T(4,128)S(1)}, f32[32,128]{1,0:T(8,128)S(1)}) custom-call(f32[2,16,1024]{2,1,0:T(8,128)S(1)} %add.33.a0, f32[2,16,1024]{2,1,0:T(8,128)S(1)} %collective-permute-done.2.a1, f32[2,16,1024]{2,1,0:T(8,128)S(1)} %add.34.b0, ...), custom_call_target="tpu_custom_call" | custom-call | tf_op jit(solution)/shard_map/pallas_call | solution.py:346
  33.5 8.9 %all_to_all.23 = f32[32,1,128]{2,1,0:T(1,128)S(1)} all-to-all(f32[32,1,128]{2,1,0:T(1,128)S(1)} %bitcast.13), channel_id=1, replica_groups=mesh['ev'=8,'ch'=4] {'ev','ch'}, dimensions={0} | all-to-all | bytes 32768 | tf_op jit(solution)/shard_map/all_to_all | solution.py:327
  42.4 1.5 %shard_map.90 = (f32[2,16,1024]{2,1,0:T(8,128)S(1)}, f32[2,16,1024]{2,1,0:T(8,128)S(1)}, f32[1,8,128]{2,1,0:T(8,128)S(1)}) custom-call(f32[32,128]{1,0:T(8,128)S(1)} %bitcast.12, f32[32,128]{1,0:T(8,128)S(1)} %bitcast.11, f32[17,16,2048]{2,1,0:T(8,128)S(1)} %get-tuple-element.25.mine_ref, f32[17,16,2048]{2,1,0:T(8,128)S(1)} %get-tuple-element.26.theirs_ref), custom_call_target="tpu_custom_call" | custom-call | tf_op jit(solution)/shard_map/pallas_call | solution.py:329
  43.9 0.6 %collective-permute-start.9 = (f32[2,16,1024]{2,1,0:T(8,128)S(1)}, f32[2,16,1024]{2,1,0:T(8,128)S(1)}, u32[]{:S(2)}, u32[]{:S(2)}) collective-permute-start(f32[2,16,1024]{2,1,0:T(8,128)S(1)} %get-tuple-element.27), channel_id=1, source_target_pairs={{0,8},{4,12},{8,0},{12,4},{16,24},{20,28},{24,16},{28,20},{1,9},{5... | collective-permute-start | bytes 393224 | tf_op jit(solution)/shard_map/ppermute | solution.py:299
  44.5 0.5 collective-permute-start.11
  45.1 4.1 %collective-permute-done.9 = f32[2,16,1024]{2,1,0:T(8,128)S(1)} collective-permute-done((f32[2,16,1024]{2,1,0:T(8,128)S(1)}, f32[2,16,1024]{2,1,0:T(8,128)S(1)}, u32[]{:S(2)}, u32[]{:S(2)}) %collective-permute-start.9) | collective-permute-done | bytes 131104 | tf_op jit(solution)/shard_map/ppermute | solution.py:299
  49.1 0.7 %collective-permute-start.10 = (f32[2,16,1024]{2,1,0:T(8,128)S(1)}, f32[2,16,1024]{2,1,0:T(8,128)S(1)}, u32[]{:S(2)}, u32[]{:S(2)}) collective-permute-start(f32[2,16,1024]{2,1,0:T(8,128)S(1)} %add.38.a0), channel_id=1, source_target_pairs={{0,16},{4,20},{8,24},{12,28},{16,0},{20,4},{24,8},{28,12},{1,17},{... | collective-permute-start | bytes 393224 | tf_op jit(solution)/shard_map/ppermute | solution.py:299
  49.8 1.2 %collective-permute-start.12 = (f32[2,16,1024]{2,1,0:T(8,128)S(1)}, f32[2,16,1024]{2,1,0:T(8,128)S(1)}, u32[]{:S(2)}, u32[]{:S(2)}) collective-permute-start(f32[2,16,1024]{2,1,0:T(8,128)S(1)} %add.39.b0), channel_id=1, source_target_pairs={{0,8},{4,12},{8,0},{12,4},{16,24},{20,28},{24,16},{28,20},{1,9},{5... | collective-permute-start | bytes 393224 | tf_op jit(solution)/shard_map/ppermute | solution.py:299
  51.0 3.1 %collective-permute-done.10.a1 = f32[2,16,1024]{2,1,0:T(8,128)S(1)} collective-permute-done((f32[2,16,1024]{2,1,0:T(8,128)S(1)}, f32[2,16,1024]{2,1,0:T(8,128)S(1)}, u32[]{:S(2)}, u32[]{:S(2)}) %collective-permute-start.10) | collective-permute-done | bytes 131104 | tf_op jit(solution)/shard_map/ppermute | solution.py:299
  54.2 0.7 %collective-permute-done.12.b1 = f32[2,16,1024]{2,1,0:T(8,128)S(1)} collective-permute-done((f32[2,16,1024]{2,1,0:T(8,128)S(1)}, f32[2,16,1024]{2,1,0:T(8,128)S(1)}, u32[]{:S(2)}, u32[]{:S(2)}) %collective-permute-start.12) | collective-permute-done | bytes 131104 | tf_op jit(solution)/shard_map/ppermute | solution.py:299
  54.9 0.1 shard_map.91
  55.0 1.2 %collective-permute-done.13 = f32[1,16,128]{2,1,0:T(8,128)S(1)} collective-permute-done((f32[1,16,128]{2,1,0:T(8,128)S(1)}, f32[1,16,128]{2,1,0:T(8,128)S(1)}, u32[]{:S(2)}, u32[]{:S(2)}) %collective-permute-start.13) | collective-permute-done | bytes 8224 | tf_op jit(solution)/shard_map/ppermute | solution.py:299
  56.2 0.5 collective-permute-start.16
  56.7 1.6 %collective-permute-start.15 = (f32[1,16,128]{2,1,0:T(8,128)S(1)}, f32[1,16,128]{2,1,0:T(8,128)S(1)}, u32[]{:S(2)}, u32[]{:S(2)}) collective-permute-start(f32[1,16,128]{2,1,0:T(8,128)S(1)} %add.40), channel_id=1, source_target_pairs={{0,2},{1,3},{2,0},{3,1},{4,6},{5,7},{6,4},{7,5},{8,10},{9,11},{10,... | collective-permute-start | bytes 24584 | tf_op jit(solution)/shard_map/ppermute | solution.py:299
  58.3 2.3 %collective-permute-start.14 = (f32[1,16,128]{2,1,0:T(8,128)S(1)}, f32[1,16,128]{2,1,0:T(8,128)S(1)}, u32[]{:S(2)}, u32[]{:S(2)}) collective-permute-start(f32[1,16,128]{2,1,0:T(8,128)S(1)} %add.40), channel_id=1, source_target_pairs={{0,1},{1,0},{2,3},{3,2},{4,5},{5,4},{6,7},{7,6},{8,9},{9,8},{10,11... | collective-permute-start | bytes 24584 | tf_op jit(solution)/shard_map/ppermute | solution.py:299
  60.6 1.1 %collective-permute-done.16 = f32[1,16,128]{2,1,0:T(8,128)S(1)} collective-permute-done((f32[1,16,128]{2,1,0:T(8,128)S(1)}, f32[1,16,128]{2,1,0:T(8,128)S(1)}, u32[]{:S(2)}, u32[]{:S(2)}) %collective-permute-start.16) | collective-permute-done | bytes 8224 | tf_op jit(solution)/shard_map/ppermute | solution.py:299
  61.6 0.6 collective-permute-done.14
  62.2 0.8 %shard_map.92 = (f32[16,16]{1,0:T(8,128)}, f32[16,4096]{1,0:T(8,128)}) custom-call(f32[1,16,128]{2,1,0:T(8,128)S(1)} %add_add_fusion.sums_ref, f32[16,2048]{1,0:T(8,128)S(1)} %get-tuple-element.32.mine_ref, f32[16,2048]{1,0:T(8,128)S(1)} %collective-permute-done.17.theirs_ref, f32[4,128]{1,0:T(4,128)S(1)} %get-tuple-element.33.dsrc_ref, f32[16,16]{1,0:T(8,128)S(1)} %copy-done.1), custom_call_target="tpu_custom_call" | custom-call | tf_op jit(solution)/shard_map/pallas_call | solution.py:357
  (24 shorter events, 0.2 us)
Async XLA Ops:
  3.9 14.4 %collective-permute-start = (f32[17,16,2048]{2,1,0:T(8,128)S(1)}, f32[17,16,2048]{2,1,0:T(8,128)S(1)}, u32[]{:S(2)}, u32[]{:S(2)}) collective-permute-start(f32[17,16,2048]{2,1,0:T(8,128)S(1)} %get-tuple-element.20), channel_id=1, source_target_pairs={{0,4},{4,0},{8,12},{12,8},{16,20},{20,16},{24,28},{28,24},{1,5},{5... | collective-permute-start | bytes 6684680 | tf_op jit(solution)/shard_map/ppermute | solution.py:299
  19.9 1.3 %collective-permute-start.5 = (f32[1,8,128]{2,1,0:T(8,128)S(1)}, f32[1,8,128]{2,1,0:T(8,128)S(1)}, u32[]{:S(2)}, u32[]{:S(2)}) collective-permute-start(f32[1,8,128]{2,1,0:T(8,128)S(1)} %get-tuple-element.23.x_ref), channel_id=1, source_target_pairs={{0,4},{4,0},{8,12},{12,8},{16,20},{20,16},{24,28},{28,24},{1,5},{5... | collective-permute-start | bytes 12296 | tf_op jit(solution)/shard_map/ppermute | solution.py:299
  19.9 5.9 %collective-permute-start.1 = (f32[2,16,1024]{2,1,0:T(8,128)S(1)}, f32[2,16,1024]{2,1,0:T(8,128)S(1)}, u32[]{:S(2)}, u32[]{:S(2)}) collective-permute-start(f32[2,16,1024]{2,1,0:T(8,128)S(1)} %get-tuple-element.21), channel_id=1, source_target_pairs={{0,8},{4,12},{8,0},{12,4},{16,24},{20,28},{24,16},{28,20},{1,9},{5... | collective-permute-start | bytes 393224 | tf_op jit(solution)/shard_map/ppermute | solution.py:299
  20.6 6.5 %collective-permute-start.3 = (f32[2,16,1024]{2,1,0:T(8,128)S(1)}, f32[2,16,1024]{2,1,0:T(8,128)S(1)}, u32[]{:S(2)}, u32[]{:S(2)}) collective-permute-start(f32[2,16,1024]{2,1,0:T(8,128)S(1)} %get-tuple-element.22), channel_id=1, source_target_pairs={{0,16},{4,20},{8,24},{12,28},{16,0},{20,4},{24,8},{28,12},{1,17},{... | collective-permute-start | bytes 393224 | tf_op jit(solution)/shard_map/ppermute | solution.py:299
  21.1 7.5 %collective-permute-start.8 = (f32[1,8,128]{2,1,0:T(8,128)S(1)}, f32[1,8,128]{2,1,0:T(8,128)S(1)}, u32[]{:S(2)}, u32[]{:S(2)}) collective-permute-start(f32[1,8,128]{2,1,0:T(8,128)S(1)} %shard_map.88), channel_id=1, source_target_pairs={{0,3},{1,2},{2,1},{3,0},{4,7},{5,6},{6,5},{7,4},{8,11},{9,10},{10,... | collective-permute-start | bytes 12296 | tf_op jit(solution)/shard_map/ppermute | solution.py:299
  21.7 7.0 %collective-permute-start.7 = (f32[1,8,128]{2,1,0:T(8,128)S(1)}, f32[1,8,128]{2,1,0:T(8,128)S(1)}, u32[]{:S(2)}, u32[]{:S(2)}) collective-permute-start(f32[1,8,128]{2,1,0:T(8,128)S(1)} %shard_map.88), channel_id=1, source_target_pairs={{0,2},{1,3},{2,0},{3,1},{4,6},{5,7},{6,4},{7,5},{8,10},{9,11},{10,... | collective-permute-start | bytes 12296 | tf_op jit(solution)/shard_map/ppermute | solution.py:299
  23.1 5.5 %collective-permute-start.6 = (f32[1,8,128]{2,1,0:T(8,128)S(1)}, f32[1,8,128]{2,1,0:T(8,128)S(1)}, u32[]{:S(2)}, u32[]{:S(2)}) collective-permute-start(f32[1,8,128]{2,1,0:T(8,128)S(1)} %shard_map.88), channel_id=1, source_target_pairs={{0,1},{1,0},{2,3},{3,2},{4,5},{5,4},{6,7},{7,6},{8,9},{9,8},{10,11... | collective-permute-start | bytes 12296 | tf_op jit(solution)/shard_map/ppermute | solution.py:299
  25.9 5.1 %collective-permute-start.2 = (f32[2,16,1024]{2,1,0:T(8,128)S(1)}, f32[2,16,1024]{2,1,0:T(8,128)S(1)}, u32[]{:S(2)}, u32[]{:S(2)}) collective-permute-start(f32[2,16,1024]{2,1,0:T(8,128)S(1)} %add.33.a0), channel_id=1, source_target_pairs={{0,16},{4,20},{8,24},{12,28},{16,0},{20,4},{24,8},{28,12},{1,17},{... | collective-permute-start | bytes 393224 | tf_op jit(solution)/shard_map/ppermute | solution.py:299
  27.1 5.0 %collective-permute-start.4 = (f32[2,16,1024]{2,1,0:T(8,128)S(1)}, f32[2,16,1024]{2,1,0:T(8,128)S(1)}, u32[]{:S(2)}, u32[]{:S(2)}) collective-permute-start(f32[2,16,1024]{2,1,0:T(8,128)S(1)} %add.34.b0), channel_id=1, source_target_pairs={{0,8},{4,12},{8,0},{12,4},{16,24},{20,28},{24,16},{28,20},{1,9},{5... | collective-permute-start | bytes 393224 | tf_op jit(solution)/shard_map/ppermute | solution.py:299
  42.4 12.5 %copy-start = (f32[16,4096]{1,0:T(8,128)S(1)}, f32[16,4096]{1,0:T(8,128)}, u32[]{:S(2)}) copy-start(f32[16,4096]{1,0:T(8,128)} %site_ref.1) | copy-start | bytes 786436
  42.4 19.8 %copy-start.1 = (f32[16,16]{1,0:T(8,128)S(1)}, f32[16,16]{1,0:T(8,128)}, u32[]{:S(2)}) copy-start(f32[16,16]{1,0:T(8,128)} %source_ref.1) | copy-start | bytes 3076
  43.9 5.2 %collective-permute-start.9 = (f32[2,16,1024]{2,1,0:T(8,128)S(1)}, f32[2,16,1024]{2,1,0:T(8,128)S(1)}, u32[]{:S(2)}, u32[]{:S(2)}) collective-permute-start(f32[2,16,1024]{2,1,0:T(8,128)S(1)} %get-tuple-element.27), channel_id=1, source_target_pairs={{0,8},{4,12},{8,0},{12,4},{16,24},{20,28},{24,16},{28,20},{1,9},{5... | collective-permute-start | bytes 393224 | tf_op jit(solution)/shard_map/ppermute | solution.py:299
  44.5 5.3 %collective-permute-start.11 = (f32[2,16,1024]{2,1,0:T(8,128)S(1)}, f32[2,16,1024]{2,1,0:T(8,128)S(1)}, u32[]{:S(2)}, u32[]{:S(2)}) collective-permute-start(f32[2,16,1024]{2,1,0:T(8,128)S(1)} %get-tuple-element.28), channel_id=1, source_target_pairs={{0,16},{4,20},{8,24},{12,28},{16,0},{20,4},{24,8},{28,12},{1,17},{... | collective-permute-start | bytes 393224 | tf_op jit(solution)/shard_map/ppermute | solution.py:299
  49.1 5.0 %collective-permute-start.10 = (f32[2,16,1024]{2,1,0:T(8,128)S(1)}, f32[2,16,1024]{2,1,0:T(8,128)S(1)}, u32[]{:S(2)}, u32[]{:S(2)}) collective-permute-start(f32[2,16,1024]{2,1,0:T(8,128)S(1)} %add.38.a0), channel_id=1, source_target_pairs={{0,16},{4,20},{8,24},{12,28},{16,0},{20,4},{24,8},{28,12},{1,17},{... | collective-permute-start | bytes 393224 | tf_op jit(solution)/shard_map/ppermute | solution.py:299
  49.8 5.0 %collective-permute-start.12 = (f32[2,16,1024]{2,1,0:T(8,128)S(1)}, f32[2,16,1024]{2,1,0:T(8,128)S(1)}, u32[]{:S(2)}, u32[]{:S(2)}) collective-permute-start(f32[2,16,1024]{2,1,0:T(8,128)S(1)} %add.39.b0), channel_id=1, source_target_pairs={{0,8},{4,12},{8,0},{12,4},{16,24},{20,28},{24,16},{28,20},{1,9},{5... | collective-permute-start | bytes 393224 | tf_op jit(solution)/shard_map/ppermute | solution.py:299
  55.0 1.2 %collective-permute-start.13 = (f32[1,16,128]{2,1,0:T(8,128)S(1)}, f32[1,16,128]{2,1,0:T(8,128)S(1)}, u32[]{:S(2)}, u32[]{:S(2)}) collective-permute-start(f32[1,16,128]{2,1,0:T(8,128)S(1)} %get-tuple-element.31), channel_id=1, source_target_pairs={{0,4},{4,0},{8,12},{12,8},{16,20},{20,16},{24,28},{28,24},{1,5},{5... | collective-permute-start | bytes 24584 | tf_op jit(solution)/shard_map/ppermute | solution.py:299
  56.2 5.4 %collective-permute-start.16 = (f32[1,16,128]{2,1,0:T(8,128)S(1)}, f32[1,16,128]{2,1,0:T(8,128)S(1)}, u32[]{:S(2)}, u32[]{:S(2)}) collective-permute-start(f32[1,16,128]{2,1,0:T(8,128)S(1)} %add.40), channel_id=1, source_target_pairs={{0,3},{1,2},{2,1},{3,0},{4,7},{5,6},{6,5},{7,4},{8,11},{9,10},{10,... | collective-permute-start | bytes 24584 | tf_op jit(solution)/shard_map/ppermute | solution.py:299
  56.7 4.9 %collective-permute-start.15 = (f32[1,16,128]{2,1,0:T(8,128)S(1)}, f32[1,16,128]{2,1,0:T(8,128)S(1)}, u32[]{:S(2)}, u32[]{:S(2)}) collective-permute-start(f32[1,16,128]{2,1,0:T(8,128)S(1)} %add.40), channel_id=1, source_target_pairs={{0,2},{1,3},{2,0},{3,1},{4,6},{5,7},{6,4},{7,5},{8,10},{9,11},{10,... | collective-permute-start | bytes 24584 | tf_op jit(solution)/shard_map/ppermute | solution.py:299
  58.3 3.9 %collective-permute-start.14 = (f32[1,16,128]{2,1,0:T(8,128)S(1)}, f32[1,16,128]{2,1,0:T(8,128)S(1)}, u32[]{:S(2)}, u32[]{:S(2)}) collective-permute-start(f32[1,16,128]{2,1,0:T(8,128)S(1)} %add.40), channel_id=1, source_target_pairs={{0,1},{1,0},{2,3},{3,2},{4,5},{5,4},{6,7},{7,6},{8,9},{9,8},{10,11... | collective-permute-start | bytes 24584 | tf_op jit(solution)/shard_map/ppermute | solution.py:299
  60.6 1.6 %collective-permute-start.17 = (f32[16,2048]{1,0:T(8,128)S(1)}, f32[16,2048]{1,0:T(8,128)S(1)}, u32[]{:S(2)}, u32[]{:S(2)}) collective-permute-start(f32[16,2048]{1,0:T(8,128)S(1)} %get-tuple-element.32.mine_ref), channel_id=1, source_target_pairs={{0,4},{4,0},{8,12},{12,8},{16,20},{20,16},{24,28},{28,24},{1,5},{5... | collective-permute-start | bytes 393224 | tf_op jit(solution)/shard_map/ppermute | solution.py:299

commit v8 on v7

--- a/solution.py
+++ b/solution.py
@@ -62,11 +62,11 @@
         copy.start()
         small.append(copy)
     copies = [pltpu.make_async_copy(spec_hbm.at[e], spec.at[e], sems.at[e]) for e in range(ev_n)]
-    for copy in copies[:10]:
+    for copy in copies[:12]:
         copy.start(priority=1)
     for copy in small:
         copy.wait()
-    for i, copy in enumerate(copies[10:]):
+    for i, copy in enumerate(copies[12:]):
         copy.start(priority=0)
     maskf = mask_ref[...].astype(F32)
     low, high = maskf[:, :half_tiles], maskf[:, half_tiles:]

time: 63.2 us -> 63.2 us (level)
  no operation moved by 1% of the time
where the time goes in v8:
time: 63.2 us; the launch traced here: 63 us
  blocking collectives  22.8 us (36%)
  starting transfers between devices  16.3 us (26%)
  waiting for transfers between devices  14.5 us (23%)
  Pallas kernels  8.6 us (14%)
  between operations  0.71 us (1%)
    all_to_all x2, blocking collectives, on_device(): total = lax.all_to_all(sums, ('ev', 'ch'), 0, 0)  22.8 us
    ppermute x18, starting transfers between devices, swap(): return lax.ppermute(value, axis, [(i, i ^ bit) for i in range(size)])  16.3 us
    ppermute x18, waiting for transfers between devices, swap(): return lax.ppermute(value, axis, [(i, i ^ bit) for i in range(size)])  14.5 us
    pallas_call x1, Pallas kernels, on_device(): call(resid_kernel, [slabs, slabs, (devices, LANES)], [HBM] * 7, [pltpu.VM...  3.24 us
    pallas_call x2, Pallas kernels, on_device(): call(functools.partial(weight_kernel, freqs), [(2, freqs, quarter), (2, f...  3.04 us
    pallas_call x1, Pallas kernels, on_device(): call(update_kernel, [slabs, slabs, (freqs, half), (src_rows, LANES), (dev...  1.35 us
  transfers between devices with their start and end apart: 18, of which 9 were waited for; matrix products, arithmetic and copies ran while one was open for 0% of the time, Pallas kernels for 0%

profile of v8, /device:TPU:0, one launch (start us, length us, event | category | flops | bytes accessed | tf_op | source)
XLA Modules:
  0.0 63.0 jit_solution(13428353256229723769)
XLA Ops:
  0.6 3.2 %shard_map.86 = (f32[17,16,2048]{2,1,0:T(8,128)S(1)}, f32[17,16,2048]{2,1,0:T(8,128)S(1)}, f32[32,128]{1,0:T(8,128)S(1)}) custom-call(f32[16,16,4096]{2,1,0:T(8,128)} %spec_hbm.1, s32[16,32]{1,0:T(8,128)} %mask_hbm.1, f32[16,16]{1,0:T(8,128)} %source_ref.1, f32[16,4096]{1,0:T(8,128)} %site_ref.1, f32[3,16]{1,0:T(4,128)} %pos_hbm.1, f32[2,4096]{1,0:T(2,128)} %chan_hbm.1, ...), custom_call_target="tpu_custom_call" | custom-call | tf_op jit(solution)/shard_map/pallas_call | solution.py:316
  3.9 0.5 collective-permute-start
  4.4 13.9 %all_to_all.22 = f32[32,1,128]{2,1,0:T(1,128)S(1)} all-to-all(f32[32,1,128]{2,1,0:T(1,128)S(1)} %bitcast.14), channel_id=1, replica_groups=mesh['ev'=8,'ch'=4] {'ev','ch'}, dimensions={0} | all-to-all | bytes 32768 | tf_op jit(solution)/shard_map/all_to_all | solution.py:327
  18.3 1.5 %shard_map.87 = (f32[2,16,1024]{2,1,0:T(8,128)S(1)}, f32[2,16,1024]{2,1,0:T(8,128)S(1)}, f32[1,8,128]{2,1,0:T(8,128)S(1)}) custom-call(f32[32,128]{1,0:T(8,128)S(1)} %bitcast.9, f32[32,128]{1,0:T(8,128)S(1)} %bitcast.10, f32[17,16,2048]{2,1,0:T(8,128)S(1)} %get-tuple-element.19.mine_ref, f32[17,16,2048]{2,1,0:T(8,128)S(1)} %collective-permute-done.theirs_ref), custom_call_target="tpu_custom_call" | custom-call | tf_op jit(solution)/shard_map/pallas_call | solution.py:329
  19.9 0.6 %collective-permute-start.1 = (f32[2,16,1024]{2,1,0:T(8,128)S(1)}, f32[2,16,1024]{2,1,0:T(8,128)S(1)}, u32[]{:S(2)}, u32[]{:S(2)}) collective-permute-start(f32[2,16,1024]{2,1,0:T(8,128)S(1)} %get-tuple-element.21), channel_id=1, source_target_pairs={{0,8},{4,12},{8,0},{12,4},{16,24},{20,28},{24,16},{28,20},{1,9},{5... | collective-permute-start | bytes 393224 | tf_op jit(solution)/shard_map/ppermute | solution.py:299
  20.6 0.5 collective-permute-start.3
  21.1 0.6 collective-permute-start.8
  21.7 1.4 %collective-permute-start.7 = (f32[1,8,128]{2,1,0:T(8,128)S(1)}, f32[1,8,128]{2,1,0:T(8,128)S(1)}, u32[]{:S(2)}, u32[]{:S(2)}) collective-permute-start(f32[1,8,128]{2,1,0:T(8,128)S(1)} %shard_map.88), channel_id=1, source_target_pairs={{0,2},{1,3},{2,0},{3,1},{4,6},{5,7},{6,4},{7,5},{8,10},{9,11},{10,... | collective-permute-start | bytes 12296 | tf_op jit(solution)/shard_map/ppermute | solution.py:299
  23.1 2.4 %collective-permute-start.6 = (f32[1,8,128]{2,1,0:T(8,128)S(1)}, f32[1,8,128]{2,1,0:T(8,128)S(1)}, u32[]{:S(2)}, u32[]{:S(2)}) collective-permute-start(f32[1,8,128]{2,1,0:T(8,128)S(1)} %shard_map.88), channel_id=1, source_target_pairs={{0,1},{1,0},{2,3},{3,2},{4,5},{5,4},{6,7},{7,6},{8,9},{9,8},{10,11... | collective-permute-start | bytes 12296 | tf_op jit(solution)/shard_map/ppermute | solution.py:299
  25.5 0.3 collective-permute-done.1
  25.9 1.2 %collective-permute-start.2 = (f32[2,16,1024]{2,1,0:T(8,128)S(1)}, f32[2,16,1024]{2,1,0:T(8,128)S(1)}, u32[]{:S(2)}, u32[]{:S(2)}) collective-permute-start(f32[2,16,1024]{2,1,0:T(8,128)S(1)} %add.33.a0), channel_id=1, source_target_pairs={{0,16},{4,20},{8,24},{12,28},{16,0},{20,4},{24,8},{28,12},{1,17},{... | collective-permute-start | bytes 393224 | tf_op jit(solution)/shard_map/ppermute | solution.py:299
  27.1 1.5 %collective-permute-start.4 = (f32[2,16,1024]{2,1,0:T(8,128)S(1)}, f32[2,16,1024]{2,1,0:T(8,128)S(1)}, u32[]{:S(2)}, u32[]{:S(2)}) collective-permute-start(f32[2,16,1024]{2,1,0:T(8,128)S(1)} %add.34.b0), channel_id=1, source_target_pairs={{0,8},{4,12},{8,0},{12,4},{16,24},{20,28},{24,16},{28,20},{1,9},{5... | collective-permute-start | bytes 393224 | tf_op jit(solution)/shard_map/ppermute | solution.py:299
  28.7 2.3 %collective-permute-done.2.a1 = f32[2,16,1024]{2,1,0:T(8,128)S(1)} collective-permute-done((f32[2,16,1024]{2,1,0:T(8,128)S(1)}, f32[2,16,1024]{2,1,0:T(8,128)S(1)}, u32[]{:S(2)}, u32[]{:S(2)}) %collective-permute-start.2) | collective-permute-done | bytes 131104 | tf_op jit(solution)/shard_map/ppermute | solution.py:299
  31.0 1.2 %collective-permute-done.4.b1 = f32[2,16,1024]{2,1,0:T(8,128)S(1)} collective-permute-done((f32[2,16,1024]{2,1,0:T(8,128)S(1)}, f32[2,16,1024]{2,1,0:T(8,128)S(1)}, u32[]{:S(2)}, u32[]{:S(2)}) %collective-permute-start.4) | collective-permute-done | bytes 131104 | tf_op jit(solution)/shard_map/ppermute | solution.py:299
  32.2 1.3 %shard_map.89 = (f32[17,16,2048]{2,1,0:T(8,128)S(1)}, f32[17,16,2048]{2,1,0:T(8,128)S(1)}, f32[16,2048]{1,0:T(8,128)S(1)}, f32[4,128]{1,0:T(4,128)S(1)}, f32[32,128]{1,0:T(8,128)S(1)}) custom-call(f32[2,16,1024]{2,1,0:T(8,128)S(1)} %add.33.a0, f32[2,16,1024]{2,1,0:T(8,128)S(1)} %collective-permute-done.2.a1, f32[2,16,1024]{2,1,0:T(8,128)S(1)} %add.34.b0, ...), custom_call_target="tpu_custom_call" | custom-call | tf_op jit(solution)/shard_map/pallas_call | solution.py:346
  33.5 8.9 %all_to_all.23 = f32[32,1,128]{2,1,0:T(1,128)S(1)} all-to-all(f32[32,1,128]{2,1,0:T(1,128)S(1)} %bitcast.13), channel_id=1, replica_groups=mesh['ev'=8,'ch'=4] {'ev','ch'}, dimensions={0} | all-to-all | bytes 32768 | tf_op jit(solution)/shard_map/all_to_all | solution.py:327
  42.4 1.5 %shard_map.90 = (f32[2,16,1024]{2,1,0:T(8,128)S(1)}, f32[2,16,1024]{2,1,0:T(8,128)S(1)}, f32[1,8,128]{2,1,0:T(8,128)S(1)}) custom-call(f32[32,128]{1,0:T(8,128)S(1)} %bitcast.12, f32[32,128]{1,0:T(8,128)S(1)} %bitcast.11, f32[17,16,2048]{2,1,0:T(8,128)S(1)} %get-tuple-element.25.mine_ref, f32[17,16,2048]{2,1,0:T(8,128)S(1)} %get-tuple-element.26.theirs_ref), custom_call_target="tpu_custom_call" | custom-call | tf_op jit(solution)/shard_map/pallas_call | solution.py:329
  43.9 0.6 %collective-permute-start.9 = (f32[2,16,1024]{2,1,0:T(8,128)S(1)}, f32[2,16,1024]{2,1,0:T(8,128)S(1)}, u32[]{:S(2)}, u32[]{:S(2)}) collective-permute-start(f32[2,16,1024]{2,1,0:T(8,128)S(1)} %get-tuple-element.27), channel_id=1, source_target_pairs={{0,8},{4,12},{8,0},{12,4},{16,24},{20,28},{24,16},{28,20},{1,9},{5... | collective-permute-start | bytes 393224 | tf_op jit(solution)/shard_map/ppermute | solution.py:299
  44.5 0.5 collective-permute-start.11
  45.1 4.1 %collective-permute-done.9 = f32[2,16,1024]{2,1,0:T(8,128)S(1)} collective-permute-done((f32[2,16,1024]{2,1,0:T(8,128)S(1)}, f32[2,16,1024]{2,1,0:T(8,128)S(1)}, u32[]{:S(2)}, u32[]{:S(2)}) %collective-permute-start.9) | collective-permute-done | bytes 131104 | tf_op jit(solution)/shard_map/ppermute | solution.py:299
  49.1 0.7 %collective-permute-start.10 = (f32[2,16,1024]{2,1,0:T(8,128)S(1)}, f32[2,16,1024]{2,1,0:T(8,128)S(1)}, u32[]{:S(2)}, u32[]{:S(2)}) collective-permute-start(f32[2,16,1024]{2,1,0:T(8,128)S(1)} %add.38.a0), channel_id=1, source_target_pairs={{0,16},{4,20},{8,24},{12,28},{16,0},{20,4},{24,8},{28,12},{1,17},{... | collective-permute-start | bytes 393224 | tf_op jit(solution)/shard_map/ppermute | solution.py:299
  49.8 1.2 %collective-permute-start.12 = (f32[2,16,1024]{2,1,0:T(8,128)S(1)}, f32[2,16,1024]{2,1,0:T(8,128)S(1)}, u32[]{:S(2)}, u32[]{:S(2)}) collective-permute-start(f32[2,16,1024]{2,1,0:T(8,128)S(1)} %add.39.b0), channel_id=1, source_target_pairs={{0,8},{4,12},{8,0},{12,4},{16,24},{20,28},{24,16},{28,20},{1,9},{5... | collective-permute-start | bytes 393224 | tf_op jit(solution)/shard_map/ppermute | solution.py:299
  51.0 3.1 %collective-permute-done.10.a1 = f32[2,16,1024]{2,1,0:T(8,128)S(1)} collective-permute-done((f32[2,16,1024]{2,1,0:T(8,128)S(1)}, f32[2,16,1024]{2,1,0:T(8,128)S(1)}, u32[]{:S(2)}, u32[]{:S(2)}) %collective-permute-start.10) | collective-permute-done | bytes 131104 | tf_op jit(solution)/shard_map/ppermute | solution.py:299
  54.2 0.7 %collective-permute-done.12.b1 = f32[2,16,1024]{2,1,0:T(8,128)S(1)} collective-permute-done((f32[2,16,1024]{2,1,0:T(8,128)S(1)}, f32[2,16,1024]{2,1,0:T(8,128)S(1)}, u32[]{:S(2)}, u32[]{:S(2)}) %collective-permute-start.12) | collective-permute-done | bytes 131104 | tf_op jit(solution)/shard_map/ppermute | solution.py:299
  54.9 0.1 shard_map.91
  55.0 1.2 %collective-permute-done.13 = f32[1,16,128]{2,1,0:T(8,128)S(1)} collective-permute-done((f32[1,16,128]{2,1,0:T(8,128)S(1)}, f32[1,16,128]{2,1,0:T(8,128)S(1)}, u32[]{:S(2)}, u32[]{:S(2)}) %collective-permute-start.13) | collective-permute-done | bytes 8224 | tf_op jit(solution)/shard_map/ppermute | solution.py:299
  56.2 0.5 collective-permute-start.16
  56.7 1.6 %collective-permute-start.15 = (f32[1,16,128]{2,1,0:T(8,128)S(1)}, f32[1,16,128]{2,1,0:T(8,128)S(1)}, u32[]{:S(2)}, u32[]{:S(2)}) collective-permute-start(f32[1,16,128]{2,1,0:T(8,128)S(1)} %add.40), channel_id=1, source_target_pairs={{0,2},{1,3},{2,0},{3,1},{4,6},{5,7},{6,4},{7,5},{8,10},{9,11},{10,... | collective-permute-start | bytes 24584 | tf_op jit(solution)/shard_map/ppermute | solution.py:299
  58.3 2.3 %collective-permute-start.14 = (f32[1,16,128]{2,1,0:T(8,128)S(1)}, f32[1,16,128]{2,1,0:T(8,128)S(1)}, u32[]{:S(2)}, u32[]{:S(2)}) collective-permute-start(f32[1,16,128]{2,1,0:T(8,128)S(1)} %add.40), channel_id=1, source_target_pairs={{0,1},{1,0},{2,3},{3,2},{4,5},{5,4},{6,7},{7,6},{8,9},{9,8},{10,11... | collective-permute-start | bytes 24584 | tf_op jit(solution)/shard_map/ppermute | solution.py:299
  60.6 1.1 %collective-permute-done.16 = f32[1,16,128]{2,1,0:T(8,128)S(1)} collective-permute-done((f32[1,16,128]{2,1,0:T(8,128)S(1)}, f32[1,16,128]{2,1,0:T(8,128)S(1)}, u32[]{:S(2)}, u32[]{:S(2)}) %collective-permute-start.16) | collective-permute-done | bytes 8224 | tf_op jit(solution)/shard_map/ppermute | solution.py:299
  61.6 0.6 collective-permute-done.14
  62.2 0.8 %shard_map.92 = (f32[16,16]{1,0:T(8,128)}, f32[16,4096]{1,0:T(8,128)}) custom-call(f32[1,16,128]{2,1,0:T(8,128)S(1)} %add_add_fusion.sums_ref, f32[16,2048]{1,0:T(8,128)S(1)} %get-tuple-element.32.mine_ref, f32[16,2048]{1,0:T(8,128)S(1)} %collective-permute-done.17.theirs_ref, f32[4,128]{1,0:T(4,128)S(1)} %get-tuple-element.33.dsrc_ref, f32[16,16]{1,0:T(8,128)S(1)} %copy-done.1), custom_call_target="tpu_custom_call" | custom-call | tf_op jit(solution)/shard_map/pallas_call | solution.py:357
  (24 shorter events, 0.2 us)
Async XLA Ops:
  3.9 14.4 %collective-permute-start = (f32[17,16,2048]{2,1,0:T(8,128)S(1)}, f32[17,16,2048]{2,1,0:T(8,128)S(1)}, u32[]{:S(2)}, u32[]{:S(2)}) collective-permute-start(f32[17,16,2048]{2,1,0:T(8,128)S(1)} %get-tuple-element.20), channel_id=1, source_target_pairs={{0,4},{4,0},{8,12},{12,8},{16,20},{20,16},{24,28},{28,24},{1,5},{5... | collective-permute-start | bytes 6684680 | tf_op jit(solution)/shard_map/ppermute | solution.py:299
  19.9 1.3 %collective-permute-start.5 = (f32[1,8,128]{2,1,0:T(8,128)S(1)}, f32[1,8,128]{2,1,0:T(8,128)S(1)}, u32[]{:S(2)}, u32[]{:S(2)}) collective-permute-start(f32[1,8,128]{2,1,0:T(8,128)S(1)} %get-tuple-element.23.x_ref), channel_id=1, source_target_pairs={{0,4},{4,0},{8,12},{12,8},{16,20},{20,16},{24,28},{28,24},{1,5},{5... | collective-permute-start | bytes 12296 | tf_op jit(solution)/shard_map/ppermute | solution.py:299
  19.9 5.9 %collective-permute-start.1 = (f32[2,16,1024]{2,1,0:T(8,128)S(1)}, f32[2,16,1024]{2,1,0:T(8,128)S(1)}, u32[]{:S(2)}, u32[]{:S(2)}) collective-permute-start(f32[2,16,1024]{2,1,0:T(8,128)S(1)} %get-tuple-element.21), channel_id=1, source_target_pairs={{0,8},{4,12},{8,0},{12,4},{16,24},{20,28},{24,16},{28,20},{1,9},{5... | collective-permute-start | bytes 393224 | tf_op jit(solution)/shard_map/ppermute | solution.py:299
  20.6 6.5 %collective-permute-start.3 = (f32[2,16,1024]{2,1,0:T(8,128)S(1)}, f32[2,16,1024]{2,1,0:T(8,128)S(1)}, u32[]{:S(2)}, u32[]{:S(2)}) collective-permute-start(f32[2,16,1024]{2,1,0:T(8,128)S(1)} %get-tuple-element.22), channel_id=1, source_target_pairs={{0,16},{4,20},{8,24},{12,28},{16,0},{20,4},{24,8},{28,12},{1,17},{... | collective-permute-start | bytes 393224 | tf_op jit(solution)/shard_map/ppermute | solution.py:299
  21.1 7.5 %collective-permute-start.8 = (f32[1,8,128]{2,1,0:T(8,128)S(1)}, f32[1,8,128]{2,1,0:T(8,128)S(1)}, u32[]{:S(2)}, u32[]{:S(2)}) collective-permute-start(f32[1,8,128]{2,1,0:T(8,128)S(1)} %shard_map.88), channel_id=1, source_target_pairs={{0,3},{1,2},{2,1},{3,0},{4,7},{5,6},{6,5},{7,4},{8,11},{9,10},{10,... | collective-permute-start | bytes 12296 | tf_op jit(solution)/shard_map/ppermute | solution.py:299
  21.7 7.0 %collective-permute-start.7 = (f32[1,8,128]{2,1,0:T(8,128)S(1)}, f32[1,8,128]{2,1,0:T(8,128)S(1)}, u32[]{:S(2)}, u32[]{:S(2)}) collective-permute-start(f32[1,8,128]{2,1,0:T(8,128)S(1)} %shard_map.88), channel_id=1, source_target_pairs={{0,2},{1,3},{2,0},{3,1},{4,6},{5,7},{6,4},{7,5},{8,10},{9,11},{10,... | collective-permute-start | bytes 12296 | tf_op jit(solution)/shard_map/ppermute | solution.py:299
  23.1 5.5 %collective-permute-start.6 = (f32[1,8,128]{2,1,0:T(8,128)S(1)}, f32[1,8,128]{2,1,0:T(8,128)S(1)}, u32[]{:S(2)}, u32[]{:S(2)}) collective-permute-start(f32[1,8,128]{2,1,0:T(8,128)S(1)} %shard_map.88), channel_id=1, source_target_pairs={{0,1},{1,0},{2,3},{3,2},{4,5},{5,4},{6,7},{7,6},{8,9},{9,8},{10,11... | collective-permute-start | bytes 12296 | tf_op jit(solution)/shard_map/ppermute | solution.py:299
  25.9 5.1 %collective-permute-start.2 = (f32[2,16,1024]{2,1,0:T(8,128)S(1)}, f32[2,16,1024]{2,1,0:T(8,128)S(1)}, u32[]{:S(2)}, u32[]{:S(2)}) collective-permute-start(f32[2,16,1024]{2,1,0:T(8,128)S(1)} %add.33.a0), channel_id=1, source_target_pairs={{0,16},{4,20},{8,24},{12,28},{16,0},{20,4},{24,8},{28,12},{1,17},{... | collective-permute-start | bytes 393224 | tf_op jit(solution)/shard_map/ppermute | solution.py:299
  27.1 5.0 %collective-permute-start.4 = (f32[2,16,1024]{2,1,0:T(8,128)S(1)}, f32[2,16,1024]{2,1,0:T(8,128)S(1)}, u32[]{:S(2)}, u32[]{:S(2)}) collective-permute-start(f32[2,16,1024]{2,1,0:T(8,128)S(1)} %add.34.b0), channel_id=1, source_target_pairs={{0,8},{4,12},{8,0},{12,4},{16,24},{20,28},{24,16},{28,20},{1,9},{5... | collective-permute-start | bytes 393224 | tf_op jit(solution)/shard_map/ppermute | solution.py:299
  42.4 12.5 %copy-start = (f32[16,4096]{1,0:T(8,128)S(1)}, f32[16,4096]{1,0:T(8,128)}, u32[]{:S(2)}) copy-start(f32[16,4096]{1,0:T(8,128)} %site_ref.1) | copy-start | bytes 786436
  42.4 19.8 %copy-start.1 = (f32[16,16]{1,0:T(8,128)S(1)}, f32[16,16]{1,0:T(8,128)}, u32[]{:S(2)}) copy-start(f32[16,16]{1,0:T(8,128)} %source_ref.1) | copy-start | bytes 3076
  43.9 5.2 %collective-permute-start.9 = (f32[2,16,1024]{2,1,0:T(8,128)S(1)}, f32[2,16,1024]{2,1,0:T(8,128)S(1)}, u32[]{:S(2)}, u32[]{:S(2)}) collective-permute-start(f32[2,16,1024]{2,1,0:T(8,128)S(1)} %get-tuple-element.27), channel_id=1, source_target_pairs={{0,8},{4,12},{8,0},{12,4},{16,24},{20,28},{24,16},{28,20},{1,9},{5... | collective-permute-start | bytes 393224 | tf_op jit(solution)/shard_map/ppermute | solution.py:299
  44.5 5.3 %collective-permute-start.11 = (f32[2,16,1024]{2,1,0:T(8,128)S(1)}, f32[2,16,1024]{2,1,0:T(8,128)S(1)}, u32[]{:S(2)}, u32[]{:S(2)}) collective-permute-start(f32[2,16,1024]{2,1,0:T(8,128)S(1)} %get-tuple-element.28), channel_id=1, source_target_pairs={{0,16},{4,20},{8,24},{12,28},{16,0},{20,4},{24,8},{28,12},{1,17},{... | collective-permute-start | bytes 393224 | tf_op jit(solution)/shard_map/ppermute | solution.py:299
  49.1 5.0 %collective-permute-start.10 = (f32[2,16,1024]{2,1,0:T(8,128)S(1)}, f32[2,16,1024]{2,1,0:T(8,128)S(1)}, u32[]{:S(2)}, u32[]{:S(2)}) collective-permute-start(f32[2,16,1024]{2,1,0:T(8,128)S(1)} %add.38.a0), channel_id=1, source_target_pairs={{0,16},{4,20},{8,24},{12,28},{16,0},{20,4},{24,8},{28,12},{1,17},{... | collective-permute-start | bytes 393224 | tf_op jit(solution)/shard_map/ppermute | solution.py:299
  49.8 5.0 %collective-permute-start.12 = (f32[2,16,1024]{2,1,0:T(8,128)S(1)}, f32[2,16,1024]{2,1,0:T(8,128)S(1)}, u32[]{:S(2)}, u32[]{:S(2)}) collective-permute-start(f32[2,16,1024]{2,1,0:T(8,128)S(1)} %add.39.b0), channel_id=1, source_target_pairs={{0,8},{4,12},{8,0},{12,4},{16,24},{20,28},{24,16},{28,20},{1,9},{5... | collective-permute-start | bytes 393224 | tf_op jit(solution)/shard_map/ppermute | solution.py:299
  55.0 1.2 %collective-permute-start.13 = (f32[1,16,128]{2,1,0:T(8,128)S(1)}, f32[1,16,128]{2,1,0:T(8,128)S(1)}, u32[]{:S(2)}, u32[]{:S(2)}) collective-permute-start(f32[1,16,128]{2,1,0:T(8,128)S(1)} %get-tuple-element.31), channel_id=1, source_target_pairs={{0,4},{4,0},{8,12},{12,8},{16,20},{20,16},{24,28},{28,24},{1,5},{5... | collective-permute-start | bytes 24584 | tf_op jit(solution)/shard_map/ppermute | solution.py:299
  56.2 5.4 %collective-permute-start.16 = (f32[1,16,128]{2,1,0:T(8,128)S(1)}, f32[1,16,128]{2,1,0:T(8,128)S(1)}, u32[]{:S(2)}, u32[]{:S(2)}) collective-permute-start(f32[1,16,128]{2,1,0:T(8,128)S(1)} %add.40), channel_id=1, source_target_pairs={{0,3},{1,2},{2,1},{3,0},{4,7},{5,6},{6,5},{7,4},{8,11},{9,10},{10,... | collective-permute-start | bytes 24584 | tf_op jit(solution)/shard_map/ppermute | solution.py:299
  56.7 4.9 %collective-permute-start.15 = (f32[1,16,128]{2,1,0:T(8,128)S(1)}, f32[1,16,128]{2,1,0:T(8,128)S(1)}, u32[]{:S(2)}, u32[]{:S(2)}) collective-permute-start(f32[1,16,128]{2,1,0:T(8,128)S(1)} %add.40), channel_id=1, source_target_pairs={{0,2},{1,3},{2,0},{3,1},{4,6},{5,7},{6,4},{7,5},{8,10},{9,11},{10,... | collective-permute-start | bytes 24584 | tf_op jit(solution)/shard_map/ppermute | solution.py:299
  58.3 3.9 %collective-permute-start.14 = (f32[1,16,128]{2,1,0:T(8,128)S(1)}, f32[1,16,128]{2,1,0:T(8,128)S(1)}, u32[]{:S(2)}, u32[]{:S(2)}) collective-permute-start(f32[1,16,128]{2,1,0:T(8,128)S(1)} %add.40), channel_id=1, source_target_pairs={{0,1},{1,0},{2,3},{3,2},{4,5},{5,4},{6,7},{7,6},{8,9},{9,8},{10,11... | collective-permute-start | bytes 24584 | tf_op jit(solution)/shard_map/ppermute | solution.py:299
  60.6 1.6 %collective-permute-start.17 = (f32[16,2048]{1,0:T(8,128)S(1)}, f32[16,2048]{1,0:T(8,128)S(1)}, u32[]{:S(2)}, u32[]{:S(2)}) collective-permute-start(f32[16,2048]{1,0:T(8,128)S(1)} %get-tuple-element.32.mine_ref), channel_id=1, source_target_pairs={{0,4},{4,0},{8,12},{12,8},{16,20},{20,16},{24,28},{28,24},{1,5},{5... | collective-permute-start | bytes 393224 | tf_op jit(solution)/shard_map/ppermute | solution.py:299
